TPU v7x, 256 devices: a whole 4x4x8 slice. The times are simulated.
256 devices in a mesh: ctx: 32 (over y, x, core), qry: 8 (over z).
Axes of the slice: x: 4, y: 4, z: 8, core: 2. Of those that a mesh axis runs over, the one named last changes fastest.
Arguments:
- idx_query: bfloat16 [256, 8192], P('ctx', 'qry'), may hold values from -200 to 200
- idx_weight: bfloat16 [256, 64], P('ctx', 'qry'), may hold values from -3 to 3
- idx_keys: bfloat16 [65536, 128], P('ctx'), may hold values from -6 to 6
- q_latent: bfloat16 [256, 73728], P(('ctx', 'qry')), may hold values from -400 to 400
- latent_cache: bfloat16 [65536, 576], P('ctx'), may hold values from -20 to 20
- page_ids: int32 [256, 32], P(('ctx', 'qry')), may hold values from 0 to 1023, as said below
Outputs:
- index_logp: float32 [256, 65536], P(('ctx', 'qry'))
- latent_out: bfloat16 [256, 65536], P(('ctx', 'qry'))
Inputs may be any that keep to these rules, and one draw needn't show every extreme that they name: `page_ids`: each row names 32 distinct pages, and no page id appears twice in the 1 row of one device (aligned blocks of 1 row). Page p holds tokens p * 64 to p * 64 + 63; ctx index j holds pages j * 32 to (j + 1) * 32 - 1. Of the 32 ids in the rows of one device, at most 2 lie on one ctx index, and in every such block some ctx index holds exactly 2.
All inputs are finite; a program needn't handle non-finite values.
Results may differ from a plain program's by a relative error of at most 0.013.
Values may be sent and summed in bfloat16 or wider, within the bound.
No kernel may reach another device: no remote copies, remote signals or barrier semaphores. Data moves between devices by JAX's collectives and lax.ppermute only.
A program may use at most 64 MiB of HBM per device.

v0:
```python
import jax
import jax.numpy as jnp
from jax import lax
from jax.sharding import PartitionSpec as P

H_IDX = 64
D_IDX = 128
H = 128
D_LAT = 512
D_ROPE = 64
QK_NOPE = 128
PAGE = 64
TOPP = 32


def combined_all(part, axis, combine):
    gathered = jax.tree.map(lambda a: lax.all_gather(a, axis), part)

    def take(source):
        return jax.tree.map(lambda a: lax.dynamic_index_in_dim(a, source, 0, False), gathered)

    return lax.fori_loop(
        1, lax.axis_size(axis), lambda source, state: combine(state, take(source)), take(0)
    )


def combine_stats(left_stats, right_stats):
    left_max, left_total = left_stats
    right_max, right_total = right_stats
    joint_max = jnp.maximum(left_max, right_max)
    joint_total = left_total * jnp.exp(left_max - joint_max) + right_total * jnp.exp(
        right_max - joint_max
    )
    return (joint_max, joint_total)


def slot_ranks(requests, pages_dev):
    owner_shard = requests // pages_dev
    positions = jnp.arange(requests.shape[-1])
    earlier = positions[None, :] < positions[:, None]
    same_owner = owner_shard[..., :, None] == owner_shard[..., None, :]
    slot_rank = jnp.sum((same_owner & earlier).astype(jnp.int32), axis=-1)
    return (owner_shard, slot_rank)


def per_device(idx_query, idx_weight, idx_keys, q_latent, latent_cache, page_ids):
    shard_count = lax.axis_size("ctx")
    group_count = lax.axis_size("qry")
    ctx_index = lax.axis_index("ctx")
    rows_dev = q_latent.shape[0]
    ctx_dev = idx_keys.shape[0]
    latent_width = latent_cache.shape[1]
    pages_dev = ctx_dev // PAGE
    capacity = max(2, 2 * rows_dev * TOPP // shard_count)
    group_size = shard_count * rows_dev
    local_query = idx_query.reshape(group_count, rows_dev, idx_query.shape[1])
    local_weight = idx_weight.reshape(group_count, rows_dev, idx_weight.shape[1])
    every_query, every_weight = (
        lax.all_gather(local_query, "ctx", axis=0, tiled=True),
        lax.all_gather(local_weight, "ctx", axis=0, tiled=True),
    )
    group_query, group_weight = (
        lax.all_to_all(
            every_query.reshape(shard_count, group_count, rows_dev, idx_query.shape[1]),
            "qry",
            split_axis=1,
            concat_axis=3,
            tiled=True,
        ),
        lax.all_to_all(
            every_weight.reshape(shard_count, group_count, rows_dev, idx_weight.shape[1]),
            "qry",
            split_axis=1,
            concat_axis=3,
            tiled=True,
        ),
    )
    flat_query = group_query.reshape(group_size * H_IDX, D_IDX)
    head_weights = group_weight.reshape(group_size, H_IDX).astype(jnp.float32)
    block_width = min(512, ctx_dev)

    def score_block(step, table):
        key_block = lax.dynamic_slice_in_dim(idx_keys, step * block_width, block_width, 0)
        head_dots = lax.dot_general(
            flat_query, key_block, (((1,), (1,)), ((), ())), preferred_element_type=jnp.float32
        )
        active = jnp.maximum(head_dots, 0.0).reshape(group_size, H_IDX, block_width)
        summed = jnp.sum(active * head_weights[:, :, None], axis=1)
        return lax.dynamic_update_slice_in_dim(table, summed, step * block_width, 1)

    scores = lax.fori_loop(
        0, ctx_dev // block_width, score_block, jnp.zeros((group_size, ctx_dev), jnp.float32)
    )
    log_length = jnp.log(jnp.float32(ctx_dev * shard_count))
    score_table = lax.all_to_all(
        scores.astype(jnp.bfloat16), "ctx", split_axis=0, concat_axis=1, tiled=True
    ).astype(scores.dtype)
    row_max = jnp.max(score_table, axis=1, keepdims=True)
    row_total = jnp.sum(jnp.exp(score_table - row_max), axis=1, keepdims=True)
    index_logp = score_table - (row_max + jnp.log(row_total)) + log_length
    group_ids = lax.all_gather(page_ids, "ctx", axis=0, tiled=True)
    owner_shard, slot_rank = slot_ranks(group_ids, pages_dev)
    local_page = group_ids % pages_dev
    which_row = jnp.arange(rows_dev * TOPP) // TOPP
    chosen = (owner_shard == ctx_index)[:, None, :] & (
        slot_rank[:, None, :] == jnp.arange(capacity)[None, :, None]
    )
    slot_page = jnp.sum(jnp.where(chosen, local_page[:, None, :], 0), axis=2)
    slot_used = jnp.any(chosen, axis=2)
    slot_row = jnp.sum(jnp.where(chosen, which_row[None, None, :], 0), axis=2)
    page_store = latent_cache.reshape(pages_dev, PAGE, latent_width)
    slot_keys = page_store[slot_page]
    logit_scale = (QK_NOPE + D_ROPE) ** (-0.5)
    query_group = lax.all_gather(q_latent, "ctx", axis=0, tiled=True)
    query_rows = query_group.reshape(shard_count, rows_dev, H, latent_width)
    key_rows = slot_keys.reshape(shard_count, capacity * PAGE, latent_width)
    logits = (
        jnp.einsum("cqhd,ckd->cqhk", query_rows, key_rows, preferred_element_type=jnp.float32)
        * logit_scale
    )
    slot_live = slot_used[:, None, :] & (
        slot_row[:, None, :] == jnp.arange(rows_dev)[None, :, None]
    )
    slot_live = jnp.repeat(slot_live, PAGE, axis=2)[:, :, None, :]
    masked = jnp.where(slot_live, logits, -1e30)
    local_max = jnp.max(masked, axis=3)
    local_total = jnp.sum(jnp.where(slot_live, jnp.exp(masked - local_max[..., None]), 0.0), axis=3)
    joint_max, joint_total = combined_all((local_max, local_total), "ctx", combine_stats)
    att_weights = jnp.where(
        slot_live, jnp.exp(masked - joint_max[..., None]) / joint_total[..., None], 0.0
    ).astype(jnp.bfloat16)
    value_part = key_rows[:, :, :D_LAT]
    mixed_rows = jnp.einsum(
        "cqhk,ckd->cqhd", att_weights, value_part, preferred_element_type=jnp.float32
    )
    summed = lax.psum_scatter(
        mixed_rows.reshape(rows_dev * lax.axis_size("ctx"), H * D_LAT),
        "ctx",
        scatter_dimension=0,
        tiled=True,
    )
    latent_out = summed.astype(jnp.bfloat16)
    return (index_logp, latent_out)


def solution(mesh):
    in_specs = (
        P("ctx", "qry"),
        P("ctx", "qry"),
        P("ctx", None),
        P(("ctx", "qry"), None),
        P("ctx", None),
        P(("ctx", "qry"), None),
    )
    out_specs = (P(("ctx", "qry"), None), P(("ctx", "qry"), None))
    return jax.shard_map(
        per_device, mesh=mesh, in_specs=in_specs, out_specs=out_specs, check_vma=False
    )
```

profile of v0, /device:TPU:1, one launch (start us, length us, event | category | flops | bytes accessed | tf_op | source)
XLA Modules:
  0.0 450.8 jit_solution(766966655252993307)
XLA Ops:
  7.2 0.7 all-gather.8.cloned.1.call-update
  7.9 25.8 %all-gather.1 = bf16[256,8]{1,0:T(8,128)(2,1)S(1)} all-gather(bf16[8,8]{1,0:T(8,128)(2,1)} %param.11), channel_id=3, replica_groups=mesh['ctx'=32,'qry'=8] {'ctx'}, dimensions={0}, use_global_device_ids=true | all-gather | bytes 4224 | tf_op jit(solution)/shard_map/all_gather | solution.py:60
  33.8 0.7 reshape.219
  34.5 8.2 %all-to-all-start.1 = ((bf16[8,2,128]{2,1,0:T(2,128)(2,1)}), bf16[8,2,128]{2,1,0:T(2,128)(2,1)S(1)}, u32[]{:S(2)}, u32[]{:S(2)}) async-start(bf16[8,2,128]{2,1,0:T(2,128)(2,1)} %reshape.219), calls=%async_computation.1 | async-start | bytes 8192 | tf_op jit(solution)/shard_map/all_to_all | solution.py:70
  42.7 20.8 %all-gather.4 = s32[32,1,32]{2,1,0:T(1,128)S(1)} all-gather(s32[1,1,32]{2,1,0:T(1,128)} %bitcast.115), channel_id=1, replica_groups=mesh['ctx'=32,'qry'=8] {'ctx'}, dimensions={0}, use_global_device_ids=true | all-gather | bytes 4224 | tf_op jit(solution)/shard_map/all_gather | solution.py:101
  63.5 22.9 %all-gather = bf16[256,1024]{1,0:T(8,128)(2,1)S(1)} all-gather(bf16[8,1024]{1,0:T(8,128)(2,1)} %param.10), channel_id=2, replica_groups=mesh['ctx'=32,'qry'=8] {'ctx'}, dimensions={0}, use_global_device_ids=true | all-gather | bytes 540672 | tf_op jit(solution)/shard_map/all_gather | solution.py:59
  86.4 0.8 convert_reduce_fusion
  87.2 1.1 copy.39
  88.3 6.9 %all-to-all-start = ((bf16[32,8,1,1024]{3,0,2,1:T(8,128)(2,1)}), bf16[32,8,1,1024]{3,0,2,1:T(8,128)(2,1)S(1)}, u32[]{:S(2)}, u32[]{:S(2)}) async-start(bf16[32,8,1,1024]{3,0,2,1:T(8,128)(2,1)} %copy.39), calls=%async_computation | async-start | bytes 1048576 | tf_op jit(solution)/shard_map/all_to_all | solution.py:63
  95.2 0.1 fusion.17
  95.3 0.1 select_reduce_fusion.1
  95.7 17.5 %all-to-all-done = bf16[32,8,1,1024]{3,0,2,1:T(8,128)(2,1)S(1)} async-done(((bf16[32,8,1,1024]{3,0,2,1:T(8,128)(2,1)}), bf16[32,8,1,1024]{3,0,2,1:T(8,128)(2,1)S(1)}, u32[]{:S(2)}, u32[]{:S(2)}) %all-to-all-start) | async-done | bytes 524320 | tf_op jit(solution)/shard_map/all_to_all | solution.py:63
  113.2 0.3 copy.40
  113.5 0.2 reshape.184
  113.7 47.9 %while.30 = (s32[]{:T(128)}, bf16[32,2048]{1,0:T(8,128)(2,1)S(1)}, bf16[2048,128]{1,0:T(8,128)(2,1)}, bf16[2048,128]{1,0:T(8,128)(2,1)S(1)}, f32[32,64]{1,0:T(8,...) while((s32[]{:T(128)}, bf16[32,2048]{1,0:T(8,128)(2,1)S(1)}, bf16[2048,128]{1,0:T(8,128)(2,1)}, ...), condition=%wide.region_2.0_spmd, body=%wide.region_0.0_spmd.sunk | while | flops 271564800 | bytes 17539220 | solution.py:91
  113.7 3.7 maximum_bitcast_fusion.2
  117.4 5.4 %copy.59 = f32[2048,512]{1,0:T(8,128)} copy(f32[2048,512]{0,1:T(8,128)} %maximum_bitcast_fusion.2) | data formatting | bytes 8388608 | tf_op jit(solution)/shard_map/while/body/eval_jaxpr/max | solution.py:87
  122.8 2.9 multiply_reduce_fusion.2
  125.7 3.7 maximum_bitcast_fusion.2
  129.4 5.4 %copy.59 = f32[2048,512]{1,0:T(8,128)} copy(f32[2048,512]{0,1:T(8,128)} %maximum_bitcast_fusion.2) | data formatting | bytes 8388608 | tf_op jit(solution)/shard_map/while/body/eval_jaxpr/max | solution.py:87
  134.8 2.9 multiply_reduce_fusion.2
  137.7 3.7 maximum_bitcast_fusion.2
  141.4 5.4 %copy.59 = f32[2048,512]{1,0:T(8,128)} copy(f32[2048,512]{0,1:T(8,128)} %maximum_bitcast_fusion.2) | data formatting | bytes 8388608 | tf_op jit(solution)/shard_map/while/body/eval_jaxpr/max | solution.py:87
  146.8 2.9 multiply_reduce_fusion.2
  149.7 3.7 maximum_bitcast_fusion.2
  153.4 5.4 %copy.59 = f32[2048,512]{1,0:T(8,128)} copy(f32[2048,512]{0,1:T(8,128)} %maximum_bitcast_fusion.2) | data formatting | bytes 8388608 | tf_op jit(solution)/shard_map/while/body/eval_jaxpr/max | solution.py:87
  158.7 2.9 multiply_reduce_fusion.2
  161.7 0.5 broadcast.146
  162.2 0.7 reduce.9
  162.9 0.7 reshape.221
  163.6 5.8 %all-to-all-start.2 = ((bf16[32,2,1024]{2,1,0:T(2,128)(2,1)}), bf16[32,2,1024]{2,1,0:T(2,128)(2,1)S(1)}, u32[]{:S(2)}, u32[]{:S(2)}) async-start(bf16[32,2,1024]{2,1,0:T(2,128)(2,1)} %reshape.221), calls=%async_computation.2 | async-start | bytes 262144 | tf_op jit(solution)/shard_map/all_to_all | solution.py:95
  170.0 3.1 copy.46
  173.1 0.7 dynamic-slice
  173.7 3.6 gather_fusion
  177.4 1.1 reduce_max.23
  179.2 1.1 exponential_reduce_fusion
  181.7 1.1 subtract_add_fusion
  182.8 29.2 %reduce.8 = bf16[32,73728]{1,0:T(8,128)(2,1)} reduce(bf16[32,1,73728]{2,1,0:T(2,128)(2,1)} %all-gather.8.cloned.1.call-done, bf16[]{:T(256)} %constant.152), dimensions={1}, to_apply=%all-gather.5.reduce_sub_computation | reduce | bytes 9437186 | tf_op jit(solution)/shard_map/all_gather | solution.py:114
  211.9 8.8 %reshape.189 = bf16[32,128,576]{2,1,0:T(8,128)(2,1)} reshape(bf16[32,73728]{1,0:T(8,128)(2,1)} %reduce.8) | data formatting | bytes 9437184 | tf_op jit(solution)/shard_map/reshape.28
  220.7 5.1 %bitcast_reduce_fusion = (f32[32,128]{1,0:T(8,128)S(1)}, f32[32,128,128]{2,1,0:T(8,128)S(1)}) fusion(bf16[32,128,576]{2,1,0:T(8,128)(2,1)} %bitcast.90, bf16[32,128,576]{2,1,0:T(8,128)(2,1)} %reshape.189, pred[32,128]{1,0:T(8,128)(4,1)S(1)} %broadcast_in_dim.79), kind=kOutput, calls=%fused_computation.13 | convolution fusion | flops 605548544 | bytes 11554816 | tf_op jit(solution)/shard_map/cqhd,ckd->cqhk/dot_general | solution.py:118
  225.9 25.2 %all-gather.2 = f32[1024,128]{1,0:T(8,128)S(1)} all-gather(f32[32,128]{1,0:T(8,128)S(1)} %get-tuple-element.280), channel_id=4, replica_groups=mesh['ctx'=32,'qry'=8] {'ctx'}, dimensions={0}, use_global_device_ids=true | all-gather | bytes 540672 | tf_op jit(solution)/shard_map/all_gather | solution.py:17
  251.0 0.7 fusion.6
  251.7 24.4 %all-gather.3 = f32[1024,128]{1,0:T(8,128)S(1)} all-gather(f32[32,128]{1,0:T(8,128)S(1)} %fusion.6), channel_id=5, replica_groups=mesh['ctx'=32,'qry'=8] {'ctx'}, dimensions={0}, use_global_device_ids=true | all-gather | bytes 540672 | tf_op jit(solution)/shard_map/all_gather | solution.py:17
  276.1 1.9 while.31
  278.0 4.7 %fusion.2 = f32[32,128,512]{2,1,0:T(8,128)S(1)} fusion(bf16[32,128,576]{2,1,0:T(8,128)(2,1)} %bitcast.91, f32[32,128,128]{2,1,0:T(8,128)S(1)} %get-tuple-element.281, f32[32,128]{1,0:T(8,128)S(1)} %bitcast.105, f32[32,128]{1,0:T(8,128)S(1)} %bitcast.101, pred[32,128]{1,0:T(8,128)(4,1)S(1)} %broadcast_in_dim.79), kind=kOutput, calls=%fused_computation.9 | convolution fusion | flops 538968064 | bytes 14716928 | tf_op jit(solution)/shard_map/cqhk,ckd->cqhd/dot_general | solution.py:133
  282.7 8.1 %copy.56 = f32[4,8,128,512]{3,1,2,0:T(8,128)} copy(f32[4,8,128,512]{3,2,1,0:T(8,128)S(1)} %bitcast.92) | data formatting | bytes 16777216
  290.8 150.3 %all-reduce.2 = bf16[32,65536]{1,0:T(8,128)(2,1)} all-reduce(f32[32,65536]{1,0:T(8,128)} %bitcast.93), channel_id=6, replica_groups=mesh['ctx'=32,'qry'=8] {'ctx'}, use_global_device_ids=true, to_apply=%region_13.14.clone | all-reduce | flops 2097152 | bytes 12582912
  441.1 2.8 dynamic-slice_convert_fusion
  (92 shorter events, 2.0 us)
Async XLA Ops:
  7.2 175.6 %all-gather.8.cloned.1.call-start = ((), (), s32[]{:S(2)}) async-start(), calls=%async_computation.3 | async-start | bytes 9732096 | tf_op jit(solution)/shard_map/all_gather | solution.py:114
  34.5 53.8 %all-to-all-start.1 = ((bf16[8,2,128]{2,1,0:T(2,128)(2,1)}), bf16[8,2,128]{2,1,0:T(2,128)(2,1)S(1)}, u32[]{:S(2)}, u32[]{:S(2)}) async-start(bf16[8,2,128]{2,1,0:T(2,128)(2,1)} %reshape.219), calls=%async_computation.1 | async-start | bytes 8192 | tf_op jit(solution)/shard_map/all_to_all | solution.py:70
  88.3 24.9 %all-to-all-start = ((bf16[32,8,1,1024]{3,0,2,1:T(8,128)(2,1)}), bf16[32,8,1,1024]{3,0,2,1:T(8,128)(2,1)S(1)}, u32[]{:S(2)}, u32[]{:S(2)}) async-start(bf16[32,8,1,1024]{3,0,2,1:T(8,128)(2,1)} %copy.39), calls=%async_computation | async-start | bytes 1048576 | tf_op jit(solution)/shard_map/all_to_all | solution.py:63
  161.7 11.4 %copy-start = (u32[256]{0:T(256)S(1)}, u32[256]{0:T(256)}, u32[]{:S(2)}) copy-start(u32[256]{0:T(256)} %constant.150) | copy-start | bytes 3076
  163.6 13.7 %all-to-all-start.2 = ((bf16[32,2,1024]{2,1,0:T(2,128)(2,1)}), bf16[32,2,1024]{2,1,0:T(2,128)(2,1)S(1)}, u32[]{:S(2)}, u32[]{:S(2)}) async-start(bf16[32,2,1024]{2,1,0:T(2,128)(2,1)} %reshape.221), calls=%async_computation.2 | async-start | bytes 262144 | tf_op jit(solution)/shard_map/all_to_all | solution.py:95
Sparse Core Ops, SparseCore 0:
  10.5 64.8 all-gather.7
where the time goes:
time: 454 us; the launch traced here: 451 us
  blocking collectives  269 us (59%)
  local copies, waits for them, and re-layouts  53.2 us (12%)
  other arithmetic  47.3 us (10%)
  matrix products  24.5 us (5%)
  starting transfers between devices  21 us (5%)
  waiting for transfers between devices  18.2 us (4%)
  between operations  16.2 us (4%)
    unnamed x1, blocking collectives  150 us
    all_gather x2, blocking collectives, combined_all(): gathered = jax.tree.map(lambda a: lax.all_gather(a, axis), part)  49.5 us
    all_gather x1, other arithmetic, per_device(): query_group = lax.all_gather(q_latent, 'ctx', axis=0, tiled=True)  29.2 us
    all_gather x1, blocking collectives, per_device(): lax.all_gather(local_weight, 'ctx', axis=0, tiled=True)  25.8 us
    all_gather x1, blocking collectives, per_device(): lax.all_gather(local_query, 'ctx', axis=0, tiled=True)  22.9 us
    max x4, local copies, waits for them, and re-layouts, score_block(): active = jnp.maximum(head_dots, 0.0).reshape(group_size, H_IDX, block_width)  21.4 us
    all_gather x1, blocking collectives, per_device(): group_ids = lax.all_gather(page_ids, 'ctx', axis=0, tiled=True)  20.8 us
    all_to_all x1, waiting for transfers between devices, per_device(): lax.all_to_all(every_query.reshape(shard_count, group_count, rows_dev, id...  17.5 us
  transfers between devices with their start and end apart: 4, of which 1 were waited for; matrix products, arithmetic and copies ran while one was open for 14% of the time, Pallas kernels for 0%

commit v1 on v0

v1 whole, which is shorter than its diff:
```python
import functools

import jax
import jax.numpy as jnp
from jax import lax
from jax.experimental import pallas as pl
from jax.experimental.pallas import tpu as pltpu
from jax.sharding import PartitionSpec as P

H_IDX = 64
D_IDX = 128
H = 128
D_LAT = 512
D_ROPE = 64
QK_NOPE = 128
PAGE = 64
TOPP = 32
MOST = 2
LANES = 128
BLOB = PAGE * (D_LAT // LANES) + PAGE * D_ROPE // LANES
HALF = PAGE // 2
QROWS_MSG = 80
NEG = -1e30
MIB = 1 << 20


def pack_kernel(table_ref, cache_ref, out_ref):
    step = pl.program_id(0)
    rows = out_ref.shape[0]
    for r in range(rows):
        for s in range(MOST):
            page = jnp.maximum(table_ref[(step * rows + r) * MOST + s] - 1, 0)
            start = pl.multiple_of(page * PAGE, PAGE)
            for j in range(D_LAT // LANES):
                out_ref[r, s, j * PAGE : (j + 1) * PAGE, :] = cache_ref[
                    pl.ds(start, PAGE), j * LANES : (j + 1) * LANES
                ]
            low = cache_ref[pl.ds(start, HALF), D_LAT : D_LAT + D_ROPE]
            high = cache_ref[pl.ds(start + HALF, HALF), D_LAT : D_LAT + D_ROPE]
            out_ref[r, s, D_LAT // LANES * PAGE : BLOB, :] = jnp.concatenate([low, high], axis=1)


def pack_pages(table, cache, peers):
    rows = 4
    return pl.pallas_call(
        pack_kernel,
        grid_spec=pltpu.PrefetchScalarGridSpec(
            num_scalar_prefetch=1,
            grid=(peers // rows,),
            in_specs=[pl.BlockSpec(cache.shape, lambda i, t: (0, 0))],
            out_specs=pl.BlockSpec((rows, MOST, BLOB, LANES), lambda i, t: (i, 0, 0, 0)),
        ),
        out_shape=jax.ShapeDtypeStruct((peers, MOST, BLOB, LANES), cache.dtype),
        compiler_params=pltpu.CompilerParams(vmem_limit_bytes=24 * MIB),
        cost_estimate=pl.CostEstimate(flops=0, bytes_accessed=7 * MIB, transcendentals=0),
        name="pack_pages",
    )(table, cache)


def score_kernel(query_ref, key_ref, out_ref, weight_ref, sum_ref):
    rows = query_ref.shape[0]
    eye = lax.broadcasted_iota(jnp.int32, (H_IDX, H_IDX), 0) == lax.broadcasted_iota(
        jnp.int32, (H_IDX, H_IDX), 1
    )
    ones = jnp.ones((H_IDX, LANES), jnp.bfloat16)
    for r in range(rows):
        row = query_ref[r, H_IDX : H_IDX + 16, :][0:1, :H_IDX].astype(jnp.float32)
        diagonal = jnp.where(eye, row, 0.0).astype(jnp.bfloat16)
        weight_ref[r] = jnp.dot(diagonal, ones, preferred_element_type=jnp.float32)
    width = 2 * LANES
    for r in range(rows):
        query = query_ref[r, :H_IDX, :]
        weight = weight_ref[r]
        for b in range(key_ref.shape[0] // width):
            keys = key_ref[b * width : (b + 1) * width, :]
            dots = lax.dot_general(
                query, keys, (((1,), (1,)), ((), ())), preferred_element_type=jnp.float32
            )
            for j in range(2):
                part = jnp.maximum(dots[:, j * LANES : (j + 1) * LANES], 0.0) * weight
                sum_ref[r, 2 * b + j : 2 * b + j + 1, :] = jnp.sum(part, axis=0, keepdims=True)
        out_ref[r] = sum_ref[r].astype(out_ref.dtype)


def index_scores(queries, keys):
    rows = 4
    peers = queries.shape[0]
    blocks = keys.shape[0] // LANES
    return pl.pallas_call(
        score_kernel,
        grid=(peers // rows,),
        in_specs=[
            pl.BlockSpec((rows, QROWS_MSG, LANES), lambda i: (i, 0, 0)),
            pl.BlockSpec(keys.shape, lambda i: (0, 0)),
        ],
        out_specs=pl.BlockSpec((rows, blocks, LANES), lambda i: (i, 0, 0)),
        out_shape=jax.ShapeDtypeStruct((peers, blocks, LANES), jnp.bfloat16),
        scratch_shapes=[
            pltpu.VMEM((rows, H_IDX, LANES), jnp.float32),
            pltpu.VMEM((rows, blocks, LANES), jnp.float32),
        ],
        compiler_params=pltpu.CompilerParams(vmem_limit_bytes=16 * MIB),
        cost_estimate=pl.CostEstimate(
            flops=2 * peers * H_IDX * keys.shape[0] * D_IDX,
            bytes_accessed=2 * MIB,
            transcendentals=0,
        ),
        name="index_scores",
    )(queries, keys)


def logp_kernel(score_ref, out_ref):
    scores = score_ref[...].astype(jnp.float32)
    top = jnp.max(scores)
    total = jnp.sum(jnp.exp(scores - top), keepdims=True)
    out_ref[...] = scores - (top + jnp.log(total)) + jnp.log(jnp.float32(scores.size))


def log_distribution(scores):
    return pl.pallas_call(
        logp_kernel,
        out_shape=jax.ShapeDtypeStruct(scores.shape, jnp.float32),
        compiler_params=pltpu.CompilerParams(vmem_limit_bytes=8 * MIB),
        cost_estimate=pl.CostEstimate(
            flops=4 * scores.size, bytes_accessed=6 * scores.size, transcendentals=scores.size
        ),
        name="log_distribution",
    )(scores)


def attend_kernel(used_ref, query_ref, low_ref, high_ref, page_ref, out_ref, top_ref, total_ref, sum_ref):
    step = pl.program_id(0)
    sources = page_ref.shape[0]
    pages = sources * MOST

    @pl.when(step == 0)
    def _():
        top_ref[...] = jnp.full_like(top_ref, NEG)
        total_ref[...] = jnp.zeros_like(total_ref)
        sum_ref[...] = jnp.zeros_like(sum_ref)

    def latents(first):
        return jnp.concatenate(
            [
                jnp.concatenate(
                    [
                        page_ref[i, s, j * PAGE + first : j * PAGE + first + HALF, :]
                        for j in range(D_LAT // LANES)
                    ],
                    axis=1,
                )
                for i in range(sources)
                for s in range(MOST)
            ],
            axis=0,
        )

    rotary = jnp.concatenate(
        [
            page_ref[i, s, D_LAT // LANES * PAGE : BLOB, :]
            for i in range(sources)
            for s in range(MOST)
        ],
        axis=0,
    )
    across = (((1,), (1,)), ((), ()))
    scale = (QK_NOPE + D_ROPE) ** (-0.5)
    place = lax.broadcasted_iota(jnp.int32, (1, pages * HALF), 1) // HALF
    live = jnp.zeros((1, pages * HALF), jnp.int32)
    for p in range(pages):
        live = jnp.where(place == p, used_ref[step * pages + p], live)
    keys = [latents(0), latents(HALF)]
    logits = [
        jnp.where(
            live > 0,
            (
                lax.dot_general(query_ref[...], k, across, preferred_element_type=jnp.float32)
                + lax.dot_general(q[...], rotary, across, preferred_element_type=jnp.float32)
            )
            * scale,
            NEG,
        )
        for k, q in zip(keys, (low_ref, high_ref))
    ]
    old = top_ref[...]
    new = jnp.maximum(
        old,
        jnp.maximum(
            jnp.max(logits[0], axis=1, keepdims=True), jnp.max(logits[1], axis=1, keepdims=True)
        ),
    )
    fade = jnp.exp(old - new)
    top_ref[...] = new
    expo = [jnp.exp(v - new[:, :1]) for v in logits]
    total_ref[...] = (
        total_ref[...] * fade
        + jnp.sum(expo[0], axis=1, keepdims=True)
        + jnp.sum(expo[1], axis=1, keepdims=True)
    )
    mixed = sum(
        jnp.dot(e.astype(jnp.bfloat16), k, preferred_element_type=jnp.float32)
        for e, k in zip(expo, keys)
    )
    sum_ref[...] = sum_ref[...] * fade[:, :1] + mixed

    @pl.when(step == pl.num_programs(0) - 1)
    def _():
        out_ref[...] = (sum_ref[...] / total_ref[...][:, :1]).astype(out_ref.dtype)


def attend(used, query, pages):
    sources = 4
    peers = pages.shape[0]
    latent = query[:, :D_LAT]
    rotary = query[:, D_LAT:]
    nothing = jnp.zeros_like(rotary)
    low = jnp.concatenate([rotary, nothing], axis=1)
    high = jnp.concatenate([nothing, rotary], axis=1)
    whole = lambda shape: pl.BlockSpec(shape, lambda i, u: (0, 0))
    return pl.pallas_call(
        attend_kernel,
        grid_spec=pltpu.PrefetchScalarGridSpec(
            num_scalar_prefetch=1,
            grid=(peers // sources,),
            in_specs=[
                whole((H, D_LAT)),
                whole((H, LANES)),
                whole((H, LANES)),
                pl.BlockSpec((sources, MOST, BLOB, LANES), lambda i, u: (i, 0, 0, 0)),
            ],
            out_specs=whole((H, D_LAT)),
            scratch_shapes=[
                pltpu.VMEM((H, LANES), jnp.float32),
                pltpu.VMEM((H, LANES), jnp.float32),
                pltpu.VMEM((H, D_LAT), jnp.float32),
            ],
        ),
        out_shape=jax.ShapeDtypeStruct((H, D_LAT), jnp.bfloat16),
        compiler_params=pltpu.CompilerParams(vmem_limit_bytes=24 * MIB),
        cost_estimate=pl.CostEstimate(
            flops=2 * H * peers * MOST * PAGE * (2 * D_LAT + D_ROPE),
            bytes_accessed=5 * MIB,
            transcendentals=H * peers * MOST * PAGE,
        ),
        name="attend",
    )(used, latent, low, high, pages)


def request_table(page_ids, owners, pages_dev):
    ids = page_ids[0]
    owner, local = ids // pages_dev, ids % pages_dev
    earlier = jnp.arange(TOPP)[None, :] < jnp.arange(TOPP)[:, None]
    rank = jnp.sum(((owner[:, None] == owner[None, :]) & earlier).astype(jnp.int32), axis=1)
    chosen = (owner[None, None, :] == jnp.arange(owners)[:, None, None]) & (
        rank[None, None, :] == jnp.arange(MOST)[None, :, None]
    )
    return jnp.sum(jnp.where(chosen, local[None, None, :] + 1, 0), axis=2)


def per_device(idx_query, idx_weight, idx_keys, q_latent, latent_cache, page_ids):
    owners = lax.axis_size("ctx")
    groups = lax.axis_size("qry")
    ctx_dev = idx_keys.shape[0]
    exchange = functools.partial(lax.all_to_all, split_axis=0, concat_axis=0, tiled=True)

    table = request_table(page_ids, owners, ctx_dev // PAGE)
    wide = jnp.pad(table[:, None, :], ((0, 0), (0, 7), (0, LANES - MOST)))
    asked = exchange(wide, "ctx")[:, 0, :MOST]
    packed = pack_pages(asked.reshape(-1), latent_cache, owners)
    pages = exchange(packed, "ctx")

    heads_dev = H_IDX // groups
    parts = jnp.concatenate(
        [
            idx_query.reshape(groups, heads_dev, D_IDX),
            jnp.pad(idx_weight[:, None, :], ((0, 0), (0, 7), (0, LANES - heads_dev))),
        ],
        axis=1,
    )
    parts = exchange(parts, "qry")
    own = jnp.concatenate(
        [
            parts[:, :heads_dev, :].reshape(H_IDX, D_IDX),
            jnp.pad(
                parts[:, heads_dev, :heads_dev].reshape(1, H_IDX),
                ((0, QROWS_MSG - H_IDX - 1), (0, LANES - H_IDX)),
            ),
        ],
        axis=0,
    )
    queries = exchange(jnp.broadcast_to(own[None], (owners, QROWS_MSG, LANES)), "ctx")
    scores = exchange(index_scores(queries, idx_keys), "ctx")
    index_logp = log_distribution(scores.reshape(-1, LANES)).reshape(1, -1)

    latent_out = attend(
        table.reshape(-1), q_latent.reshape(H, D_LAT + D_ROPE), pages
    ).reshape(1, -1)
    return (index_logp, latent_out)


def solution(mesh):
    in_specs = (
        P("ctx", "qry"),
        P("ctx", "qry"),
        P("ctx", None),
        P(("ctx", "qry"), None),
        P("ctx", None),
        P(("ctx", "qry"), None),
    )
    out_specs = (P(("ctx", "qry"), None), P(("ctx", "qry"), None))
    return jax.shard_map(
        per_device, mesh=mesh, in_specs=in_specs, out_specs=out_specs, check_vma=False
    )
```

time: 454 us -> 144 us (0.32)
  blocking collectives: 269 us -> 0 us
  waiting for transfers between devices: 18.2 us -> 70.9 us
  other arithmetic: 47.3 us -> 3.26 us
  local copies, waits for them, and re-layouts: 53.2 us -> 10.2 us
  matrix products: 24.5 us -> 0 us
  Pallas kernels: 0 us -> 19.6 us
  starting transfers between devices: 21 us -> 37.1 us
  between operations: 16.2 us -> 0.75 us
    unnamed x1 -> x0, blocking collectives: 150 us -> none
    all_gather x5 -> x0, blocking collectives: 119 us -> none  [the longest x2 49.5 us: combined_all(): gathered = jax.tree.map(lambda a: lax.all_gather(a, axis), part)]
    all_to_all x3 -> x5, waiting for transfers between devices: 17.5 us -> 70.9 us  [the longest x1 53.3 us: per_device(): pages = exchange(packed, 'ctx')]
    all_gather x1 -> x0, other arithmetic: 29.2 us -> none  [per_device(): query_group = lax.all_gather(q_latent, 'ctx', axis=0, tiled=True)]
    dot_general x6 -> x0, matrix products: 24.5 us -> none  [the longest x4 14.8 us: score_block(): lax.dot_general(flat_query, key_block, (((1,), (1,)), ((), ())), preferre...]
    max x4 -> x0, local copies, waits for them, and re-layouts: 21.4 us -> none  [score_block(): active = jnp.maximum(head_dots, 0.0).reshape(group_size, H_IDX, block_width)]
    pallas_call x0 -> x4, Pallas kernels: none -> 19.6 us  [the longest x1 8.66 us: attend(): pl.pallas_call(attend_kernel, grid_spec=pltpu.PrefetchScalarGridSpec(num_...]
    all_to_all x3 -> x5, starting transfers between devices: 21 us -> 37.1 us  [the longest x1 9.19 us: per_device(): exchange(jnp.broadcast_to(own[None], (owners, QROWS_MSG, LANES)), 'ctx')]
  transfers between devices with their start and end apart: 4 -> 5, of which waited for: 1 -> 4; matrix products, arithmetic and copies ran while one was open for 14% -> 5% of each run, Pallas kernels for 0% -> 8%
where the time goes in v1:
time: 144 us; the launch traced here: 142 us
  waiting for transfers between devices  70.9 us (49%)
  starting transfers between devices  37.1 us (26%)
  Pallas kernels  19.6 us (14%)
  local copies, waits for them, and re-layouts  10.2 us (7%)
  other arithmetic  3.26 us (2%)
    all_to_all x1, waiting for transfers between devices, per_device(): pages = exchange(packed, 'ctx')  53.3 us
    all_to_all x1, waiting for transfers between devices, per_device(): exchange(jnp.broadcast_to(own[None], (owners, QROWS_MSG, LANES)), 'ctx')  11.8 us
    all_to_all x1, starting transfers between devices, per_device(): exchange(jnp.broadcast_to(own[None], (owners, QROWS_MSG, LANES)), 'ctx')  9.19 us
    all_to_all x1, starting transfers between devices, per_device(): parts = exchange(parts, 'qry')  9.01 us
    pallas_call x1, Pallas kernels, attend(): pl.pallas_call(attend_kernel, grid_spec=pltpu.PrefetchScalarGridSpec(num_...  8.66 us
    pallas_call x1, Pallas kernels, index_scores(): pl.pallas_call(score_kernel, grid=(peers // rows,), in_specs=[pl.BlockSpe...  7.81 us
    all_to_all x1, starting transfers between devices, per_device(): scores = exchange(index_scores(queries, idx_keys), 'ctx')  7.49 us
    all_to_all x1, starting transfers between devices, per_device(): pages = exchange(packed, 'ctx')  7.33 us
  transfers between devices with their start and end apart: 5, of which 4 were waited for; matrix products, arithmetic and copies ran while one was open for 5% of the time, Pallas kernels for 8%

profile of v1, /device:TPU:1, one launch (start us, length us, event | category | flops | bytes accessed | tf_op | source)
XLA Modules:
  0.0 141.8 jit_solution(5155945783149098782)
XLA Ops:
  0.6 0.7 fusion.2
  1.4 0.6 copy.23
  2.0 9.0 %all-to-all-start = ((bf16[8,16,128]{2,1,0:T(8,128)(2,1)}), bf16[8,16,128]{2,1,0:T(8,128)(2,1)S(1)}, u32[]{:S(2)}, u32[]{:S(2)}) async-start(bf16[8,16,128]{2,1,0:T(8,128)(2,1)} %copy.23), calls=%async_computation | async-start | bytes 65536 | tf_op jit(solution)/shard_map/all_to_all | solution.py:280
  11.0 0.7 and_select_fusion.2
  11.7 0.7 fusion.6
  12.3 5.5 %all-to-all-done = bf16[8,16,128]{2,1,0:T(8,128)(2,1)S(1)} async-done(((bf16[8,16,128]{2,1,0:T(8,128)(2,1)}), bf16[8,16,128]{2,1,0:T(8,128)(2,1)S(1)}, u32[]{:S(2)}, u32[]{:S(2)}) %all-to-all-start) | async-done | bytes 32800 | tf_op jit(solution)/shard_map/all_to_all | solution.py:280
  17.9 0.1 reshape_squeeze.6
  18.0 0.9 broadcast_in_dim.19
  18.9 9.2 %all-to-all-start.1 = ((bf16[32,80,128]{2,1,0:T(8,128)(2,1)}), bf16[32,80,128]{2,1,0:T(8,128)(2,1)S(1)}, u32[]{:S(2)}, u32[]{:S(2)}) async-start(bf16[32,80,128]{2,1,0:T(8,128)(2,1)} %broadcast_in_dim.19), calls=%async_computation.1 | async-start | bytes 1310720 | tf_op jit(solution)/shard_map/all_to_all | solution.py:291
  28.1 0.2 convert_reduce_fusion
  28.3 0.1 select_reduce_fusion
  28.5 0.1 copy.27
  28.6 0.7 pad.16.clone
  29.2 11.8 %all-to-all-done.1.query_ref = bf16[32,80,128]{2,1,0:T(8,128)(2,1)S(1)} async-done(((bf16[32,80,128]{2,1,0:T(8,128)(2,1)}), bf16[32,80,128]{2,1,0:T(8,128)(2,1)S(1)}, u32[]{:S(2)}, u32[]{:S(2)}) %all-to-all-start.1) | async-done | bytes 655392 | tf_op jit(solution)/shard_map/all_to_all | solution.py:291
  41.1 4.1 %all-to-all-start.3 = ((s32[32,8,128]{2,1,0:T(8,128)}), s32[32,8,128]{2,1,0:T(8,128)S(1)}, u32[]{:S(2)}, u32[]{:S(2)}) async-start(s32[32,8,128]{2,1,0:T(8,128)} %pad.16.clone), calls=%async_computation.3 | async-start | bytes 262144 | tf_op jit(solution)/shard_map/all_to_all | solution.py:268
  45.1 0.0 copy-start.1
  45.1 1.0 copy-done.1
  46.2 7.8 %index_scores.1 = bf16[32,16,128]{2,1,0:T(8,128)(2,1)} custom-call(bf16[32,80,128]{2,1,0:T(8,128)(2,1)S(1)} %all-to-all-done.1.query_ref, bf16[2048,128]{1,0:T(8,128)(2,1)S(1)} %copy-done.1), custom_call_target="tpu_custom_call" | custom-call | flops 1073741824 | bytes 2097152 | tf_op jit(solution)/shard_map/index_scores/pallas_call | solution.py:89
  54.0 0.0 all-to-all-done.3
  54.0 7.5 %all-to-all-start.2 = ((bf16[32,16,128]{2,1,0:T(8,128)(2,1)}), bf16[32,16,128]{2,1,0:T(8,128)(2,1)S(1)}, u32[]{:S(2)}, u32[]{:S(2)}) async-start(bf16[32,16,128]{2,1,0:T(8,128)(2,1)} %index_scores.1), calls=%async_computation.2 | async-start | bytes 262144 | tf_op jit(solution)/shard_map/all_to_all | solution.py:292
  61.5 3.1 %copy.26.cache_ref = bf16[2048,576]{1,0:T(8,128)(2,1)S(1)} copy(bf16[2048,576]{0,1:T(8,128)(2,1)} %param.10) | data formatting | bytes 4718592 | tf_op args[4]
  64.6 0.1 reshape_squeeze.7.table_ref
  64.7 2.0 %pack_pages.1 = bf16[32,2,288,128]{3,2,1,0:T(8,128)(2,1)S(1)} custom-call(s32[64]{0:T(128)S(1)} %reshape_squeeze.7.table_ref, bf16[2048,576]{1,0:T(8,128)(2,1)S(1)} %copy.26.cache_ref), custom_call_target="tpu_custom_call" | custom-call | bytes 7340032 | tf_op jit(solution)/shard_map/pack_pages/pallas_call | solution.py:45
  66.7 0.0 copy-start
  66.7 2.2 %copy-done = bf16[32,2,288,128]{3,2,1,0:T(8,128)(2,1)} copy-done((bf16[32,2,288,128]{3,2,1,0:T(8,128)(2,1)}, bf16[32,2,288,128]{3,2,1,0:T(8,128)(2,1)S(1)}, u32[]{:S(2)}) %copy-start) | copy-done | bytes 4718616
  68.9 0.0 copy-start.2
  68.9 0.2 all-to-all-done.2
  69.1 7.3 %all-to-all-start.4 = ((bf16[32,2,288,128]{3,2,1,0:T(8,128)(2,1)}), bf16[32,2,288,128]{3,2,1,0:T(8,128)(2,1)}, u32[]{:S(2)}, u32[]{:S(2)}) async-start(bf16[32,2,288,128]{3,2,1,0:T(8,128)(2,1)} %copy-done), calls=%async_computation.4 | async-start | bytes 9437184 | tf_op jit(solution)/shard_map/all_to_all | solution.py:270
  76.4 0.1 copy.24
  76.5 0.0 copy-done.2
  76.5 0.9 reduce.1
  77.4 0.2 reshape.157
  77.6 0.1 reshape.156.used_ref
  77.7 0.1 fusion.7
  77.8 1.1 log_distribution.1
  78.9 53.3 %all-to-all-done.4.page_ref = bf16[32,2,288,128]{3,2,1,0:T(8,128)(2,1)} async-done(((bf16[32,2,288,128]{3,2,1,0:T(8,128)(2,1)}), bf16[32,2,288,128]{3,2,1,0:T(8,128)(2,1)}, u32[]{:S(2)}, u32[]{:S(2)}) %all-to-all-start.4) | async-done | bytes 4718624 | tf_op jit(solution)/shard_map/all_to_all | solution.py:270
  132.2 8.7 %attend.1 = bf16[128,512]{1,0:T(8,128)(2,1)S(1)} custom-call(s32[64]{0:T(128)S(1)} %reshape.156.used_ref, bf16[128,512]{1,0:T(8,128)(2,1)S(1)} %slice.22.query_ref, bf16[128,128]{1,0:T(8,128)(2,1)S(1)} %get-tuple-element.3.low_ref, bf16[128,128]{1,0:T(8,128)(2,1)S(1)} %get-tuple-element.2.high_ref, bf16[32,2,288,128]{3,2,1,0:T(8,128)(2,1)} %all-to-all-done.4.page_ref), custom_call_target="tpu_custom_call" | custom-call | flops 1140850688 | bytes 5242880 | tf_op jit(solution)/shard_map/attend/pallas_call | solution.py:220
  140.9 0.9 copy.28
  (8 shorter events, 0.1 us)
Async XLA Ops:
  2.0 15.9 %all-to-all-start = ((bf16[8,16,128]{2,1,0:T(8,128)(2,1)}), bf16[8,16,128]{2,1,0:T(8,128)(2,1)S(1)}, u32[]{:S(2)}, u32[]{:S(2)}) async-start(bf16[8,16,128]{2,1,0:T(8,128)(2,1)} %copy.23), calls=%async_computation | async-start | bytes 65536 | tf_op jit(solution)/shard_map/all_to_all | solution.py:280
  18.9 22.1 %all-to-all-start.1 = ((bf16[32,80,128]{2,1,0:T(8,128)(2,1)}), bf16[32,80,128]{2,1,0:T(8,128)(2,1)S(1)}, u32[]{:S(2)}, u32[]{:S(2)}) async-start(bf16[32,80,128]{2,1,0:T(8,128)(2,1)} %broadcast_in_dim.19), calls=%async_computation.1 | async-start | bytes 1310720 | tf_op jit(solution)/shard_map/all_to_all | solution.py:291
  41.1 12.9 %all-to-all-start.3 = ((s32[32,8,128]{2,1,0:T(8,128)}), s32[32,8,128]{2,1,0:T(8,128)S(1)}, u32[]{:S(2)}, u32[]{:S(2)}) async-start(s32[32,8,128]{2,1,0:T(8,128)} %pad.16.clone), calls=%async_computation.3 | async-start | bytes 262144 | tf_op jit(solution)/shard_map/all_to_all | solution.py:268
  45.1 1.0 copy-start.1
  54.0 15.1 %all-to-all-start.2 = ((bf16[32,16,128]{2,1,0:T(8,128)(2,1)}), bf16[32,16,128]{2,1,0:T(8,128)(2,1)S(1)}, u32[]{:S(2)}, u32[]{:S(2)}) async-start(bf16[32,16,128]{2,1,0:T(8,128)(2,1)} %index_scores.1), calls=%async_computation.2 | async-start | bytes 262144 | tf_op jit(solution)/shard_map/all_to_all | solution.py:292
  66.7 2.2 %copy-start = (bf16[32,2,288,128]{3,2,1,0:T(8,128)(2,1)}, bf16[32,2,288,128]{3,2,1,0:T(8,128)(2,1)S(1)}, u32[]{:S(2)}) copy-start(bf16[32,2,288,128]{3,2,1,0:T(8,128)(2,1)S(1)} %pack_pages.1) | copy-start | bytes 14155780
  68.9 7.7 %copy-start.2 = (bf16[1,73728]{1,0:T(2,128)(2,1)S(1)}, bf16[1,73728]{1,0:T(2,128)(2,1)}, u32[]{:S(2)}) copy-start(bf16[1,73728]{1,0:T(2,128)(2,1)} %param.9) | copy-start | bytes 442372
  69.1 63.1 %all-to-all-start.4 = ((bf16[32,2,288,128]{3,2,1,0:T(8,128)(2,1)}), bf16[32,2,288,128]{3,2,1,0:T(8,128)(2,1)}, u32[]{:S(2)}, u32[]{:S(2)}) async-start(bf16[32,2,288,128]{3,2,1,0:T(8,128)(2,1)} %copy-done), calls=%async_computation.4 | async-start | bytes 9437184 | tf_op jit(solution)/shard_map/all_to_all | solution.py:270

commit v2 on v1

v2 whole, which is shorter than its diff:
```python
import functools

import jax
import jax.numpy as jnp
from jax import lax
from jax.experimental import pallas as pl
from jax.experimental.pallas import tpu as pltpu
from jax.sharding import PartitionSpec as P

H_IDX = 64
D_IDX = 128
H = 128
D_LAT = 512
D_ROPE = 64
DK = D_LAT + D_ROPE
QK_NOPE = 128
PAGE = 64
TOPP = 32
LANES = 128
MSG = 80
NEG = -1e30
MIB = 1 << 20


def request_kernel(pages_dev, ids_ref, out_ref):
    owners = out_ref.shape[0]
    ids = ids_ref[...]
    owner, local = ids // pages_dev, ids % pages_dev
    mine = owner == lax.broadcasted_iota(jnp.int32, (owners, TOPP), 0)
    count = jnp.sum(mine.astype(jnp.int32), axis=1, keepdims=True)
    low = jnp.min(jnp.where(mine, local, pages_dev), axis=1, keepdims=True)
    high = jnp.max(jnp.where(mine, local, -1), axis=1, keepdims=True)
    first = jnp.where(count >= 1, low + 1, 0)
    second = jnp.where(count >= 2, high + 1, 0)
    lane = lax.broadcasted_iota(jnp.int32, (owners, LANES), 1)
    table = jnp.where(lane == 0, first, jnp.where(lane == 1, second, 0))
    out_ref[...] = table.reshape(owners, 1, LANES)


def request_table(page_ids, owners, pages_dev):
    return pl.pallas_call(
        functools.partial(request_kernel, pages_dev),
        out_shape=jax.ShapeDtypeStruct((owners, 1, LANES), jnp.int32),
        name="request_table",
    )(page_ids)


def tile_kernel(cache_ref, out_ref):
    for t in range(out_ref.shape[1]):
        tile = cache_ref[:, t * LANES : (t + 1) * LANES]
        out_ref[0, t] = tile
        out_ref[1, t] = jnp.concatenate([tile[:, PAGE:], tile[:, :PAGE]], axis=1)


def tile_pages(cache):
    tiles = cache.shape[1] // LANES
    step = 4
    return pl.pallas_call(
        tile_kernel,
        grid=(tiles // step,),
        in_specs=[pl.BlockSpec((DK, step * LANES), lambda i: (0, i))],
        out_specs=pl.BlockSpec((2, step, DK, LANES), lambda i: (0, i, 0, 0)),
        out_shape=jax.ShapeDtypeStruct((2, tiles, DK, LANES), cache.dtype),
        compiler_params=pltpu.CompilerParams(vmem_limit_bytes=16 * MIB),
        cost_estimate=pl.CostEstimate(flops=0, bytes_accessed=7 * MIB, transcendentals=0),
        name="tile_pages",
    )(cache)


def pack_kernel(table_ref, tile_ref, out_ref):
    step = pl.program_id(0)
    rows = out_ref.shape[0]
    left = lax.broadcasted_iota(jnp.int32, (DK, LANES), 1) < PAGE
    for r in range(rows):
        first = jnp.maximum(table_ref[step * rows + r, 0, 0] - 1, 0)
        second = jnp.maximum(table_ref[step * rows + r, 0, 1] - 1, 0)
        out_ref[r] = jnp.where(
            left, tile_ref[first % 2, first // 2], tile_ref[1 - second % 2, second // 2]
        )


def pack_pages(table, tiles):
    peers = table.shape[0]
    rows = 4
    return pl.pallas_call(
        pack_kernel,
        grid=(peers // rows,),
        in_specs=[
            pl.BlockSpec(memory_space=pltpu.SMEM),
            pl.BlockSpec(tiles.shape, lambda i: (0, 0, 0, 0)),
        ],
        out_specs=pl.BlockSpec((rows, DK, LANES), lambda i: (i, 0, 0)),
        out_shape=pltpu.HBM((peers, DK, LANES), tiles.dtype),
        compiler_params=pltpu.CompilerParams(vmem_limit_bytes=24 * MIB),
        cost_estimate=pl.CostEstimate(flops=0, bytes_accessed=9 * MIB, transcendentals=0),
        name="pack_pages",
    )(table, tiles)


def score_kernel(key_ref, *refs):
    query_refs, (out_ref, sum_ref) = refs[:-2], refs[-2:]
    eye = lax.broadcasted_iota(jnp.int32, (H_IDX, H_IDX), 0) == lax.broadcasted_iota(
        jnp.int32, (H_IDX, H_IDX), 1
    )
    ones = jnp.ones((H_IDX, LANES), jnp.bfloat16)
    width = 2 * LANES
    for g, query_ref in enumerate(query_refs):
        row = query_ref[0, H_IDX : H_IDX + 16, :][0:1, :H_IDX].astype(jnp.float32)
        diagonal = jnp.where(eye, row, 0.0).astype(jnp.bfloat16)
        weight = jnp.dot(diagonal, ones, preferred_element_type=jnp.float32)
        query = query_ref[0, :H_IDX, :]
        for b in range(key_ref.shape[0] // width):
            keys = key_ref[b * width : (b + 1) * width, :]
            dots = lax.dot_general(
                query, keys, (((1,), (1,)), ((), ())), preferred_element_type=jnp.float32
            )
            for j in range(2):
                part = jnp.maximum(dots[:, j * LANES : (j + 1) * LANES], 0.0) * weight
                sum_ref[g, 2 * b + j : 2 * b + j + 1, :] = jnp.sum(part, axis=0, keepdims=True)
        out_ref[g, 0] = sum_ref[g].astype(out_ref.dtype)


def index_scores(queries, keys):
    groups, rows = len(queries), queries[0].shape[0]
    blocks = keys.shape[0] // LANES
    return pl.pallas_call(
        score_kernel,
        grid=(rows,),
        in_specs=[pl.BlockSpec(keys.shape, lambda i: (0, 0))]
        + [pl.BlockSpec((1, MSG, LANES), lambda i: (i, 0, 0))] * groups,
        out_specs=pl.BlockSpec((groups, 1, blocks, LANES), lambda i: (0, i, 0, 0)),
        out_shape=jax.ShapeDtypeStruct((groups, rows, blocks, LANES), jnp.bfloat16),
        scratch_shapes=[pltpu.VMEM((groups, blocks, LANES), jnp.float32)],
        compiler_params=pltpu.CompilerParams(vmem_limit_bytes=16 * MIB),
        cost_estimate=pl.CostEstimate(
            flops=2 * groups * rows * H_IDX * keys.shape[0] * D_IDX,
            bytes_accessed=2 * MIB,
            transcendentals=0,
        ),
        name="index_scores",
    )(keys, *queries)


def logp_kernel(me_ref, *refs):
    part_refs, out_ref = refs[:-1], refs[-1]
    parts = [ref[...].astype(jnp.float32) for ref in part_refs]
    top = functools.reduce(jnp.maximum, [jnp.max(p) for p in parts])
    total = sum(jnp.sum(jnp.exp(p - top), axis=0) for p in parts)
    total = jnp.sum(total, keepdims=True)
    count = sum(p.size for p in parts)
    shift = jnp.log(jnp.float32(count)) - (top + jnp.log(total))
    rows = part_refs[0].shape[1]
    for g, p in enumerate(parts):
        for s in range(p.shape[0]):
            source = me_ref[0] ^ (p.shape[0] * g + s)
            out_ref[pl.ds(pl.multiple_of(source * rows, rows), rows), :] = p[s] + shift


def log_distribution(me, parts):
    count = sum(p.size for p in parts)
    return pl.pallas_call(
        logp_kernel,
        in_specs=[pl.BlockSpec(memory_space=pltpu.SMEM)]
        + [pl.BlockSpec(memory_space=pltpu.VMEM)] * len(parts),
        out_shape=jax.ShapeDtypeStruct((count // LANES, LANES), jnp.float32),
        compiler_params=pltpu.CompilerParams(vmem_limit_bytes=8 * MIB),
        cost_estimate=pl.CostEstimate(
            flops=4 * count, bytes_accessed=6 * count, transcendentals=count
        ),
        name="log_distribution",
    )(me, *parts)


def attend_kernel(used_ref, query_ref, page_ref, out_ref, top_ref, total_ref, sum_ref):
    step = pl.program_id(0)
    sources = page_ref.shape[0]

    @pl.when(step == 0)
    def _():
        top_ref[...] = jnp.full_like(top_ref, NEG)
        total_ref[...] = jnp.zeros_like(total_ref)
        sum_ref[...] = jnp.zeros_like(sum_ref)

    left = lax.broadcasted_iota(jnp.int32, (1, LANES), 1) < PAGE
    live = []
    for i in range(sources):
        slots = [
            jnp.where(used_ref[step * sources + i, 0, s] > 0, 0.0, NEG) for s in range(2)
        ]
        live.append(jnp.where(left, slots[0], slots[1]))
    live = jnp.concatenate(live, axis=1)
    keys = jnp.concatenate([page_ref[i] for i in range(sources)], axis=1)
    scale = (QK_NOPE + D_ROPE) ** (-0.5)
    logits = jnp.dot(query_ref[...], keys, preferred_element_type=jnp.float32) * scale + live
    old = top_ref[...]
    new = jnp.maximum(old, jnp.max(logits, axis=1, keepdims=True))
    fade = jnp.exp(old - new)
    top_ref[...] = new
    expo = jnp.exp(logits - new[:, :1])
    total_ref[...] = total_ref[...] * fade + jnp.sum(expo, axis=1, keepdims=True)
    mixed = lax.dot_general(
        expo.astype(jnp.bfloat16),
        keys[:D_LAT],
        (((1,), (1,)), ((), ())),
        preferred_element_type=jnp.float32,
    )
    sum_ref[...] = sum_ref[...] * fade[:, :1] + mixed

    @pl.when(step == pl.num_programs(0) - 1)
    def _():
        out_ref[...] = (sum_ref[...] / total_ref[...][:, :1]).astype(out_ref.dtype)


def attend(used, query, pages):
    sources = 8
    peers = pages.shape[0]
    tokens = peers * LANES
    return pl.pallas_call(
        attend_kernel,
        grid=(peers // sources,),
        in_specs=[
            pl.BlockSpec(memory_space=pltpu.SMEM),
            pl.BlockSpec((H, DK), lambda i: (0, 0)),
            pl.BlockSpec((sources, DK, LANES), lambda i: (i, 0, 0)),
        ],
        out_specs=pl.BlockSpec((H, D_LAT), lambda i: (0, 0)),
        scratch_shapes=[
            pltpu.VMEM((H, LANES), jnp.float32),
            pltpu.VMEM((H, LANES), jnp.float32),
            pltpu.VMEM((H, D_LAT), jnp.float32),
        ],
        out_shape=jax.ShapeDtypeStruct((H, D_LAT), jnp.bfloat16),
        compiler_params=pltpu.CompilerParams(vmem_limit_bytes=24 * MIB),
        cost_estimate=pl.CostEstimate(
            flops=2 * H * tokens * (2 * D_LAT + D_ROPE),
            bytes_accessed=5 * MIB,
            transcendentals=H * tokens,
        ),
        name="attend",
    )(used, query, pages)


def swap(x, axis, bits):
    size = lax.axis_size(axis)
    return lax.ppermute(x, axis, [(i, i ^ bits) for i in range(size)])


def head_parts(idx_query, idx_weight):
    groups = lax.axis_size("qry")
    me = lax.axis_index("qry")
    heads = idx_weight.shape[1]
    parts = jnp.concatenate(
        [
            idx_query.reshape(groups, heads, D_IDX),
            jnp.pad(idx_weight[:, None, :], ((0, 0), (0, 7), (0, LANES - heads))),
        ],
        axis=1,
    )
    got = []
    for d in range(groups):
        part = lax.dynamic_index_in_dim(parts, me ^ d, 0, False)
        got.append(swap(part, "qry", d) if d else part)
    queries = jnp.concatenate([g[:heads] for g in got], axis=0)
    weights = jnp.concatenate([g[heads, :heads] for g in got], axis=0)[None]
    return jnp.concatenate(
        [queries, jnp.pad(weights, ((0, MSG - H_IDX - 1), (0, LANES - H_IDX)))], axis=0
    )


def per_device(idx_query, idx_weight, idx_keys, q_latent, latent_cache, page_ids):
    owners = lax.axis_size("ctx")
    ctx_dev = idx_keys.shape[0]
    exchange = functools.partial(
        lax.all_to_all, axis_name="ctx", split_axis=0, concat_axis=0, tiled=True
    )

    table = request_table(page_ids, owners, ctx_dev // PAGE)
    tiles = tile_pages(latent_cache.T)
    pages = exchange(pack_pages(exchange(table), tiles))

    own = head_parts(idx_query, idx_weight)
    pair = jnp.stack([own, swap(own, "ctx", 1)])
    line = jnp.concatenate([pair] + [swap(pair, "ctx", d << 1) for d in range(1, 4)], axis=0)
    plane = [line] + [swap(line, "ctx", d << 3) for d in range(1, 4)]
    scores = index_scores(plane, idx_keys)
    scores = scores.reshape(4, 4, 2, *scores.shape[2:])
    scores = jnp.stack([scores[:, :, 0], swap(scores[:, :, 1], "ctx", 1)], axis=2)
    scores = jnp.concatenate(
        [scores[:, 0]] + [swap(scores[:, d], "ctx", d << 1) for d in range(1, 4)], axis=1
    )
    scores = [scores[0]] + [swap(scores[d], "ctx", d << 3) for d in range(1, 4)]
    me = lax.axis_index("ctx").astype(jnp.int32).reshape(1)
    index_logp = log_distribution(me, scores).reshape(1, -1)

    latent_out = attend(table, q_latent.reshape(H, DK), pages).reshape(1, -1)
    return (index_logp, latent_out)


def solution(mesh):
    in_specs = (
        P("ctx", "qry"),
        P("ctx", "qry"),
        P("ctx", None),
        P(("ctx", "qry"), None),
        P("ctx", None),
        P(("ctx", "qry"), None),
    )
    out_specs = (P(("ctx", "qry"), None), P(("ctx", "qry"), None))
    return jax.shard_map(
        per_device, mesh=mesh, in_specs=in_specs, out_specs=out_specs, check_vma=False
    )
```

time: 144 us -> 151 us (1.049)
  starting transfers between devices: 37.1 us -> 49.5 us
  waiting for transfers between devices: 70.9 us -> 66.6 us
  other arithmetic: 3.26 us -> 0.91 us
  Pallas kernels: 19.6 us -> 21.8 us
    all_to_all x5 -> x2, waiting for transfers between devices: 70.9 us -> 0.01 us  [per_device(): pages = exchange(pack_pages(exchange(table), tiles))]
    ppermute x0 -> x21, waiting for transfers between devices: none -> 66.6 us  [swap(): return lax.ppermute(x, axis, [(i, i ^ bits) for i in range(size)])]
    ppermute x0 -> x21, starting transfers between devices: none -> 32.8 us  [swap(): return lax.ppermute(x, axis, [(i, i ^ bits) for i in range(size)])]
    all_to_all x5 -> x2, starting transfers between devices: 37.1 us -> 16.7 us  [per_device(): pages = exchange(pack_pages(exchange(table), tiles))]
    pallas_call x4 -> x6, Pallas kernels: 19.6 us -> 21.8 us  [the longest x1 6.87 us: index_scores(): pl.pallas_call(score_kernel, grid=(rows,), in_specs=[pl.BlockSpec(keys.sh...]
    unnamed x9 -> x27, local copies, waits for them, and re-layouts: 7.29 us -> 7.88 us
  transfers between devices with their start and end apart: 5 -> 23, of which waited for: 4 -> 10; matrix products, arithmetic and copies ran while one was open for 5% -> 1% of each run, Pallas kernels for 8% -> 11%
where the time goes in v2:
time: 151 us; the launch traced here: 149 us
  waiting for transfers between devices  66.6 us (44%)
  starting transfers between devices  49.5 us (33%)
  Pallas kernels  21.8 us (14%)
  local copies, waits for them, and re-layouts  8.91 us (6%)
    ppermute x21, waiting for transfers between devices, swap(): return lax.ppermute(x, axis, [(i, i ^ bits) for i in range(size)])  66.6 us
    ppermute x21, starting transfers between devices, swap(): return lax.ppermute(x, axis, [(i, i ^ bits) for i in range(size)])  32.8 us
    all_to_all x2, starting transfers between devices, per_device(): pages = exchange(pack_pages(exchange(table), tiles))  16.7 us
    unnamed x27, local copies, waits for them, and re-layouts  7.88 us
    pallas_call x1, Pallas kernels, index_scores(): pl.pallas_call(score_kernel, grid=(rows,), in_specs=[pl.BlockSpec(keys.sh...  6.87 us
    pallas_call x1, Pallas kernels, attend(): pl.pallas_call(attend_kernel, grid=(peers // sources,), in_specs=[pl.Bloc...  5.72 us
    pallas_call x1, Pallas kernels, pack_pages(): pl.pallas_call(pack_kernel, grid=(peers // rows,), in_specs=[pl.BlockSpec...  5.15 us
  transfers between devices with their start and end apart: 23, of which 10 were waited for; matrix products, arithmetic and copies ran while one was open for 1% of the time, Pallas kernels for 11%

profile of v2, /device:TPU:1, one launch (start us, length us, event | category | flops | bytes accessed | tf_op | source)
XLA Modules:
  0.0 148.6 jit_solution(12357133131050706352)
XLA Ops:
  0.7 0.7 copy.22
  1.4 0.7 copy.10
  2.1 2.6 %collective-permute-start = (bf16[16,128]{1,0:T(8,128)(2,1)S(1)}, bf16[16,128]{1,0:T(8,128)(2,1)S(1)}, u32[]{:S(2)}, u32[]{:S(2)}) collective-permute-start(bf16[16,128]{1,0:T(8,128)(2,1)S(1)} %get-tuple-element.19), channel_id=1, source_target_pairs={{0,1},{1,0},{2,3},{3,2},{4,5},{5,4},{6,7},{7,6},{8,9},{9,8},{10,11... | collective-permute-start | bytes 12296 | tf_op jit(solution)/shard_map/ppermute | solution.py:245
  4.7 4.7 %collective-permute-start.6 = (bf16[16,128]{1,0:T(8,128)(2,1)S(1)}, bf16[16,128]{1,0:T(8,128)(2,1)S(1)}, u32[]{:S(2)}, u32[]{:S(2)}) collective-permute-start(bf16[16,128]{1,0:T(8,128)(2,1)S(1)} %get-tuple-element.13), channel_id=1, source_target_pairs={{0,7},{1,6},{2,5},{3,4},{4,3},{5,2},{6,1},{7,0},{8,15},{9,14},{10,... | collective-permute-start | bytes 12296 | tf_op jit(solution)/shard_map/ppermute | solution.py:245
  9.3 0.5 collective-permute-start.5
  9.8 3.6 %collective-permute-start.4 = (bf16[16,128]{1,0:T(8,128)(2,1)S(1)}, bf16[16,128]{1,0:T(8,128)(2,1)S(1)}, u32[]{:S(2)}, u32[]{:S(2)}) collective-permute-start(bf16[16,128]{1,0:T(8,128)(2,1)S(1)} %get-tuple-element.15), channel_id=1, source_target_pairs={{0,5},{1,4},{2,7},{3,6},{4,1},{5,0},{6,3},{7,2},{8,13},{9,12},{10,... | collective-permute-start | bytes 12296 | tf_op jit(solution)/shard_map/ppermute | solution.py:245
  13.4 1.8 %collective-permute-start.3 = (bf16[16,128]{1,0:T(8,128)(2,1)S(1)}, bf16[16,128]{1,0:T(8,128)(2,1)S(1)}, u32[]{:S(2)}, u32[]{:S(2)}) collective-permute-start(bf16[16,128]{1,0:T(8,128)(2,1)S(1)} %get-tuple-element.16), channel_id=1, source_target_pairs={{0,4},{1,5},{2,6},{3,7},{4,0},{5,1},{6,2},{7,3},{8,12},{9,13},{10,... | collective-permute-start | bytes 12296 | tf_op jit(solution)/shard_map/ppermute | solution.py:245
  15.2 1.4 request_table.1.used_ref
  16.6 8.9 %all-to-all-start = ((s32[32,1,128]{2,1,0:T(1,128)}), s32[32,1,128]{2,1,0:T(1,128)S(1)}, u32[]{:S(2)}, u32[]{:S(2)}) async-start(s32[32,1,128]{2,1,0:T(1,128)} %request_table.1.used_ref), calls=%async_computation | async-start | bytes 32768 | tf_op jit(solution)/shard_map/all_to_all | solution.py:279
  25.5 1.7 %copy-done.2 = bf16[2048,576]{0,1:T(8,128)(2,1)S(1)} copy-done((bf16[2048,576]{0,1:T(8,128)(2,1)S(1)}, bf16[2048,576]{0,1:T(8,128)(2,1)}, u32[]{:S(2)}) %copy-start.2) | copy-done | bytes 2359320
  27.2 1.6 %tile_pages.1.tile_ref = bf16[2,16,576,128]{3,2,1,0:T(8,128)(2,1)S(1)} custom-call(bf16[576,2048]{1,0:T(8,128)(2,1)S(1)} %bitcast.73), custom_call_target="tpu_custom_call" | custom-call | bytes 7340032 | tf_op jit(solution)/shard_map/tile_pages/pallas_call | solution.py:58
  28.8 2.1 %copy-done = bf16[2,16,576,128]{3,2,1,0:T(8,128)(2,1)} copy-done((bf16[2,16,576,128]{3,2,1,0:T(8,128)(2,1)}, bf16[2,16,576,128]{3,2,1,0:T(8,128)(2,1)S(1)}, u32[]{:S(2)}) %copy-start) | copy-done | bytes 4718616
  30.9 1.6 %collective-permute-start.2 = (bf16[16,128]{1,0:T(8,128)(2,1)S(1)}, bf16[16,128]{1,0:T(8,128)(2,1)S(1)}, u32[]{:S(2)}, u32[]{:S(2)}) collective-permute-start(bf16[16,128]{1,0:T(8,128)(2,1)S(1)} %get-tuple-element.17), channel_id=1, source_target_pairs={{0,3},{1,2},{2,1},{3,0},{4,7},{5,6},{6,5},{7,4},{8,11},{9,10},{10,... | collective-permute-start | bytes 12296 | tf_op jit(solution)/shard_map/ppermute | solution.py:245
  32.5 0.2 collective-permute-start.1
  32.8 2.3 %copy-done.1 = bf16[2,16,576,128]{3,2,1,0:T(8,128)(2,1)S(1)} copy-done((bf16[2,16,576,128]{3,2,1,0:T(8,128)(2,1)S(1)}, bf16[2,16,576,128]{3,2,1,0:T(8,128)(2,1)}, u32[]{:S(2)}) %copy-start.1) | copy-done | bytes 4718616
  35.1 5.1 %pack_pages.1 = bf16[32,576,128]{2,1,0:T(8,128)(2,1)} custom-call(s32[32,1,128]{2,1,0:T(1,128)S(1)} %all-to-all-done.table_ref, bf16[2,16,576,128]{3,2,1,0:T(8,128)(2,1)S(1)} %copy-done.1), custom_call_target="tpu_custom_call" | custom-call | bytes 9437184 | tf_op jit(solution)/shard_map/pack_pages/pallas_call | solution.py:85
  40.2 7.8 %all-to-all-start.1 = ((bf16[32,576,128]{2,1,0:T(8,128)(2,1)}), bf16[32,576,128]{2,1,0:T(8,128)(2,1)}, u32[]{:S(2)}, u32[]{:S(2)}) async-start(bf16[32,576,128]{2,1,0:T(8,128)(2,1)} %pack_pages.1), calls=%async_computation.1 | async-start | bytes 9437184 | tf_op jit(solution)/shard_map/all_to_all | solution.py:279
  48.1 0.0 copy-start.5
  48.2 0.1 concatenate.17
  48.4 0.4 collective-permute-start.7
  48.8 0.9 collective-permute-done.7
  49.7 1.4 collective-permute-start.8
  51.1 2.4 %collective-permute-start.9 = (bf16[2,80,128]{2,1,0:T(8,128)(2,1)S(1)}, bf16[2,80,128]{2,1,0:T(8,128)(2,1)S(1)}, u32[]{:S(2)}, u32[]{:S(2)}) collective-permute-start(bf16[2,80,128]{2,1,0:T(8,128)(2,1)S(1)} %pad_maximum_fusion.1), channel_id=1, source_target_pairs={{0,32},{8,40},{16,48},{24,56},{32,0},{40,8},{48,16},{56,24},{64,96... | collective-permute-start | bytes 122888 | tf_op jit(solution)/shard_map/ppermute | solution.py:245
  53.5 0.1 collective-permute-start.10
  53.6 50.4 %collective-permute-done.8 = bf16[2,80,128]{2,1,0:T(8,128)(2,1)S(1)} collective-permute-done((bf16[2,80,128]{2,1,0:T(8,128)(2,1)S(1)}, bf16[2,80,128]{2,1,0:T(8,128)(2,1)S(1)}, u32[]{:S(2)}, u32[]{:S(2)}) %collective-permute-start.8) | collective-permute-done | bytes 40992 | tf_op jit(solution)/shard_map/ppermute | solution.py:245
  104.0 2.5 %collective-permute-done.9 = bf16[2,80,128]{2,1,0:T(8,128)(2,1)S(1)} collective-permute-done((bf16[2,80,128]{2,1,0:T(8,128)(2,1)S(1)}, bf16[2,80,128]{2,1,0:T(8,128)(2,1)S(1)}, u32[]{:S(2)}, u32[]{:S(2)}) %collective-permute-start.9) | collective-permute-done | bytes 40992 | tf_op jit(solution)/shard_map/ppermute | solution.py:245
  106.6 1.6 %collective-permute-start.11 = (bf16[8,80,128]{2,1,0:T(8,128)(2,1)S(1)}, bf16[8,80,128]{2,1,0:T(8,128)(2,1)S(1)}, u32[]{:S(2)}, u32[]{:S(2)}) collective-permute-start(bf16[8,80,128]{2,1,0:T(8,128)(2,1)S(1)} %constant_dynamic-update-slice_fusion.9.refs_0_), channel_id=1, source_target_pairs={{0,64},{8,72},{16,80},{24,88},{32,96},{40,104},{48,112},{56,120},{... | collective-permute-start | bytes 491528 | tf_op jit(solution)/shard_map/ppermute | solution.py:245
  108.1 2.5 %collective-permute-start.12 = (bf16[8,80,128]{2,1,0:T(8,128)(2,1)S(1)}, bf16[8,80,128]{2,1,0:T(8,128)(2,1)S(1)}, u32[]{:S(2)}, u32[]{:S(2)}) collective-permute-start(bf16[8,80,128]{2,1,0:T(8,128)(2,1)S(1)} %constant_dynamic-update-slice_fusion.9.refs_0_), channel_id=1, source_target_pairs={{0,128},{8,136},{16,144},{24,152},{32,160},{40,168},{48,176},{56,1... | collective-permute-start | bytes 491528 | tf_op jit(solution)/shard_map/ppermute | solution.py:245
  110.7 0.8 collective-permute-done.11.refs_1_
  111.5 5.7 %collective-permute-done.12.refs_2_ = bf16[8,80,128]{2,1,0:T(8,128)(2,1)S(1)} collective-permute-done((bf16[8,80,128]{2,1,0:T(8,128)(2,1)S(1)}, bf16[8,80,128]{2,1,0:T(8,128)(2,1)S(1)}, u32[]{:S(2)}, u32[]{:S(2)}) %collective-permute-start.12) | collective-permute-done | bytes 163872 | tf_op jit(solution)/shard_map/ppermute | solution.py:245
  117.3 2.8 %collective-permute-done.13.refs_3_ = bf16[8,80,128]{2,1,0:T(8,128)(2,1)S(1)} collective-permute-done((bf16[8,80,128]{2,1,0:T(8,128)(2,1)S(1)}, bf16[8,80,128]{2,1,0:T(8,128)(2,1)S(1)}, u32[]{:S(2)}, u32[]{:S(2)}) %collective-permute-start.13) | collective-permute-done | bytes 163872 | tf_op jit(solution)/shard_map/ppermute | solution.py:245
  120.0 6.9 %index_scores.1 = bf16[4,8,16,128]{3,2,1,0:T(8,128)(2,1)S(1)} custom-call(bf16[2048,128]{1,0:T(8,128)(2,1)S(1)} %copy-done.4, bf16[8,80,128]{2,1,0:T(8,128)(2,1)S(1)} %constant_dynamic-update-slice_fusion.9.refs_0_, bf16[8,80,128]{2,1,0:T(8,128)(2,1)S(1)} %collective-permute-done.11.refs_1_, bf16[8,80,128]{2,1,0:T(8,128)(2,1)S(1)} %collective-permute-done.12.refs_2_, ...), custom_call_target="tpu_custom_call" | custom-call | flops 1073741824 | bytes 2097152 | tf_op jit(solution)/shard_map/index_scores/pallas_call | solution.py:126
  127.0 1.6 %collective-permute-start.14 = (bf16[4,4,16,128]{3,2,0,1:T(8,128)(2,1)S(1)}, bf16[4,4,16,128]{3,2,0,1:T(8,128)(2,1)S(1)}, u32[]{:S(2)}, u32[]{:S(2)}) collective-permute-start(bf16[4,4,16,128]{3,2,0,1:T(8,128)(2,1)S(1)} %bitcast.80), channel_id=1, source_target_pairs={{0,8},{8,0},{16,24},{24,16},{32,40},{40,32},{48,56},{56,48},{64,72... | collective-permute-start | bytes 196616 | tf_op jit(solution)/shard_map/ppermute | solution.py:245
  128.6 0.9 collective-permute-done.14
  129.5 0.1 collective-permute-start.15
  129.6 0.8 collective-permute-start.16
  130.4 3.0 %collective-permute-start.17 = (bf16[4,2,16,128]{3,2,1,0:T(8,128)(2,1)S(1)}, bf16[4,2,16,128]{3,2,1,0:T(8,128)(2,1)S(1)}, u32[]{:S(2)}, u32[]{:S(2)}) collective-permute-start(bf16[4,2,16,128]{3,2,1,0:T(8,128)(2,1)S(1)} %get-tuple-element.8), channel_id=1, source_target_pairs={{0,48},{8,56},{16,32},{24,40},{32,16},{40,24},{48,0},{56,8},{64,11... | collective-permute-start | bytes 98312 | tf_op jit(solution)/shard_map/ppermute | solution.py:245
  133.5 0.7 collective-permute-done.16
  134.1 1.1 collective-permute-done.17
  135.3 0.1 collective-permute-start.18
  135.4 1.6 %collective-permute-start.19 = (bf16[8,16,128]{2,1,0:T(8,128)(2,1)S(1)}, bf16[8,16,128]{2,1,0:T(8,128)(2,1)S(1)}, u32[]{:S(2)}, u32[]{:S(2)}) collective-permute-start(bf16[8,16,128]{2,1,0:T(8,128)(2,1)S(1)} %get-tuple-element.3), channel_id=1, source_target_pairs={{0,128},{8,136},{16,144},{24,152},{32,160},{40,168},{48,176},{56,1... | collective-permute-start | bytes 98312 | tf_op jit(solution)/shard_map/ppermute | solution.py:245
  137.0 2.2 %collective-permute-start.20 = (bf16[8,16,128]{2,1,0:T(8,128)(2,1)S(1)}, bf16[8,16,128]{2,1,0:T(8,128)(2,1)S(1)}, u32[]{:S(2)}, u32[]{:S(2)}) collective-permute-start(bf16[8,16,128]{2,1,0:T(8,128)(2,1)S(1)} %get-tuple-element.2), channel_id=1, source_target_pairs={{0,192},{8,200},{16,208},{24,216},{32,224},{40,232},{48,240},{56,2... | collective-permute-start | bytes 98312 | tf_op jit(solution)/shard_map/ppermute | solution.py:245
  139.2 0.9 reduce
  140.1 0.2 reshape.27.query_ref
  140.3 0.7 collective-permute-done.20.refs_3_
  141.0 1.0 log_distribution.1
  142.0 5.7 %attend.1 = bf16[128,512]{1,0:T(8,128)(2,1)S(1)} custom-call(s32[32,1,128]{2,1,0:T(1,128)S(1)} %copy-done.3, bf16[128,576]{1,0:T(8,128)(2,1)S(1)} %reshape.27.query_ref, bf16[32,576,128]{2,1,0:T(8,128)(2,1)} %all-to-all-done.1.page_ref), custom_call_target="tpu_custom_call" | custom-call | flops 1140850688 | bytes 5242880 | tf_op jit(solution)/shard_map/attend/pallas_call | solution.py:218
  147.7 0.9 copy.16
  (52 shorter events, 0.3 us)
Async XLA Ops:
  2.1 28.8 %collective-permute-start = (bf16[16,128]{1,0:T(8,128)(2,1)S(1)}, bf16[16,128]{1,0:T(8,128)(2,1)S(1)}, u32[]{:S(2)}, u32[]{:S(2)}) collective-permute-start(bf16[16,128]{1,0:T(8,128)(2,1)S(1)} %get-tuple-element.19), channel_id=1, source_target_pairs={{0,1},{1,0},{2,3},{3,2},{4,5},{5,4},{6,7},{7,6},{8,9},{9,8},{10,11... | collective-permute-start | bytes 12296 | tf_op jit(solution)/shard_map/ppermute | solution.py:245
  4.7 27.9 %collective-permute-start.6 = (bf16[16,128]{1,0:T(8,128)(2,1)S(1)}, bf16[16,128]{1,0:T(8,128)(2,1)S(1)}, u32[]{:S(2)}, u32[]{:S(2)}) collective-permute-start(bf16[16,128]{1,0:T(8,128)(2,1)S(1)} %get-tuple-element.13), channel_id=1, source_target_pairs={{0,7},{1,6},{2,5},{3,4},{4,3},{5,2},{6,1},{7,0},{8,15},{9,14},{10,... | collective-permute-start | bytes 12296 | tf_op jit(solution)/shard_map/ppermute | solution.py:245
  9.3 23.4 %collective-permute-start.5 = (bf16[16,128]{1,0:T(8,128)(2,1)S(1)}, bf16[16,128]{1,0:T(8,128)(2,1)S(1)}, u32[]{:S(2)}, u32[]{:S(2)}) collective-permute-start(bf16[16,128]{1,0:T(8,128)(2,1)S(1)} %get-tuple-element.14), channel_id=1, source_target_pairs={{0,6},{1,7},{2,4},{3,5},{4,2},{5,3},{6,0},{7,1},{8,14},{9,15},{10,... | collective-permute-start | bytes 12296 | tf_op jit(solution)/shard_map/ppermute | solution.py:245
  9.8 38.3 %collective-permute-start.4 = (bf16[16,128]{1,0:T(8,128)(2,1)S(1)}, bf16[16,128]{1,0:T(8,128)(2,1)S(1)}, u32[]{:S(2)}, u32[]{:S(2)}) collective-permute-start(bf16[16,128]{1,0:T(8,128)(2,1)S(1)} %get-tuple-element.15), channel_id=1, source_target_pairs={{0,5},{1,4},{2,7},{3,6},{4,1},{5,0},{6,3},{7,2},{8,13},{9,12},{10,... | collective-permute-start | bytes 12296 | tf_op jit(solution)/shard_map/ppermute | solution.py:245
  13.4 34.8 %collective-permute-start.3 = (bf16[16,128]{1,0:T(8,128)(2,1)S(1)}, bf16[16,128]{1,0:T(8,128)(2,1)S(1)}, u32[]{:S(2)}, u32[]{:S(2)}) collective-permute-start(bf16[16,128]{1,0:T(8,128)(2,1)S(1)} %get-tuple-element.16), channel_id=1, source_target_pairs={{0,4},{1,5},{2,6},{3,7},{4,0},{5,1},{6,2},{7,3},{8,12},{9,13},{10,... | collective-permute-start | bytes 12296 | tf_op jit(solution)/shard_map/ppermute | solution.py:245
  16.6 16.1 %all-to-all-start = ((s32[32,1,128]{2,1,0:T(1,128)}), s32[32,1,128]{2,1,0:T(1,128)S(1)}, u32[]{:S(2)}, u32[]{:S(2)}) async-start(s32[32,1,128]{2,1,0:T(1,128)} %request_table.1.used_ref), calls=%async_computation | async-start | bytes 32768 | tf_op jit(solution)/shard_map/all_to_all | solution.py:279
  25.5 1.7 %copy-start.2 = (bf16[2048,576]{0,1:T(8,128)(2,1)S(1)}, bf16[2048,576]{0,1:T(8,128)(2,1)}, u32[]{:S(2)}) copy-start(bf16[2048,576]{0,1:T(8,128)(2,1)} %param.10) | copy-start | bytes 7077892
  28.8 2.2 %copy-start = (bf16[2,16,576,128]{3,2,1,0:T(8,128)(2,1)}, bf16[2,16,576,128]{3,2,1,0:T(8,128)(2,1)S(1)}, u32[]{:S(2)}) copy-start(bf16[2,16,576,128]{3,2,1,0:T(8,128)(2,1)S(1)} %tile_pages.1.tile_ref) | copy-start | bytes 14155780
  30.9 17.2 %collective-permute-start.2 = (bf16[16,128]{1,0:T(8,128)(2,1)S(1)}, bf16[16,128]{1,0:T(8,128)(2,1)S(1)}, u32[]{:S(2)}, u32[]{:S(2)}) collective-permute-start(bf16[16,128]{1,0:T(8,128)(2,1)S(1)} %get-tuple-element.17), channel_id=1, source_target_pairs={{0,3},{1,2},{2,1},{3,0},{4,7},{5,6},{6,5},{7,4},{8,11},{9,10},{10,... | collective-permute-start | bytes 12296 | tf_op jit(solution)/shard_map/ppermute | solution.py:245
  32.5 15.6 %collective-permute-start.1 = (bf16[16,128]{1,0:T(8,128)(2,1)S(1)}, bf16[16,128]{1,0:T(8,128)(2,1)S(1)}, u32[]{:S(2)}, u32[]{:S(2)}) collective-permute-start(bf16[16,128]{1,0:T(8,128)(2,1)S(1)} %get-tuple-element.18), channel_id=1, source_target_pairs={{0,2},{1,3},{2,0},{3,1},{4,6},{5,7},{6,4},{7,5},{8,10},{9,11},{10,... | collective-permute-start | bytes 12296 | tf_op jit(solution)/shard_map/ppermute | solution.py:245
  32.8 2.3 %copy-start.1 = (bf16[2,16,576,128]{3,2,1,0:T(8,128)(2,1)S(1)}, bf16[2,16,576,128]{3,2,1,0:T(8,128)(2,1)}, u32[]{:S(2)}) copy-start(bf16[2,16,576,128]{3,2,1,0:T(8,128)(2,1)} %copy-done) | copy-start | bytes 14155780
  40.2 79.8 %copy-start.4 = (bf16[2048,128]{1,0:T(8,128)(2,1)S(1)}, bf16[2048,128]{1,0:T(8,128)(2,1)}, u32[]{:S(2)}) copy-start(bf16[2048,128]{1,0:T(8,128)(2,1)} %key_ref.1) | copy-start | bytes 1572868
  40.2 101.8 %all-to-all-start.1 = ((bf16[32,576,128]{2,1,0:T(8,128)(2,1)}), bf16[32,576,128]{2,1,0:T(8,128)(2,1)}, u32[]{:S(2)}, u32[]{:S(2)}) async-start(bf16[32,576,128]{2,1,0:T(8,128)(2,1)} %pack_pages.1), calls=%async_computation.1 | async-start | bytes 9437184 | tf_op jit(solution)/shard_map/all_to_all | solution.py:279
  48.1 91.1 %copy-start.5 = (bf16[1,73728]{1,0:T(2,128)(2,1)S(1)}, bf16[1,73728]{1,0:T(2,128)(2,1)}, u32[]{:S(2)}) copy-start(bf16[1,73728]{1,0:T(2,128)(2,1)} %param.9) | copy-start | bytes 442372
  48.1 93.9 %copy-start.3 = (s32[32,1,128]{2,1,0:T(1,128)S(1)}, s32[32,1,128]{2,1,0:T(1,128)}, u32[]{:S(2)}) copy-start(s32[32,1,128]{2,1,0:T(1,128)} %request_table.1.used_ref) | copy-start | bytes 49156
  48.4 1.3 collective-permute-start.7
  49.7 54.3 %collective-permute-start.8 = (bf16[2,80,128]{2,1,0:T(8,128)(2,1)S(1)}, bf16[2,80,128]{2,1,0:T(8,128)(2,1)S(1)}, u32[]{:S(2)}, u32[]{:S(2)}) collective-permute-start(bf16[2,80,128]{2,1,0:T(8,128)(2,1)S(1)} %pad_maximum_fusion.1), channel_id=1, source_target_pairs={{0,16},{8,24},{16,0},{24,8},{32,48},{40,56},{48,32},{56,40},{64,80... | collective-permute-start | bytes 122888 | tf_op jit(solution)/shard_map/ppermute | solution.py:245
  51.1 55.5 %collective-permute-start.9 = (bf16[2,80,128]{2,1,0:T(8,128)(2,1)S(1)}, bf16[2,80,128]{2,1,0:T(8,128)(2,1)S(1)}, u32[]{:S(2)}, u32[]{:S(2)}) collective-permute-start(bf16[2,80,128]{2,1,0:T(8,128)(2,1)S(1)} %pad_maximum_fusion.1), channel_id=1, source_target_pairs={{0,32},{8,40},{16,48},{24,56},{32,0},{40,8},{48,16},{56,24},{64,96... | collective-permute-start | bytes 122888 | tf_op jit(solution)/shard_map/ppermute | solution.py:245
  53.5 53.1 %collective-permute-start.10 = (bf16[2,80,128]{2,1,0:T(8,128)(2,1)S(1)}, bf16[2,80,128]{2,1,0:T(8,128)(2,1)S(1)}, u32[]{:S(2)}, u32[]{:S(2)}) collective-permute-start(bf16[2,80,128]{2,1,0:T(8,128)(2,1)S(1)} %pad_maximum_fusion.1), channel_id=1, source_target_pairs={{0,48},{8,56},{16,32},{24,40},{32,16},{40,24},{48,0},{56,8},{64,11... | collective-permute-start | bytes 122888 | tf_op jit(solution)/shard_map/ppermute | solution.py:245
  106.6 4.9 %collective-permute-start.11 = (bf16[8,80,128]{2,1,0:T(8,128)(2,1)S(1)}, bf16[8,80,128]{2,1,0:T(8,128)(2,1)S(1)}, u32[]{:S(2)}, u32[]{:S(2)}) collective-permute-start(bf16[8,80,128]{2,1,0:T(8,128)(2,1)S(1)} %constant_dynamic-update-slice_fusion.9.refs_0_), channel_id=1, source_target_pairs={{0,64},{8,72},{16,80},{24,88},{32,96},{40,104},{48,112},{56,120},{... | collective-permute-start | bytes 491528 | tf_op jit(solution)/shard_map/ppermute | solution.py:245
  108.1 9.1 %collective-permute-start.12 = (bf16[8,80,128]{2,1,0:T(8,128)(2,1)S(1)}, bf16[8,80,128]{2,1,0:T(8,128)(2,1)S(1)}, u32[]{:S(2)}, u32[]{:S(2)}) collective-permute-start(bf16[8,80,128]{2,1,0:T(8,128)(2,1)S(1)} %constant_dynamic-update-slice_fusion.9.refs_0_), channel_id=1, source_target_pairs={{0,128},{8,136},{16,144},{24,152},{32,160},{40,168},{48,176},{56,1... | collective-permute-start | bytes 491528 | tf_op jit(solution)/shard_map/ppermute | solution.py:245
  110.7 9.4 %collective-permute-start.13 = (bf16[8,80,128]{2,1,0:T(8,128)(2,1)S(1)}, bf16[8,80,128]{2,1,0:T(8,128)(2,1)S(1)}, u32[]{:S(2)}, u32[]{:S(2)}) collective-permute-start(bf16[8,80,128]{2,1,0:T(8,128)(2,1)S(1)} %constant_dynamic-update-slice_fusion.9.refs_0_), channel_id=1, source_target_pairs={{0,192},{8,200},{16,208},{24,216},{32,224},{40,232},{48,240},{56,2... | collective-permute-start | bytes 491528 | tf_op jit(solution)/shard_map/ppermute | solution.py:245
  127.0 2.5 %collective-permute-start.14 = (bf16[4,4,16,128]{3,2,0,1:T(8,128)(2,1)S(1)}, bf16[4,4,16,128]{3,2,0,1:T(8,128)(2,1)S(1)}, u32[]{:S(2)}, u32[]{:S(2)}) collective-permute-start(bf16[4,4,16,128]{3,2,0,1:T(8,128)(2,1)S(1)} %bitcast.80), channel_id=1, source_target_pairs={{0,8},{8,0},{16,24},{24,16},{32,40},{40,32},{48,56},{56,48},{64,72... | collective-permute-start | bytes 196616 | tf_op jit(solution)/shard_map/ppermute | solution.py:245
  129.5 4.0 %collective-permute-start.15 = (bf16[4,2,16,128]{3,2,1,0:T(8,128)(2,1)S(1)}, bf16[4,2,16,128]{3,2,1,0:T(8,128)(2,1)S(1)}, u32[]{:S(2)}, u32[]{:S(2)}) collective-permute-start(bf16[4,2,16,128]{3,2,1,0:T(8,128)(2,1)S(1)} %get-tuple-element.7), channel_id=1, source_target_pairs={{0,16},{8,24},{16,0},{24,8},{32,48},{40,56},{48,32},{56,40},{64,80... | collective-permute-start | bytes 98312 | tf_op jit(solution)/shard_map/ppermute | solution.py:245
  129.6 4.5 %collective-permute-start.16 = (bf16[4,2,16,128]{3,2,1,0:T(8,128)(2,1)S(1)}, bf16[4,2,16,128]{3,2,1,0:T(8,128)(2,1)S(1)}, u32[]{:S(2)}, u32[]{:S(2)}) collective-permute-start(bf16[4,2,16,128]{3,2,1,0:T(8,128)(2,1)S(1)} %get-tuple-element.9), channel_id=1, source_target_pairs={{0,32},{8,40},{16,48},{24,56},{32,0},{40,8},{48,16},{56,24},{64,96... | collective-permute-start | bytes 98312 | tf_op jit(solution)/shard_map/ppermute | solution.py:245
  130.4 4.8 %collective-permute-start.17 = (bf16[4,2,16,128]{3,2,1,0:T(8,128)(2,1)S(1)}, bf16[4,2,16,128]{3,2,1,0:T(8,128)(2,1)S(1)}, u32[]{:S(2)}, u32[]{:S(2)}) collective-permute-start(bf16[4,2,16,128]{3,2,1,0:T(8,128)(2,1)S(1)} %get-tuple-element.8), channel_id=1, source_target_pairs={{0,48},{8,56},{16,32},{24,40},{32,16},{40,24},{48,0},{56,8},{64,11... | collective-permute-start | bytes 98312 | tf_op jit(solution)/shard_map/ppermute | solution.py:245
  135.3 5.0 %collective-permute-start.18 = (bf16[8,16,128]{2,1,0:T(8,128)(2,1)S(1)}, bf16[8,16,128]{2,1,0:T(8,128)(2,1)S(1)}, u32[]{:S(2)}, u32[]{:S(2)}) collective-permute-start(bf16[8,16,128]{2,1,0:T(8,128)(2,1)S(1)} %get-tuple-element.4), channel_id=1, source_target_pairs={{0,64},{8,72},{16,80},{24,88},{32,96},{40,104},{48,112},{56,120},{... | collective-permute-start | bytes 98312 | tf_op jit(solution)/shard_map/ppermute | solution.py:245
  135.4 4.9 %collective-permute-start.19 = (bf16[8,16,128]{2,1,0:T(8,128)(2,1)S(1)}, bf16[8,16,128]{2,1,0:T(8,128)(2,1)S(1)}, u32[]{:S(2)}, u32[]{:S(2)}) collective-permute-start(bf16[8,16,128]{2,1,0:T(8,128)(2,1)S(1)} %get-tuple-element.3), channel_id=1, source_target_pairs={{0,128},{8,136},{16,144},{24,152},{32,160},{40,168},{48,176},{56,1... | collective-permute-start | bytes 98312 | tf_op jit(solution)/shard_map/ppermute | solution.py:245
  137.0 4.0 %collective-permute-start.20 = (bf16[8,16,128]{2,1,0:T(8,128)(2,1)S(1)}, bf16[8,16,128]{2,1,0:T(8,128)(2,1)S(1)}, u32[]{:S(2)}, u32[]{:S(2)}) collective-permute-start(bf16[8,16,128]{2,1,0:T(8,128)(2,1)S(1)} %get-tuple-element.2), channel_id=1, source_target_pairs={{0,192},{8,200},{16,208},{24,216},{32,224},{40,232},{48,240},{56,2... | collective-permute-start | bytes 98312 | tf_op jit(solution)/shard_map/ppermute | solution.py:245

commit v3 on v2

v3 whole, which is shorter than its diff:
```python
import functools

import jax
import jax.numpy as jnp
from jax import lax
from jax.experimental import pallas as pl
from jax.experimental.pallas import tpu as pltpu
from jax.sharding import PartitionSpec as P

H_IDX = 64
D_IDX = 128
H = 128
D_LAT = 512
D_ROPE = 64
DK = D_LAT + D_ROPE
QK_NOPE = 128
PAGE = 64
TOPP = 32
LANES = 128
NEG = -1e30
MIB = 1 << 20


def request_kernel(pages_dev, ids_ref, query_ref, weight_ref, out_ref, table_ref):
    owners = out_ref.shape[0]
    rows, heads = weight_ref.shape
    ids = ids_ref[...]
    owner, local = ids // pages_dev, ids % pages_dev
    mine = owner == lax.broadcasted_iota(jnp.int32, (owners, TOPP), 0)
    low = jnp.min(jnp.where(mine, local, pages_dev), axis=1, keepdims=True)
    high = jnp.max(jnp.where(mine, local, -1), axis=1, keepdims=True)
    turn = (low < high) & (low % 2 == 1) & (high % 2 == 0)
    first = jnp.where(turn, high, low)
    second = jnp.where(turn, low, high)
    single = low == high
    left = jnp.where((high < 0) | (single & (low % 2 == 1)), 0, first + 1)
    right = jnp.where((high < 0) | (single & (low % 2 == 0)), 0, second + 1)
    lane = lax.broadcasted_iota(jnp.int32, (owners, LANES), 1)
    table = jnp.where(lane == 0, left, jnp.where(lane == 1, right, 0)).reshape(owners, 1, LANES)
    table_ref[...] = table
    weight = jnp.concatenate(
        [weight_ref[...].astype(jnp.float32), jnp.zeros((rows, LANES - heads), jnp.float32)], axis=1
    )
    asked = jnp.broadcast_to(table.astype(jnp.float32), (owners, rows, LANES))
    tail = jnp.concatenate(
        [jnp.broadcast_to(weight[None], (owners, rows, LANES)), asked], axis=1
    )
    out_ref[:, : rows * heads, :] = jnp.broadcast_to(
        query_ref[...][None], (owners, rows * heads, LANES)
    )
    out_ref[:, rows * heads :, :] = tail.astype(out_ref.dtype)


def requests(page_ids, query, weight, owners, pages_dev):
    length = query.shape[0] + 2 * weight.shape[0]
    return pl.pallas_call(
        functools.partial(request_kernel, pages_dev),
        out_shape=(
            pltpu.HBM((owners, length, LANES), query.dtype),
            jax.ShapeDtypeStruct((owners, 1, LANES), jnp.int32),
        ),
        name="requests",
    )(page_ids, query, weight)


def pack_kernel(table_ref, cache_ref, out_ref):
    step = pl.program_id(0)
    rows = out_ref.shape[0]
    left = lax.broadcasted_iota(jnp.int32, (DK, LANES), 1) < PAGE

    def tile(page):
        return cache_ref[:, pl.ds(pl.multiple_of(page // 2 * LANES, LANES), LANES)]

    def turned(x):
        return jnp.concatenate([x[:, PAGE:], x[:, :PAGE]], axis=1)

    for r in range(rows):
        first = table_ref[step * rows + r, 0]
        second = table_ref[step * rows + r, 1]
        first = jnp.where(first > 0, first - 1, 0)
        second = jnp.where(second > 0, second - 1, 1)
        straight = (first % 2 == 0) & (second % 2 == 1)

        @pl.when(straight)
        def _(r=r, first=first, second=second):
            out_ref[r] = jnp.where(left, tile(first), tile(second))

        @pl.when(jnp.logical_not(straight))
        def _(r=r, first=first, second=second):
            a, b = tile(first), tile(second)
            a = jnp.where(first % 2 == 0, a, turned(a))
            b = jnp.where(second % 2 == 1, b, turned(b))
            out_ref[r] = jnp.where(left, a, b)


def pack_pages(table, cache):
    peers = table.shape[0]
    rows = 4
    return pl.pallas_call(
        pack_kernel,
        grid=(peers // rows,),
        in_specs=[
            pl.BlockSpec(memory_space=pltpu.SMEM),
            pl.BlockSpec(cache.shape, lambda i: (0, 0)),
        ],
        out_specs=pl.BlockSpec((rows, DK, LANES), lambda i: (i, 0, 0)),
        out_shape=pltpu.HBM((peers, DK, LANES), cache.dtype),
        compiler_params=pltpu.CompilerParams(vmem_limit_bytes=24 * MIB),
        cost_estimate=pl.CostEstimate(flops=0, bytes_accessed=7 * MIB, transcendentals=0),
        name="pack_pages",
    )(table, cache)


def score_kernel(query_ref, key_ref, out_ref, sum_ref):
    sources = query_ref.shape[0]
    rows = out_ref.shape[0]
    heads = (query_ref.shape[1] - 2 * rows) // rows
    flat = rows * heads
    blocks = key_ref.shape[0] // LANES
    queries = jnp.concatenate([query_ref[i, :flat, :] for i in range(sources)], axis=0)
    weights = []
    for i in range(sources):
        tail = query_ref[i, flat:, :].astype(jnp.float32)[:rows]
        weights.append(
            [jnp.broadcast_to(tail[:, h : h + 1], (rows, LANES)) for h in range(heads)]
        )
    for b in range(blocks // 2):
        keys = key_ref[2 * b * LANES : 2 * (b + 1) * LANES, :]
        dots = lax.dot_general(
            queries, keys, (((1,), (1,)), ((), ())), preferred_element_type=jnp.float32
        )
        for j in range(2):
            for i in range(sources):
                total = None
                for h in range(heads):
                    at = i * flat + h * rows
                    part = (
                        jnp.maximum(dots[at : at + rows, j * LANES : (j + 1) * LANES], 0.0)
                        * weights[i][h]
                    )
                    total = part if total is None else total + part
                sum_ref[i, pl.ds(2 * b + j, rows, stride=blocks), :] = total
    for i in range(sources):
        for r in range(rows):
            out_ref[r, i] = sum_ref[i, r * blocks : (r + 1) * blocks, :]


def index_scores(queries, keys, rows):
    sources = 4
    peers, length = queries.shape[:2]
    blocks = keys.shape[0] // LANES
    return pl.pallas_call(
        score_kernel,
        grid=(peers // sources,),
        in_specs=[
            pl.BlockSpec((sources, length, LANES), lambda i: (i, 0, 0)),
            pl.BlockSpec(keys.shape, lambda i: (0, 0)),
        ],
        out_specs=pl.BlockSpec((rows, sources, blocks, LANES), lambda i: (0, i, 0, 0)),
        out_shape=jax.ShapeDtypeStruct((rows, peers, blocks, LANES), jnp.float32),
        scratch_shapes=[pltpu.VMEM((sources, rows * blocks, LANES), jnp.float32)],
        compiler_params=pltpu.CompilerParams(vmem_limit_bytes=16 * MIB),
        cost_estimate=pl.CostEstimate(
            flops=2 * peers * length * keys.shape[0] * D_IDX,
            bytes_accessed=2 * MIB,
            transcendentals=0,
        ),
        name="index_scores",
    )(queries, keys)


def logp_kernel(score_ref, out_ref):
    scores = score_ref[...].astype(jnp.float32)
    top = jnp.max(scores)
    total = jnp.sum(jnp.exp(scores - top), keepdims=True)
    out_ref[...] = scores - (top + jnp.log(total)) + jnp.log(jnp.float32(scores.size))


def log_distribution(scores):
    return pl.pallas_call(
        logp_kernel,
        out_shape=jax.ShapeDtypeStruct(scores.shape, jnp.float32),
        compiler_params=pltpu.CompilerParams(vmem_limit_bytes=8 * MIB),
        cost_estimate=pl.CostEstimate(
            flops=4 * scores.size, bytes_accessed=6 * scores.size, transcendentals=scores.size
        ),
        name="log_distribution",
    )(scores)


def attend_kernel(used_ref, query_ref, page_ref, out_ref, top_ref, total_ref, sum_ref):
    step = pl.program_id(0)
    sources = page_ref.shape[0]

    @pl.when(step == 0)
    def _():
        top_ref[...] = jnp.full_like(top_ref, NEG)
        total_ref[...] = jnp.zeros_like(total_ref)
        sum_ref[...] = jnp.zeros_like(sum_ref)

    left = lax.broadcasted_iota(jnp.int32, (1, LANES), 1) < PAGE
    live = []
    for i in range(sources):
        slots = [
            jnp.where(used_ref[step * sources + i, 0, s] > 0, 0.0, NEG) for s in range(2)
        ]
        live.append(jnp.where(left, slots[0], slots[1]))
    live = jnp.concatenate(live, axis=1)
    keys = jnp.concatenate([page_ref[i] for i in range(sources)], axis=1)
    scale = (QK_NOPE + D_ROPE) ** (-0.5)
    logits = jnp.dot(query_ref[...], keys, preferred_element_type=jnp.float32) * scale + live
    old = top_ref[...]
    new = jnp.maximum(old, jnp.max(logits, axis=1, keepdims=True))
    fade = jnp.exp(old - new)
    top_ref[...] = new
    expo = jnp.exp(logits - new[:, :1])
    total_ref[...] = total_ref[...] * fade + jnp.sum(expo, axis=1, keepdims=True)
    mixed = lax.dot_general(
        expo.astype(jnp.bfloat16),
        keys[:D_LAT],
        (((1,), (1,)), ((), ())),
        preferred_element_type=jnp.float32,
    )
    sum_ref[...] = sum_ref[...] * fade[:, :1] + mixed

    @pl.when(step == pl.num_programs(0) - 1)
    def _():
        out_ref[...] = (sum_ref[...] / total_ref[...][:, :1]).astype(out_ref.dtype)


def attend(used, query, pages):
    sources = 8
    peers = pages.shape[0]
    tokens = peers * LANES
    return pl.pallas_call(
        attend_kernel,
        grid=(peers // sources,),
        in_specs=[
            pl.BlockSpec(memory_space=pltpu.SMEM),
            pl.BlockSpec((H, DK), lambda i: (0, 0)),
            pl.BlockSpec((sources, DK, LANES), lambda i: (i, 0, 0)),
        ],
        out_specs=pl.BlockSpec((H, D_LAT), lambda i: (0, 0)),
        scratch_shapes=[
            pltpu.VMEM((H, LANES), jnp.float32),
            pltpu.VMEM((H, LANES), jnp.float32),
            pltpu.VMEM((H, D_LAT), jnp.float32),
        ],
        out_shape=jax.ShapeDtypeStruct((H, D_LAT), jnp.bfloat16),
        compiler_params=pltpu.CompilerParams(vmem_limit_bytes=24 * MIB),
        cost_estimate=pl.CostEstimate(
            flops=2 * H * tokens * (2 * D_LAT + D_ROPE),
            bytes_accessed=5 * MIB,
            transcendentals=H * tokens,
        ),
        name="attend",
    )(used, query, pages)


def per_device(idx_query, idx_weight, idx_keys, q_latent, latent_cache, page_ids):
    owners = lax.axis_size("ctx")
    rows, heads = idx_weight.shape
    exchange = functools.partial(
        lax.all_to_all, axis_name="ctx", split_axis=0, concat_axis=0, tiled=True
    )

    query = idx_query.reshape(rows, heads, D_IDX).transpose(1, 0, 2).reshape(-1, D_IDX)
    sent, table = requests(page_ids, query, idx_weight, owners, idx_keys.shape[0] // PAGE)
    got = exchange(sent)
    asked = got[:, rows * heads + rows, :2].astype(jnp.int32)
    pages = exchange(pack_pages(asked, latent_cache.T))

    scores = index_scores(got, idx_keys, rows)
    scores = lax.psum_scatter(scores, "qry", scatter_dimension=0)
    scores, pages = lax.optimization_barrier((scores, pages))
    scores = exchange(scores.astype(jnp.bfloat16))
    index_logp = log_distribution(scores.reshape(-1, LANES)).reshape(1, -1)

    latent_out = attend(table, q_latent.reshape(H, DK), pages).reshape(1, -1)
    return (index_logp, latent_out)


def solution(mesh):
    in_specs = (
        P("ctx", "qry"),
        P("ctx", "qry"),
        P("ctx", None),
        P(("ctx", "qry"), None),
        P("ctx", None),
        P(("ctx", "qry"), None),
    )
    out_specs = (P(("ctx", "qry"), None), P(("ctx", "qry"), None))
    return jax.shard_map(
        per_device, mesh=mesh, in_specs=in_specs, out_specs=out_specs, check_vma=False
    )
```

time: 151 us -> 125 us (0.83); the launches traced: 149 us -> 125 us
  starting transfers between devices: 49.5 us -> 13 us
  blocking collectives: 0 us -> 21.5 us
  waiting for transfers between devices: 66.6 us -> 50.5 us
  between operations: 0.96 us -> 14.1 us
  local copies, waits for them, and re-layouts: 8.91 us -> 2.73 us
  Pallas kernels: 21.8 us -> 20.1 us
  other arithmetic: 0.91 us -> 2.5 us
    ppermute x21 -> x0, waiting for transfers between devices: 66.6 us -> none  [swap(): return lax.ppermute(x, axis, [(i, i ^ bits) for i in range(size)])]
    reduce_scatter x0 -> x1, waiting for transfers between devices: none -> 41.1 us  [per_device(): scores = lax.psum_scatter(scores, 'qry', scatter_dimension=0)]
    ppermute x21 -> x0, starting transfers between devices: 32.8 us -> none  [swap(): return lax.ppermute(x, axis, [(i, i ^ bits) for i in range(size)])]
    all_to_all x0 -> x1, blocking collectives: none -> 21.5 us  [per_device(): got = exchange(sent)]
    all_to_all x2, waiting for transfers between devices: 0.01 us -> 9.39 us  [the longest x1 9.34 us: per_device(): pages = exchange(pack_pages(asked, latent_cache.T))]
    unnamed x27 -> x9, local copies, waits for them, and re-layouts: 7.88 us -> 2.58 us
    all_to_all x2, starting transfers between devices: 16.7 us -> 13 us  [the longest x1 7.83 us: per_device(): scores = exchange(scores.astype(jnp.bfloat16))]
    pallas_call x4 -> x3, Pallas kernels: 10.9 us -> 8.13 us  [the longest x1 5.26 us: index_scores(): pl.pallas_call(score_kernel, grid=(peers // sources,), in_specs=[pl.Block...]
  transfers between devices with their start and end apart: 23 -> 3, of which waited for: 10 -> 2; matrix products, arithmetic and copies ran while one was open for 1% -> 2% of each run, Pallas kernels for 11% -> 9%
where the time goes in v3:
time: 125 us
  waiting for transfers between devices  50.5 us (40%)
  blocking collectives  21.5 us (17%)
  Pallas kernels  20.1 us (16%)
  between operations  14.1 us (11%)
  starting transfers between devices  13 us (10%)
  local copies, waits for them, and re-layouts  2.73 us (2%)
  other arithmetic  2.5 us (2%)
    reduce_scatter x1, waiting for transfers between devices, per_device(): scores = lax.psum_scatter(scores, 'qry', scatter_dimension=0)  41.1 us
    all_to_all x1, blocking collectives, per_device(): got = exchange(sent)  21.5 us
    all_to_all x1, waiting for transfers between devices, per_device(): pages = exchange(pack_pages(asked, latent_cache.T))  9.34 us
    all_to_all x1, starting transfers between devices, per_device(): scores = exchange(scores.astype(jnp.bfloat16))  7.83 us
    pallas_call x1, Pallas kernels, pack_pages(): pl.pallas_call(pack_kernel, grid=(peers // rows,), in_specs=[pl.BlockSpec...  6.26 us
    pallas_call x1, Pallas kernels, attend(): pl.pallas_call(attend_kernel, grid=(peers // sources,), in_specs=[pl.Bloc...  5.72 us
    pallas_call x1, Pallas kernels, index_scores(): pl.pallas_call(score_kernel, grid=(peers // sources,), in_specs=[pl.Block...  5.26 us
    all_to_all x1, starting transfers between devices, per_device(): pages = exchange(pack_pages(asked, latent_cache.T))  5.14 us
  transfers between devices with their start and end apart: 3, of which 2 were waited for; matrix products, arithmetic and copies ran while one was open for 2% of the time, Pallas kernels for 9%

profile of v3, /device:TPU:1, one launch (start us, length us, event | category | flops | bytes accessed | tf_op | source)
XLA Modules:
  0.0 124.5 jit_solution(4228879271492611149)
XLA Ops:
  7.2 1.8 %requests.1 = (bf16[32,80,128]{2,1,0:T(8,128)(2,1)}, s32[32,1,128]{2,1,0:T(1,128)}) custom-call(s32[1,32]{1,0:T(1,128)} %ids_ref.1, bf16[64,128]{1,0:T(8,128)(2,1)} %bitcast.20, bf16[8,8]{1,0:T(8,128)(2,1)} %weight_ref.1), custom_call_target="tpu_custom_call" | custom-call | tf_op jit(solution)/shard_map/requests/pallas_call | solution.py:56
  8.9 21.5 %all_to_all.15.query_ref = bf16[32,80,128]{2,1,0:T(8,128)(2,1)S(1)} all-to-all(bf16[32,80,128]{2,1,0:T(8,128)(2,1)} %get-tuple-element.6), channel_id=1, replica_groups=mesh['ctx'=32,'qry'=8] {'ctx'}, dimensions={0} | all-to-all | bytes 1310720 | tf_op jit(solution)/shard_map/all_to_all | solution.py:269
  30.5 0.0 copy-start
  30.5 1.7 %copy-done = bf16[2048,576]{0,1:T(8,128)(2,1)S(1)} copy-done((bf16[2048,576]{0,1:T(8,128)(2,1)S(1)}, bf16[2048,576]{0,1:T(8,128)(2,1)}, u32[]{:S(2)}) %copy-start) | copy-done | bytes 2359320
  32.1 6.3 %pack_pages.1 = bf16[32,576,128]{2,1,0:T(8,128)(2,1)} custom-call(s32[32,2]{1,0:T(8,128)S(1)} %bitcast.16, bf16[576,2048]{1,0:T(8,128)(2,1)S(1)} %bitcast.13), custom_call_target="tpu_custom_call" | custom-call | bytes 7340032 | tf_op jit(solution)/shard_map/pack_pages/pallas_call | solution.py:99
  38.4 0.0 copy-start.2
  38.4 5.1 %all-to-all-start.1 = ((bf16[32,576,128]{2,1,0:T(8,128)(2,1)}), bf16[32,576,128]{2,1,0:T(8,128)(2,1)}, u32[]{:S(2)}, u32[]{:S(2)}) async-start(bf16[32,576,128]{2,1,0:T(8,128)(2,1)} %pack_pages.1), calls=%async_computation.2 | async-start | bytes 9437184 | tf_op jit(solution)/shard_map/all_to_all | solution.py:271
  43.5 0.0 copy-start.3
  43.5 0.0 copy-start.1
  43.6 0.0 reduce-scatter.2.cloned.1.call-start
  43.6 0.0 copy-done.2
  43.6 5.3 %index_scores.1 = f32[8,32,16,128]{3,2,1,0:T(8,128)} custom-call(bf16[32,80,128]{2,1,0:T(8,128)(2,1)S(1)} %all_to_all.15.query_ref, bf16[2048,128]{1,0:T(8,128)(2,1)S(1)} %copy-done.2), custom_call_target="tpu_custom_call" | custom-call | flops 1342177280 | bytes 2097152 | tf_op jit(solution)/shard_map/index_scores/pallas_call | solution.py:152
  48.9 0.0 reduce-scatter.2.cloned.1.call-update
  48.9 41.1 %reduce-scatter.2.cloned.1.call-done = f32[1,32,16,128]{3,2,1,0:T(8,128)} async-done(((f32[8,32,16,128]{3,2,1,0:T(8,128)}), f32[1,32,16,128]{3,2,1,0:T(8,128)}) %reduce-scatter.2.cloned.1.call-update) | async-done | bytes 262160 | tf_op jit(solution)/shard_map/reduce_scatter | solution.py:274
  90.0 9.3 %all-to-all-done.1.page_ref = bf16[32,576,128]{2,1,0:T(8,128)(2,1)} async-done(((bf16[32,576,128]{2,1,0:T(8,128)(2,1)}), bf16[32,576,128]{2,1,0:T(8,128)(2,1)}, u32[]{:S(2)}, u32[]{:S(2)}) %all-to-all-start.1) | async-done | bytes 4718624 | tf_op jit(solution)/shard_map/all_to_all | solution.py:271
  99.4 1.6 %convert_element_type.10 = bf16[32,16,128]{2,1,0:T(8,128)(2,1)} convert(f32[32,16,128]{2,1,0:T(8,128)} %bitcast.18) | non-fusion elementwise | flops 65536 | bytes 393216 | tf_op jit(solution)/shard_map/convert_element_type | solution.py:276
  101.0 7.8 %all-to-all-start.2 = ((bf16[32,16,128]{2,1,0:T(8,128)(2,1)}), bf16[32,16,128]{2,1,0:T(8,128)(2,1)S(1)}, u32[]{:S(2)}, u32[]{:S(2)}) async-start(bf16[32,16,128]{2,1,0:T(8,128)(2,1)} %convert_element_type.10), calls=%async_computation.3 | async-start | bytes 262144 | tf_op jit(solution)/shard_map/all_to_all | solution.py:276
  108.8 0.0 copy-done.3
  108.9 0.9 reduce
  109.7 0.2 reshape.28.query_ref
  109.9 0.0 copy-done.1
  109.9 5.7 %attend.1 = bf16[128,512]{1,0:T(8,128)(2,1)S(1)} custom-call(s32[32,1,128]{2,1,0:T(1,128)S(1)} %copy-done.1, bf16[128,576]{1,0:T(8,128)(2,1)S(1)} %reshape.28.query_ref, bf16[32,576,128]{2,1,0:T(8,128)(2,1)} %all-to-all-done.1.page_ref), custom_call_target="tpu_custom_call" | custom-call | flops 1140850688 | bytes 5242880 | tf_op jit(solution)/shard_map/attend/pallas_call | solution.py:235
  115.6 0.9 copy.15
  116.5 0.0 all-to-all-done.2
  116.6 1.1 log_distribution.1
  (1 shorter events, 0.0 us)
Async XLA Ops:
  30.5 1.7 %copy-start = (bf16[2048,576]{0,1:T(8,128)(2,1)S(1)}, bf16[2048,576]{0,1:T(8,128)(2,1)}, u32[]{:S(2)}) copy-start(bf16[2048,576]{0,1:T(8,128)(2,1)} %param.10) | copy-start | bytes 7077892
  38.4 5.2 %copy-start.2 = (bf16[2048,128]{1,0:T(8,128)(2,1)S(1)}, bf16[2048,128]{1,0:T(8,128)(2,1)}, u32[]{:S(2)}) copy-start(bf16[2048,128]{1,0:T(8,128)(2,1)} %key_ref.1) | copy-start | bytes 1572868
  38.4 61.0 %all-to-all-start.1 = ((bf16[32,576,128]{2,1,0:T(8,128)(2,1)}), bf16[32,576,128]{2,1,0:T(8,128)(2,1)}, u32[]{:S(2)}, u32[]{:S(2)}) async-start(bf16[32,576,128]{2,1,0:T(8,128)(2,1)} %pack_pages.1), calls=%async_computation.2 | async-start | bytes 9437184 | tf_op jit(solution)/shard_map/all_to_all | solution.py:271
  43.5 65.3 %copy-start.3 = (bf16[1,73728]{1,0:T(2,128)(2,1)S(1)}, bf16[1,73728]{1,0:T(2,128)(2,1)}, u32[]{:S(2)}) copy-start(bf16[1,73728]{1,0:T(2,128)(2,1)} %param.9) | copy-start | bytes 442372
  43.5 66.3 %copy-start.1 = (s32[32,1,128]{2,1,0:T(1,128)S(1)}, s32[32,1,128]{2,1,0:T(1,128)}, u32[]{:S(2)}) copy-start(s32[32,1,128]{2,1,0:T(1,128)} %get-tuple-element.8.used_ref) | copy-start | bytes 49156
  43.6 46.5 %reduce-scatter.2.cloned.1.call-start = ((), (), s32[]{:S(2)}) async-start(), calls=%async_computation.4 | async-start | bytes 2359296 | tf_op jit(solution)/shard_map/reduce_scatter | solution.py:274
  101.0 15.6 %all-to-all-start.2 = ((bf16[32,16,128]{2,1,0:T(8,128)(2,1)}), bf16[32,16,128]{2,1,0:T(8,128)(2,1)S(1)}, u32[]{:S(2)}, u32[]{:S(2)}) async-start(bf16[32,16,128]{2,1,0:T(8,128)(2,1)} %convert_element_type.10), calls=%async_computation.3 | async-start | bytes 262144 | tf_op jit(solution)/shard_map/all_to_all | solution.py:276
Sparse Core Ops, SparseCore 0:
  49.0 40.9 reduce-scatter.1

commit v4 on v3

--- a/solution.py
+++ b/solution.py
@@ -42,31 +42,48 @@
         [weight_ref[...].astype(jnp.float32), jnp.zeros((rows, LANES - heads), jnp.float32)], axis=1
     )
     asked = jnp.broadcast_to(table.astype(jnp.float32), (owners, rows, LANES))
-    tail = jnp.concatenate(
-        [jnp.broadcast_to(weight[None], (owners, rows, LANES)), asked], axis=1
-    )
-    out_ref[:, : rows * heads, :] = jnp.broadcast_to(
-        query_ref[...][None], (owners, rows * heads, LANES)
-    )
-    out_ref[:, rows * heads :, :] = tail.astype(out_ref.dtype)
+    out_ref[:, :rows] = jnp.broadcast_to(
+        query_ref[...].reshape(1, rows, heads, LANES), (owners, rows, heads, LANES)
+    )
+    out_ref[:, rows] = jnp.broadcast_to(weight[None], (owners, rows, LANES)).astype(out_ref.dtype)
+    out_ref[:, rows + 1] = asked.astype(out_ref.dtype)
 
 
 def requests(page_ids, query, weight, owners, pages_dev):
-    length = query.shape[0] + 2 * weight.shape[0]
+    rows, heads = weight.shape
     return pl.pallas_call(
         functools.partial(request_kernel, pages_dev),
         out_shape=(
-            pltpu.HBM((owners, length, LANES), query.dtype),
+            pltpu.HBM((owners, rows + 2, heads, LANES), query.dtype),
             jax.ShapeDtypeStruct((owners, 1, LANES), jnp.int32),
         ),
         name="requests",
     )(page_ids, query, weight)
 
 
-def pack_kernel(table_ref, cache_ref, out_ref):
+PIECES = 8
+
+
+def pack_kernel(table_ref, cache_hbm, out_ref, cache_ref, sems):
     step = pl.program_id(0)
     rows = out_ref.shape[0]
     left = lax.broadcasted_iota(jnp.int32, (DK, LANES), 1) < PAGE
+
+    @pl.when(step == 0)
+    def _():
+        width = cache_ref.shape[1] // PIECES
+        copies = [
+            pltpu.make_async_copy(
+                cache_hbm.at[:, pl.ds(i * width, width)],
+                cache_ref.at[:, pl.ds(i * width, width)],
+                sems.at[i],
+            )
+            for i in range(PIECES)
+        ]
+        for copy in copies:
+            copy.start()
+        for copy in copies:
+            copy.wait()
 
     def tile(page):
         return cache_ref[:, pl.ds(pl.multiple_of(page // 2 * LANES, LANES), LANES)]
@@ -101,29 +118,70 @@
         grid=(peers // rows,),
         in_specs=[
             pl.BlockSpec(memory_space=pltpu.SMEM),
-            pl.BlockSpec(cache.shape, lambda i: (0, 0)),
+            pl.BlockSpec(memory_space=pltpu.HBM),
         ],
         out_specs=pl.BlockSpec((rows, DK, LANES), lambda i: (i, 0, 0)),
         out_shape=pltpu.HBM((peers, DK, LANES), cache.dtype),
-        compiler_params=pltpu.CompilerParams(vmem_limit_bytes=24 * MIB),
+        scratch_shapes=[
+            pltpu.VMEM(cache.shape, cache.dtype),
+            pltpu.SemaphoreType.DMA((PIECES,)),
+        ],
+        compiler_params=pltpu.CompilerParams(vmem_limit_bytes=60 * MIB),
         cost_estimate=pl.CostEstimate(flops=0, bytes_accessed=7 * MIB, transcendentals=0),
         name="pack_pages",
     )(table, cache)
 
 
-def score_kernel(query_ref, key_ref, out_ref, sum_ref):
-    sources = query_ref.shape[0]
-    rows = out_ref.shape[0]
-    heads = (query_ref.shape[1] - 2 * rows) // rows
-    flat = rows * heads
+def partner_kernel(me_ref, got_ref, *out_refs):
+    peers = got_ref.shape[0]
+    rows = len(out_refs)
+    weights = got_ref[:, rows].astype(jnp.float32)
+    place = lax.broadcasted_iota(jnp.int32, weights.shape, 1)
+    for d, out_ref in enumerate(out_refs):
+        row = me_ref[0] ^ d
+        out_ref[:peers] = got_ref[:, row]
+        weight = jnp.sum(jnp.where(place == row, weights, 0.0), axis=1)
+        out_ref[peers:] = weight.reshape(peers // 8, 8, LANES).astype(out_ref.dtype)
+
+
+def partner_parts(me, got, rows):
+    peers, _, heads, _ = got.shape
+    part = jax.ShapeDtypeStruct((peers + peers // 8, heads, LANES), got.dtype)
+    return pl.pallas_call(
+        partner_kernel,
+        in_specs=[
+            pl.BlockSpec(memory_space=pltpu.SMEM),
+            pl.BlockSpec(memory_space=pltpu.VMEM),
+        ],
+        out_shape=(part,) * rows,
+        compiler_params=pltpu.CompilerParams(vmem_limit_bytes=16 * MIB),
+        cost_estimate=pl.CostEstimate(flops=0, bytes_accessed=2 * MIB, transcendentals=0),
+        name="partner_parts",
+    )(me, got)
+
+
+def score_kernel(key_ref, *refs):
+    part_refs, (out_ref, sum_ref) = refs[:-2], refs[-2:]
+    step = pl.program_id(0)
+    sources = out_ref.shape[0]
+    peers = part_refs[0].shape[0] // 9 * 8
     blocks = key_ref.shape[0] // LANES
-    queries = jnp.concatenate([query_ref[i, :flat, :] for i in range(sources)], axis=0)
+    heads = part_refs[0].shape[1]
+    flat = heads * len(part_refs)
+    queries = jnp.concatenate(
+        [ref[step * sources + i] for i in range(sources) for ref in part_refs], axis=0
+    )
+    corner = lax.broadcasted_iota(jnp.int32, (heads, LANES), 0) == lax.broadcasted_iota(
+        jnp.int32, (heads, LANES), 1
+    )
+    tails = [ref[peers + step // 2].astype(jnp.float32) for ref in part_refs]
+    half = step % 2 == 0
     weights = []
     for i in range(sources):
-        tail = query_ref[i, flat:, :].astype(jnp.float32)[:rows]
-        weights.append(
-            [jnp.broadcast_to(tail[:, h : h + 1], (rows, LANES)) for h in range(heads)]
-        )
+        for tail in tails:
+            row = jnp.where(half, tail[i : i + 1], tail[sources + i : sources + i + 1])
+            column = jnp.sum(jnp.where(corner, row, 0.0), axis=1, keepdims=True)
+            weights.append(jnp.broadcast_to(column, (heads, LANES)))
     for b in range(blocks // 2):
         keys = key_ref[2 * b * LANES : 2 * (b + 1) * LANES, :]
         dots = lax.dot_general(
@@ -132,41 +190,37 @@
         for j in range(2):
             for i in range(sources):
                 total = None
-                for h in range(heads):
-                    at = i * flat + h * rows
+                for d in range(len(part_refs)):
+                    at = i * flat + d * heads
                     part = (
-                        jnp.maximum(dots[at : at + rows, j * LANES : (j + 1) * LANES], 0.0)
-                        * weights[i][h]
+                        jnp.maximum(dots[at : at + heads, j * LANES : (j + 1) * LANES], 0.0)
+                        * weights[i * len(part_refs) + d]
                     )
                     total = part if total is None else total + part
-                sum_ref[i, pl.ds(2 * b + j, rows, stride=blocks), :] = total
+                sum_ref[i, 2 * b + j : 2 * b + j + 1, :] = jnp.sum(total, axis=0, keepdims=True)
     for i in range(sources):
-        for r in range(rows):
-            out_ref[r, i] = sum_ref[i, r * blocks : (r + 1) * blocks, :]
-
-
-def index_scores(queries, keys, rows):
+        out_ref[i] = sum_ref[i].astype(out_ref.dtype)
+
+
+def index_scores(keys, parts):
     sources = 4
-    peers, length = queries.shape[:2]
+    peers = parts[0].shape[0] // 9 * 8
     blocks = keys.shape[0] // LANES
     return pl.pallas_call(
         score_kernel,
         grid=(peers // sources,),
-        in_specs=[
-            pl.BlockSpec((sources, length, LANES), lambda i: (i, 0, 0)),
-            pl.BlockSpec(keys.shape, lambda i: (0, 0)),
-        ],
-        out_specs=pl.BlockSpec((rows, sources, blocks, LANES), lambda i: (0, i, 0, 0)),
-        out_shape=jax.ShapeDtypeStruct((rows, peers, blocks, LANES), jnp.float32),
-        scratch_shapes=[pltpu.VMEM((sources, rows * blocks, LANES), jnp.float32)],
+        in_specs=[pl.BlockSpec(memory_space=pltpu.VMEM)] * (1 + len(parts)),
+        out_specs=pl.BlockSpec((sources, blocks, LANES), lambda i: (i, 0, 0)),
+        out_shape=jax.ShapeDtypeStruct((peers, blocks, LANES), jnp.bfloat16),
+        scratch_shapes=[pltpu.VMEM((sources, blocks, LANES), jnp.float32)],
         compiler_params=pltpu.CompilerParams(vmem_limit_bytes=16 * MIB),
         cost_estimate=pl.CostEstimate(
-            flops=2 * peers * length * keys.shape[0] * D_IDX,
+            flops=2 * peers * H_IDX * keys.shape[0] * D_IDX,
             bytes_accessed=2 * MIB,
             transcendentals=0,
         ),
         name="index_scores",
-    )(queries, keys)
+    )(keys, *parts)
 
 
 def logp_kernel(score_ref, out_ref):
@@ -259,24 +313,31 @@
 
 def per_device(idx_query, idx_weight, idx_keys, q_latent, latent_cache, page_ids):
     owners = lax.axis_size("ctx")
+    groups = lax.axis_size("qry")
     rows, heads = idx_weight.shape
     exchange = functools.partial(
         lax.all_to_all, axis_name="ctx", split_axis=0, concat_axis=0, tiled=True
     )
 
-    query = idx_query.reshape(rows, heads, D_IDX).transpose(1, 0, 2).reshape(-1, D_IDX)
+    query = idx_query.reshape(rows, heads, D_IDX)
     sent, table = requests(page_ids, query, idx_weight, owners, idx_keys.shape[0] // PAGE)
     got = exchange(sent)
-    asked = got[:, rows * heads + rows, :2].astype(jnp.int32)
+    asked = got[:, rows + 1, 0, :2].astype(jnp.int32)
     pages = exchange(pack_pages(asked, latent_cache.T))
 
-    scores = index_scores(got, idx_keys, rows)
-    scores = lax.psum_scatter(scores, "qry", scatter_dimension=0)
-    scores, pages = lax.optimization_barrier((scores, pages))
-    scores = exchange(scores.astype(jnp.bfloat16))
+    me = lax.axis_index("qry").astype(jnp.int32).reshape(1)
+    parts = partner_parts(me, got, rows)
+    parts = [parts[0]] + [
+        lax.ppermute(parts[d], "qry", [(i, i ^ d) for i in range(groups)])
+        for d in range(1, groups)
+    ]
+    scores = index_scores(idx_keys, parts)
+    latent = q_latent.reshape(H, DK)
+    scores, pages, latent = lax.optimization_barrier((scores, pages, latent))
+    scores = exchange(scores)
     index_logp = log_distribution(scores.reshape(-1, LANES)).reshape(1, -1)
 
-    latent_out = attend(table, q_latent.reshape(H, DK), pages).reshape(1, -1)
+    latent_out = attend(table, latent, pages).reshape(1, -1)
     return (index_logp, latent_out)
 
 

time: 125 us -> 112 us (0.90)
  starting transfers between devices: 13 us -> 27.6 us
  waiting for transfers between devices: 50.5 us -> 36.1 us
  between operations: 14.1 us -> 0.74 us
  Pallas kernels: 20.1 us -> 21.9 us
    reduce_scatter x1 -> x0, waiting for transfers between devices: 41.1 us -> none  [per_device(): scores = lax.psum_scatter(scores, 'qry', scatter_dimension=0)]
    all_to_all x1, waiting for transfers between devices: 9.34 us -> 26 us  [per_device(): pages = exchange(pack_pages(asked, latent_cache.T))]
    ppermute x0 -> x7, starting transfers between devices: none -> 14.6 us  [per_device(): lax.ppermute(parts[d], 'qry', [(i, i ^ d) for i in range(groups)])]
    ppermute x0 -> x7, waiting for transfers between devices: none -> 9.02 us  [per_device(): lax.ppermute(parts[d], 'qry', [(i, i ^ d) for i in range(groups)])]
    pallas_call x1, Pallas kernels: 6.26 us -> 8.17 us  [pack_pages(): pl.pallas_call(pack_kernel, grid=(peers // rows,), in_specs=[pl.BlockSpec...]
    unnamed x9 -> x8, local copies, waits for them, and re-layouts: 2.58 us -> 2.25 us
  transfers between devices with their start and end apart: 3 -> 9, of which waited for: 2 -> 4; matrix products, arithmetic and copies ran while one was open for 2% -> 2% of each run, Pallas kernels for 9% -> 10%
where the time goes in v4:
time: 112 us
  waiting for transfers between devices  36.1 us (32%)
  starting transfers between devices  27.6 us (25%)
  Pallas kernels  21.9 us (20%)
  blocking collectives  21.5 us (19%)
  local copies, waits for them, and re-layouts  2.4 us (2%)
  other arithmetic  1.51 us (1%)
    all_to_all x1, waiting for transfers between devices, per_device(): pages = exchange(pack_pages(asked, latent_cache.T))  26 us
    all_to_all x1, blocking collectives, per_device(): got = exchange(sent)  21.5 us
    ppermute x7, starting transfers between devices, per_device(): lax.ppermute(parts[d], 'qry', [(i, i ^ d) for i in range(groups)])  14.6 us
    ppermute x7, waiting for transfers between devices, per_device(): lax.ppermute(parts[d], 'qry', [(i, i ^ d) for i in range(groups)])  9.02 us
    pallas_call x1, Pallas kernels, pack_pages(): pl.pallas_call(pack_kernel, grid=(peers // rows,), in_specs=[pl.BlockSpec...  8.17 us
    all_to_all x1, starting transfers between devices, per_device(): scores = exchange(scores)  7.83 us
    pallas_call x1, Pallas kernels, attend(): pl.pallas_call(attend_kernel, grid=(peers // sources,), in_specs=[pl.Bloc...  5.74 us
    all_to_all x1, starting transfers between devices, per_device(): pages = exchange(pack_pages(asked, latent_cache.T))  5.14 us
  transfers between devices with their start and end apart: 9, of which 4 were waited for; matrix products, arithmetic and copies ran while one was open for 2% of the time, Pallas kernels for 10%

profile of v4, /device:TPU:1, one launch (start us, length us, event | category | flops | bytes accessed | tf_op | source)
XLA Modules:
  0.0 111.7 jit_solution(4396269338175957135)
XLA Ops:
  0.6 1.3 %copy.18 = bf16[1,8,8,128]{3,2,1,0:T(8,128)(2,1)} copy(bf16[1,8,8,128]{3,1,2,0:T(8,128)(2,1)} %bitcast.19) | data formatting | bytes 32768
  2.0 1.8 %requests.1 = (bf16[32,10,8,128]{3,2,1,0:T(8,128)(2,1)}, s32[32,1,128]{2,1,0:T(1,128)}) custom-call(s32[1,32]{1,0:T(1,128)} %ids_ref.1, bf16[8,8,128]{2,1,0:T(8,128)(2,1)} %bitcast.18, bf16[8,8]{1,0:T(8,128)(2,1)} %weight_ref.1), custom_call_target="tpu_custom_call" | custom-call | tf_op jit(solution)/shard_map/requests/pallas_call | solution.py:54
  3.7 21.5 %all_to_all.15.got_ref = bf16[32,10,8,128]{3,2,1,0:T(8,128)(2,1)S(1)} all-to-all(bf16[32,10,8,128]{3,2,1,0:T(8,128)(2,1)} %get-tuple-element.15), channel_id=1, replica_groups=mesh['ctx'=32,'qry'=8] {'ctx'}, dimensions={0} | all-to-all | bytes 1310720 | tf_op jit(solution)/shard_map/all_to_all | solution.py:324
  25.2 0.6 slice_convert_fusion
  25.9 8.2 %pack_pages.1 = bf16[32,576,128]{2,1,0:T(8,128)(2,1)} custom-call(s32[32,2]{1,0:T(8,128)} %bitcast.17, bf16[576,2048]{1,0:T(8,128)(2,1)} %bitcast.14), custom_call_target="tpu_custom_call" | custom-call | bytes 7340032 | tf_op jit(solution)/shard_map/pack_pages/pallas_call | solution.py:116
  34.0 0.0 copy-start.2
  34.0 0.0 copy-start.1
  34.1 5.1 %all-to-all-start.1 = ((bf16[32,576,128]{2,1,0:T(8,128)(2,1)}), bf16[32,576,128]{2,1,0:T(8,128)(2,1)}, u32[]{:S(2)}, u32[]{:S(2)}) async-start(bf16[32,576,128]{2,1,0:T(8,128)(2,1)} %pack_pages.1), calls=%async_computation.1 | async-start | bytes 9437184 | tf_op jit(solution)/shard_map/all_to_all | solution.py:326
  39.2 0.0 copy-start
  39.2 0.4 partner_parts.1
  39.6 1.7 %collective-permute-start = (bf16[36,8,128]{2,1,0:T(8,128)(2,1)S(1)}, bf16[36,8,128]{2,1,0:T(8,128)(2,1)S(1)}, u32[]{:S(2)}, u32[]{:S(2)}) collective-permute-start(bf16[36,8,128]{2,1,0:T(8,128)(2,1)S(1)} %get-tuple-element.17), channel_id=1, source_target_pairs={{0,1},{1,0},{2,3},{3,2},{4,5},{5,4},{6,7},{7,6},{8,9},{9,8},{10,11... | collective-permute-start | bytes 221192 | tf_op jit(solution)/shard_map/ppermute | solution.py:331
  41.3 3.0 %collective-permute-start.1 = (bf16[36,8,128]{2,1,0:T(8,128)(2,1)S(1)}, bf16[36,8,128]{2,1,0:T(8,128)(2,1)S(1)}, u32[]{:S(2)}, u32[]{:S(2)}) collective-permute-start(bf16[36,8,128]{2,1,0:T(8,128)(2,1)S(1)} %get-tuple-element.18), channel_id=1, source_target_pairs={{0,2},{1,3},{2,0},{3,1},{4,6},{5,7},{6,4},{7,5},{8,10},{9,11},{10,... | collective-permute-start | bytes 221192 | tf_op jit(solution)/shard_map/ppermute | solution.py:331
  44.3 0.0 collective-permute-start.2
  44.3 5.8 %collective-permute-start.3 = (bf16[36,8,128]{2,1,0:T(8,128)(2,1)S(1)}, bf16[36,8,128]{2,1,0:T(8,128)(2,1)S(1)}, u32[]{:S(2)}, u32[]{:S(2)}) collective-permute-start(bf16[36,8,128]{2,1,0:T(8,128)(2,1)S(1)} %get-tuple-element.20), channel_id=1, source_target_pairs={{0,4},{1,5},{2,6},{3,7},{4,0},{5,1},{6,2},{7,3},{8,12},{9,13},{10,... | collective-permute-start | bytes 221192 | tf_op jit(solution)/shard_map/ppermute | solution.py:331
  50.1 0.0 collective-permute-start.4
  50.1 0.0 collective-permute-done.refs_1_
  50.2 4.0 %collective-permute-start.5 = (bf16[36,8,128]{2,1,0:T(8,128)(2,1)S(1)}, bf16[36,8,128]{2,1,0:T(8,128)(2,1)S(1)}, u32[]{:S(2)}, u32[]{:S(2)}) collective-permute-start(bf16[36,8,128]{2,1,0:T(8,128)(2,1)S(1)} %get-tuple-element.22), channel_id=1, source_target_pairs={{0,6},{1,7},{2,4},{3,5},{4,2},{5,3},{6,0},{7,1},{8,14},{9,15},{10,... | collective-permute-start | bytes 221192 | tf_op jit(solution)/shard_map/ppermute | solution.py:331
  54.2 0.0 collective-permute-done.1.refs_2_
  54.2 0.0 collective-permute-start.6
  54.2 0.0 copy-done.2
  54.2 0.9 reduce
  55.1 0.2 reshape.26.query_ref
  55.3 0.0 collective-permute-done.2.refs_3_
  55.3 0.0 collective-permute-done.3.refs_4_
  55.3 5.0 %collective-permute-done.4.refs_5_ = bf16[36,8,128]{2,1,0:T(8,128)(2,1)S(1)} collective-permute-done((bf16[36,8,128]{2,1,0:T(8,128)(2,1)S(1)}, bf16[36,8,128]{2,1,0:T(8,128)(2,1)S(1)}, u32[]{:S(2)}, u32[]{:S(2)}) %collective-permute-start.4) | collective-permute-done | bytes 73760 | tf_op jit(solution)/shard_map/ppermute | solution.py:331
  60.2 0.0 collective-permute-done.5.refs_6_
  60.2 4.0 %collective-permute-done.6.refs_7_ = bf16[36,8,128]{2,1,0:T(8,128)(2,1)S(1)} collective-permute-done((bf16[36,8,128]{2,1,0:T(8,128)(2,1)S(1)}, bf16[36,8,128]{2,1,0:T(8,128)(2,1)S(1)}, u32[]{:S(2)}, u32[]{:S(2)}) %collective-permute-start.6) | collective-permute-done | bytes 73760 | tf_op jit(solution)/shard_map/ppermute | solution.py:331
  64.3 0.0 copy-done.1
  64.3 4.7 %index_scores.1 = bf16[32,16,128]{2,1,0:T(8,128)(2,1)} custom-call(bf16[2048,128]{1,0:T(8,128)(2,1)S(1)} %copy-done.1, bf16[36,8,128]{2,1,0:T(8,128)(2,1)S(1)} %get-tuple-element.16.refs_0_, bf16[36,8,128]{2,1,0:T(8,128)(2,1)S(1)} %collective-permute-done.refs_1_, bf16[36,8,128]{2,1,0:T(8,128)(2,1)S(1)} %collective-permute-done.1.refs_2_, ...), custom_call_target="tpu_custom_call" | custom-call | flops 1073741824 | bytes 2097152 | tf_op jit(solution)/shard_map/index_scores/pallas_call | solution.py:209
  69.0 26.0 %all-to-all-done.1.page_ref = bf16[32,576,128]{2,1,0:T(8,128)(2,1)} async-done(((bf16[32,576,128]{2,1,0:T(8,128)(2,1)}), bf16[32,576,128]{2,1,0:T(8,128)(2,1)}, u32[]{:S(2)}, u32[]{:S(2)}) %all-to-all-start.1) | async-done | bytes 4718624 | tf_op jit(solution)/shard_map/all_to_all | solution.py:326
  95.0 7.8 %all-to-all-start.2 = ((bf16[32,16,128]{2,1,0:T(8,128)(2,1)}), bf16[32,16,128]{2,1,0:T(8,128)(2,1)S(1)}, u32[]{:S(2)}, u32[]{:S(2)}) async-start(bf16[32,16,128]{2,1,0:T(8,128)(2,1)} %index_scores.1), calls=%async_computation.2 | async-start | bytes 262144 | tf_op jit(solution)/shard_map/all_to_all | solution.py:337
  102.9 0.0 copy-done
  102.9 5.7 %attend.1 = bf16[128,512]{1,0:T(8,128)(2,1)S(1)} custom-call(s32[32,1,128]{2,1,0:T(1,128)S(1)} %copy-done, bf16[128,576]{1,0:T(8,128)(2,1)S(1)} %reshape.26.query_ref, bf16[32,576,128]{2,1,0:T(8,128)(2,1)} %all-to-all-done.1.page_ref), custom_call_target="tpu_custom_call" | custom-call | flops 1140850688 | bytes 5242880 | tf_op jit(solution)/shard_map/attend/pallas_call | solution.py:289
  108.6 0.9 copy.16
  109.6 1.1 all-to-all-done.2
  110.6 1.1 log_distribution.1
Async XLA Ops:
  34.0 20.2 %copy-start.2 = (bf16[1,73728]{1,0:T(2,128)(2,1)S(1)}, bf16[1,73728]{1,0:T(2,128)(2,1)}, u32[]{:S(2)}) copy-start(bf16[1,73728]{1,0:T(2,128)(2,1)} %param.9) | copy-start | bytes 442372
  34.0 30.2 %copy-start.1 = (bf16[2048,128]{1,0:T(8,128)(2,1)S(1)}, bf16[2048,128]{1,0:T(8,128)(2,1)}, u32[]{:S(2)}) copy-start(bf16[2048,128]{1,0:T(8,128)(2,1)} %key_ref.1) | copy-start | bytes 1572868
  34.1 61.0 %all-to-all-start.1 = ((bf16[32,576,128]{2,1,0:T(8,128)(2,1)}), bf16[32,576,128]{2,1,0:T(8,128)(2,1)}, u32[]{:S(2)}, u32[]{:S(2)}) async-start(bf16[32,576,128]{2,1,0:T(8,128)(2,1)} %pack_pages.1), calls=%async_computation.1 | async-start | bytes 9437184 | tf_op jit(solution)/shard_map/all_to_all | solution.py:326
  39.2 63.7 %copy-start = (s32[32,1,128]{2,1,0:T(1,128)S(1)}, s32[32,1,128]{2,1,0:T(1,128)}, u32[]{:S(2)}) copy-start(s32[32,1,128]{2,1,0:T(1,128)} %get-tuple-element.25.used_ref) | copy-start | bytes 49156
  39.6 10.6 %collective-permute-start = (bf16[36,8,128]{2,1,0:T(8,128)(2,1)S(1)}, bf16[36,8,128]{2,1,0:T(8,128)(2,1)S(1)}, u32[]{:S(2)}, u32[]{:S(2)}) collective-permute-start(bf16[36,8,128]{2,1,0:T(8,128)(2,1)S(1)} %get-tuple-element.17), channel_id=1, source_target_pairs={{0,1},{1,0},{2,3},{3,2},{4,5},{5,4},{6,7},{7,6},{8,9},{9,8},{10,11... | collective-permute-start | bytes 221192 | tf_op jit(solution)/shard_map/ppermute | solution.py:331
  41.3 12.9 %collective-permute-start.1 = (bf16[36,8,128]{2,1,0:T(8,128)(2,1)S(1)}, bf16[36,8,128]{2,1,0:T(8,128)(2,1)S(1)}, u32[]{:S(2)}, u32[]{:S(2)}) collective-permute-start(bf16[36,8,128]{2,1,0:T(8,128)(2,1)S(1)} %get-tuple-element.18), channel_id=1, source_target_pairs={{0,2},{1,3},{2,0},{3,1},{4,6},{5,7},{6,4},{7,5},{8,10},{9,11},{10,... | collective-permute-start | bytes 221192 | tf_op jit(solution)/shard_map/ppermute | solution.py:331
  44.3 10.9 %collective-permute-start.2 = (bf16[36,8,128]{2,1,0:T(8,128)(2,1)S(1)}, bf16[36,8,128]{2,1,0:T(8,128)(2,1)S(1)}, u32[]{:S(2)}, u32[]{:S(2)}) collective-permute-start(bf16[36,8,128]{2,1,0:T(8,128)(2,1)S(1)} %get-tuple-element.19), channel_id=1, source_target_pairs={{0,3},{1,2},{2,1},{3,0},{4,7},{5,6},{6,5},{7,4},{8,11},{9,10},{10,... | collective-permute-start | bytes 221192 | tf_op jit(solution)/shard_map/ppermute | solution.py:331
  44.3 11.0 %collective-permute-start.3 = (bf16[36,8,128]{2,1,0:T(8,128)(2,1)S(1)}, bf16[36,8,128]{2,1,0:T(8,128)(2,1)S(1)}, u32[]{:S(2)}, u32[]{:S(2)}) collective-permute-start(bf16[36,8,128]{2,1,0:T(8,128)(2,1)S(1)} %get-tuple-element.20), channel_id=1, source_target_pairs={{0,4},{1,5},{2,6},{3,7},{4,0},{5,1},{6,2},{7,3},{8,12},{9,13},{10,... | collective-permute-start | bytes 221192 | tf_op jit(solution)/shard_map/ppermute | solution.py:331
  50.1 10.1 %collective-permute-start.4 = (bf16[36,8,128]{2,1,0:T(8,128)(2,1)S(1)}, bf16[36,8,128]{2,1,0:T(8,128)(2,1)S(1)}, u32[]{:S(2)}, u32[]{:S(2)}) collective-permute-start(bf16[36,8,128]{2,1,0:T(8,128)(2,1)S(1)} %get-tuple-element.21), channel_id=1, source_target_pairs={{0,5},{1,4},{2,7},{3,6},{4,1},{5,0},{6,3},{7,2},{8,13},{9,12},{10,... | collective-permute-start | bytes 221192 | tf_op jit(solution)/shard_map/ppermute | solution.py:331
  50.2 10.1 %collective-permute-start.5 = (bf16[36,8,128]{2,1,0:T(8,128)(2,1)S(1)}, bf16[36,8,128]{2,1,0:T(8,128)(2,1)S(1)}, u32[]{:S(2)}, u32[]{:S(2)}) collective-permute-start(bf16[36,8,128]{2,1,0:T(8,128)(2,1)S(1)} %get-tuple-element.22), channel_id=1, source_target_pairs={{0,6},{1,7},{2,4},{3,5},{4,2},{5,3},{6,0},{7,1},{8,14},{9,15},{10,... | collective-permute-start | bytes 221192 | tf_op jit(solution)/shard_map/ppermute | solution.py:331
  54.2 10.1 %collective-permute-start.6 = (bf16[36,8,128]{2,1,0:T(8,128)(2,1)S(1)}, bf16[36,8,128]{2,1,0:T(8,128)(2,1)S(1)}, u32[]{:S(2)}, u32[]{:S(2)}) collective-permute-start(bf16[36,8,128]{2,1,0:T(8,128)(2,1)S(1)} %get-tuple-element.23), channel_id=1, source_target_pairs={{0,7},{1,6},{2,5},{3,4},{4,3},{5,2},{6,1},{7,0},{8,15},{9,14},{10,... | collective-permute-start | bytes 221192 | tf_op jit(solution)/shard_map/ppermute | solution.py:331
  95.0 15.6 %all-to-all-start.2 = ((bf16[32,16,128]{2,1,0:T(8,128)(2,1)}), bf16[32,16,128]{2,1,0:T(8,128)(2,1)S(1)}, u32[]{:S(2)}, u32[]{:S(2)}) async-start(bf16[32,16,128]{2,1,0:T(8,128)(2,1)} %index_scores.1), calls=%async_computation.2 | async-start | bytes 262144 | tf_op jit(solution)/shard_map/all_to_all | solution.py:337

commit v5 on v4

--- a/solution.py
+++ b/solution.py
@@ -18,12 +18,14 @@
 TOPP = 32
 LANES = 128
 NEG = -1e30
+FIRST = 320
 MIB = 1 << 20
 
 
-def request_kernel(pages_dev, ids_ref, query_ref, weight_ref, out_ref, table_ref):
+def request_kernel(pages_dev, ids_ref, query_ref, weight_ref, out_ref, table_ref, turn_ref):
     owners = out_ref.shape[0]
     rows, heads = weight_ref.shape
+    part = rows // 2
     ids = ids_ref[...]
     owner, local = ids // pages_dev, ids % pages_dev
     mine = owner == lax.broadcasted_iota(jnp.int32, (owners, TOPP), 0)
@@ -42,11 +44,15 @@
         [weight_ref[...].astype(jnp.float32), jnp.zeros((rows, LANES - heads), jnp.float32)], axis=1
     )
     asked = jnp.broadcast_to(table.astype(jnp.float32), (owners, rows, LANES))
-    out_ref[:, :rows] = jnp.broadcast_to(
-        query_ref[...].reshape(1, rows, heads, LANES), (owners, rows, heads, LANES)
-    )
-    out_ref[:, rows] = jnp.broadcast_to(weight[None], (owners, rows, LANES)).astype(out_ref.dtype)
-    out_ref[:, rows + 1] = asked.astype(out_ref.dtype)
+    for h in range(heads):
+        turn_ref[pl.ds(h, rows, stride=heads), :] = query_ref[
+            :, h * LANES : (h + 1) * LANES
+        ].astype(jnp.float32)
+    query = turn_ref[...].astype(out_ref.dtype).reshape(rows, heads, LANES)
+    for t in range(owners):
+        out_ref[t, :part] = query[t % 2 * part : (t % 2 + 1) * part]
+    out_ref[:, part] = jnp.broadcast_to(weight[None], (owners, rows, LANES)).astype(out_ref.dtype)
+    out_ref[:, part + 1] = asked.astype(out_ref.dtype)
 
 
 def requests(page_ids, query, weight, owners, pages_dev):
@@ -54,36 +60,27 @@
     return pl.pallas_call(
         functools.partial(request_kernel, pages_dev),
         out_shape=(
-            pltpu.HBM((owners, rows + 2, heads, LANES), query.dtype),
+            pltpu.HBM((owners, rows // 2 + 2, heads, LANES), query.dtype),
             jax.ShapeDtypeStruct((owners, 1, LANES), jnp.int32),
         ),
+        scratch_shapes=[pltpu.VMEM((rows * heads, LANES), jnp.float32)],
         name="requests",
     )(page_ids, query, weight)
 
 
-PIECES = 8
-
-
-def pack_kernel(table_ref, cache_hbm, out_ref, cache_ref, sems):
-    step = pl.program_id(0)
-    rows = out_ref.shape[0]
-    left = lax.broadcasted_iota(jnp.int32, (DK, LANES), 1) < PAGE
-
-    @pl.when(step == 0)
-    def _():
-        width = cache_ref.shape[1] // PIECES
-        copies = [
-            pltpu.make_async_copy(
-                cache_hbm.at[:, pl.ds(i * width, width)],
-                cache_ref.at[:, pl.ds(i * width, width)],
-                sems.at[i],
-            )
-            for i in range(PIECES)
-        ]
-        for copy in copies:
-            copy.start()
-        for copy in copies:
-            copy.wait()
+GROUP = 4
+
+
+def pack_kernel(first_row, table_ref, cache_hbm, *refs):
+    score_refs, (out_hbm, cache_ref, stage_ref, in_sem, out_sems) = refs[:-5], refs[-5:]
+    peers = stage_ref.shape[0]
+    depth = cache_ref.shape[0]
+    load = pltpu.make_async_copy(cache_hbm.at[pl.ds(first_row, depth)], cache_ref, in_sem)
+    load.start()
+    for score_ref in score_refs:
+        stage_ref[:, depth:, :] = score_ref[...]
+    left = lax.broadcasted_iota(jnp.int32, (depth, LANES), 1) < PAGE
+    load.wait()
 
     def tile(page):
         return cache_ref[:, pl.ds(pl.multiple_of(page // 2 * LANES, LANES), LANES)]
@@ -91,60 +88,79 @@
     def turned(x):
         return jnp.concatenate([x[:, PAGE:], x[:, :PAGE]], axis=1)
 
-    for r in range(rows):
-        first = table_ref[step * rows + r, 0]
-        second = table_ref[step * rows + r, 1]
+    def send(g):
+        rows = pl.ds(g * GROUP, GROUP)
+        return pltpu.make_async_copy(stage_ref.at[rows], out_hbm.at[rows], out_sems.at[g])
+
+    for r in range(peers):
+        first = table_ref[r, 0]
+        second = table_ref[r, 1]
         first = jnp.where(first > 0, first - 1, 0)
         second = jnp.where(second > 0, second - 1, 1)
         straight = (first % 2 == 0) & (second % 2 == 1)
 
         @pl.when(straight)
         def _(r=r, first=first, second=second):
-            out_ref[r] = jnp.where(left, tile(first), tile(second))
+            stage_ref[r, :depth] = jnp.where(left, tile(first), tile(second))
 
         @pl.when(jnp.logical_not(straight))
         def _(r=r, first=first, second=second):
             a, b = tile(first), tile(second)
             a = jnp.where(first % 2 == 0, a, turned(a))
             b = jnp.where(second % 2 == 1, b, turned(b))
-            out_ref[r] = jnp.where(left, a, b)
-
-
-def pack_pages(table, cache):
+            stage_ref[r, :depth] = jnp.where(left, a, b)
+
+        if r % GROUP == GROUP - 1:
+            send(r // GROUP).start()
+    for g in range(peers // GROUP):
+        send(g).wait()
+
+
+def pack_pages(table, cache, first_row, depth, *scores):
     peers = table.shape[0]
-    rows = 4
-    return pl.pallas_call(
-        pack_kernel,
-        grid=(peers // rows,),
+    length = depth + sum(s.shape[1] for s in scores)
+    return pl.pallas_call(
+        functools.partial(pack_kernel, first_row),
         in_specs=[
             pl.BlockSpec(memory_space=pltpu.SMEM),
             pl.BlockSpec(memory_space=pltpu.HBM),
-        ],
-        out_specs=pl.BlockSpec((rows, DK, LANES), lambda i: (i, 0, 0)),
-        out_shape=pltpu.HBM((peers, DK, LANES), cache.dtype),
+        ]
+        + [pl.BlockSpec(memory_space=pltpu.VMEM)] * len(scores),
+        out_specs=pl.BlockSpec(memory_space=pltpu.HBM),
+        out_shape=pltpu.HBM((peers, length, LANES), cache.dtype),
         scratch_shapes=[
-            pltpu.VMEM(cache.shape, cache.dtype),
-            pltpu.SemaphoreType.DMA((PIECES,)),
+            pltpu.VMEM((depth, cache.shape[1]), cache.dtype),
+            pltpu.VMEM((peers, length, LANES), cache.dtype),
+            pltpu.SemaphoreType.DMA,
+            pltpu.SemaphoreType.DMA((peers // GROUP,)),
         ],
         compiler_params=pltpu.CompilerParams(vmem_limit_bytes=60 * MIB),
-        cost_estimate=pl.CostEstimate(flops=0, bytes_accessed=7 * MIB, transcendentals=0),
+        cost_estimate=pl.CostEstimate(flops=0, bytes_accessed=8 * MIB, transcendentals=0),
         name="pack_pages",
-    )(table, cache)
-
-
-def partner_kernel(me_ref, got_ref, *out_refs):
-    peers = got_ref.shape[0]
-    rows = len(out_refs)
-    weights = got_ref[:, rows].astype(jnp.float32)
+    )(table, cache, *scores)
+
+
+def partner_kernel(place_ref, got_ref, other_ref, *out_refs):
+    peers, part = got_ref.shape[0], got_ref.shape[1] - 2
+    weights = got_ref[:, part].astype(jnp.float32)
     place = lax.broadcasted_iota(jnp.int32, weights.shape, 1)
     for d, out_ref in enumerate(out_refs):
-        row = me_ref[0] ^ d
-        out_ref[:peers] = got_ref[:, row]
+        row = place_ref[0] ^ d
+        mine = row // part == place_ref[1]
+
+        @pl.when(mine)
+        def _(out_ref=out_ref, row=row):
+            out_ref[:peers] = got_ref[:, row % part]
+
+        @pl.when(jnp.logical_not(mine))
+        def _(out_ref=out_ref, row=row):
+            out_ref[:peers] = other_ref[:, row % part]
+
         weight = jnp.sum(jnp.where(place == row, weights, 0.0), axis=1)
         out_ref[peers:] = weight.reshape(peers // 8, 8, LANES).astype(out_ref.dtype)
 
 
-def partner_parts(me, got, rows):
+def partner_parts(place, got, other, rows):
     peers, _, heads, _ = got.shape
     part = jax.ShapeDtypeStruct((peers + peers // 8, heads, LANES), got.dtype)
     return pl.pallas_call(
@@ -152,12 +168,13 @@
         in_specs=[
             pl.BlockSpec(memory_space=pltpu.SMEM),
             pl.BlockSpec(memory_space=pltpu.VMEM),
+            pl.BlockSpec(memory_space=pltpu.VMEM),
         ],
         out_shape=(part,) * rows,
         compiler_params=pltpu.CompilerParams(vmem_limit_bytes=16 * MIB),
         cost_estimate=pl.CostEstimate(flops=0, bytes_accessed=2 * MIB, transcendentals=0),
         name="partner_parts",
-    )(me, got)
+    )(place, got, other)
 
 
 def score_kernel(key_ref, *refs):
@@ -223,26 +240,9 @@
     )(keys, *parts)
 
 
-def logp_kernel(score_ref, out_ref):
-    scores = score_ref[...].astype(jnp.float32)
-    top = jnp.max(scores)
-    total = jnp.sum(jnp.exp(scores - top), keepdims=True)
-    out_ref[...] = scores - (top + jnp.log(total)) + jnp.log(jnp.float32(scores.size))
-
-
-def log_distribution(scores):
-    return pl.pallas_call(
-        logp_kernel,
-        out_shape=jax.ShapeDtypeStruct(scores.shape, jnp.float32),
-        compiler_params=pltpu.CompilerParams(vmem_limit_bytes=8 * MIB),
-        cost_estimate=pl.CostEstimate(
-            flops=4 * scores.size, bytes_accessed=6 * scores.size, transcendentals=scores.size
-        ),
-        name="log_distribution",
-    )(scores)
-
-
-def attend_kernel(used_ref, query_ref, page_ref, out_ref, top_ref, total_ref, sum_ref):
+def attend_kernel(
+    used_ref, query_ref, page_ref, rest_ref, score_ref, out_ref, logp_ref, top_ref, total_ref, sum_ref
+):
     step = pl.program_id(0)
     sources = page_ref.shape[0]
 
@@ -251,6 +251,10 @@
         top_ref[...] = jnp.full_like(top_ref, NEG)
         total_ref[...] = jnp.zeros_like(total_ref)
         sum_ref[...] = jnp.zeros_like(sum_ref)
+        scores = score_ref[...].astype(jnp.float32).reshape(logp_ref.shape)
+        top = jnp.max(scores)
+        total = jnp.sum(jnp.exp(scores - top), keepdims=True)
+        logp_ref[...] = scores - (top + jnp.log(total)) + jnp.log(jnp.float32(scores.size))
 
     left = lax.broadcasted_iota(jnp.int32, (1, LANES), 1) < PAGE
     live = []
@@ -260,7 +264,13 @@
         ]
         live.append(jnp.where(left, slots[0], slots[1]))
     live = jnp.concatenate(live, axis=1)
-    keys = jnp.concatenate([page_ref[i] for i in range(sources)], axis=1)
+    keys = jnp.concatenate(
+        [
+            jnp.concatenate([page_ref[i] for i in range(sources)], axis=1),
+            jnp.concatenate([rest_ref[i, : DK - FIRST] for i in range(sources)], axis=1),
+        ],
+        axis=0,
+    )
     scale = (QK_NOPE + D_ROPE) ** (-0.5)
     logits = jnp.dot(query_ref[...], keys, preferred_element_type=jnp.float32) * scale + live
     old = top_ref[...]
@@ -282,63 +292,74 @@
         out_ref[...] = (sum_ref[...] / total_ref[...][:, :1]).astype(out_ref.dtype)
 
 
-def attend(used, query, pages):
-    sources = 8
+def attend(used, query, pages, rest):
+    sources = 16
     peers = pages.shape[0]
+    depth = DK - FIRST
+    blocks = rest.shape[1] - depth
     tokens = peers * LANES
     return pl.pallas_call(
         attend_kernel,
         grid=(peers // sources,),
         in_specs=[
             pl.BlockSpec(memory_space=pltpu.SMEM),
-            pl.BlockSpec((H, DK), lambda i: (0, 0)),
-            pl.BlockSpec((sources, DK, LANES), lambda i: (i, 0, 0)),
-        ],
-        out_specs=pl.BlockSpec((H, D_LAT), lambda i: (0, 0)),
+            pl.BlockSpec(memory_space=pltpu.VMEM),
+            pl.BlockSpec((sources, FIRST, LANES), lambda i: (i, 0, 0)),
+            pl.BlockSpec((sources, depth, LANES), lambda i: (i, 0, 0)),
+            pl.BlockSpec((peers, blocks, LANES), lambda i: (0, depth // blocks, 0)),
+        ],
+        out_specs=(
+            pl.BlockSpec((H, D_LAT), lambda i: (0, 0)),
+            pl.BlockSpec((peers * blocks, LANES), lambda i: (0, 0)),
+        ),
         scratch_shapes=[
             pltpu.VMEM((H, LANES), jnp.float32),
             pltpu.VMEM((H, LANES), jnp.float32),
             pltpu.VMEM((H, D_LAT), jnp.float32),
         ],
-        out_shape=jax.ShapeDtypeStruct((H, D_LAT), jnp.bfloat16),
-        compiler_params=pltpu.CompilerParams(vmem_limit_bytes=24 * MIB),
+        out_shape=(
+            jax.ShapeDtypeStruct((H, D_LAT), jnp.bfloat16),
+            jax.ShapeDtypeStruct((peers * blocks, LANES), jnp.float32),
+        ),
+        compiler_params=pltpu.CompilerParams(vmem_limit_bytes=40 * MIB),
         cost_estimate=pl.CostEstimate(
             flops=2 * H * tokens * (2 * D_LAT + D_ROPE),
             bytes_accessed=5 * MIB,
             transcendentals=H * tokens,
         ),
         name="attend",
-    )(used, query, pages)
+    )(used, query, pages, rest, rest)
 
 
 def per_device(idx_query, idx_weight, idx_keys, q_latent, latent_cache, page_ids):
     owners = lax.axis_size("ctx")
     groups = lax.axis_size("qry")
-    rows, heads = idx_weight.shape
+    rows = idx_weight.shape[0]
     exchange = functools.partial(
         lax.all_to_all, axis_name="ctx", split_axis=0, concat_axis=0, tiled=True
     )
 
-    query = idx_query.reshape(rows, heads, D_IDX)
-    sent, table = requests(page_ids, query, idx_weight, owners, idx_keys.shape[0] // PAGE)
+    def swap(x, axis, size, bits):
+        return lax.ppermute(x, axis, [(i, i ^ bits) for i in range(size)])
+
+    cache = latent_cache.T
+    sent, table = requests(page_ids, idx_query, idx_weight, owners, idx_keys.shape[0] // PAGE)
     got = exchange(sent)
-    asked = got[:, rows + 1, 0, :2].astype(jnp.int32)
-    pages = exchange(pack_pages(asked, latent_cache.T))
-
-    me = lax.axis_index("qry").astype(jnp.int32).reshape(1)
-    parts = partner_parts(me, got, rows)
-    parts = [parts[0]] + [
-        lax.ppermute(parts[d], "qry", [(i, i ^ d) for i in range(groups)])
-        for d in range(1, groups)
-    ]
+    asked = got[:, rows // 2 + 1, 0, :2].astype(jnp.int32)
+    packed, got = lax.optimization_barrier((pack_pages(asked, cache, 0, FIRST), got))
+    pages = exchange(packed)
+
+    place = jnp.stack([lax.axis_index("qry"), lax.axis_index("ctx") % 2]).astype(jnp.int32)
+    parts = partner_parts(place, got, swap(got, "ctx", owners, 1), rows)
+    parts = [parts[0]] + [swap(parts[d], "qry", groups, d) for d in range(1, groups)]
     scores = index_scores(idx_keys, parts)
+    rest = pack_pages(asked, cache, FIRST, DK - FIRST, scores)
     latent = q_latent.reshape(H, DK)
-    scores, pages, latent = lax.optimization_barrier((scores, pages, latent))
-    scores = exchange(scores)
-    index_logp = log_distribution(scores.reshape(-1, LANES)).reshape(1, -1)
-
-    latent_out = attend(table, latent, pages).reshape(1, -1)
-    return (index_logp, latent_out)
+    rest, pages, latent = lax.optimization_barrier((rest, pages, latent))
+    rest = exchange(rest)
+
+    latent_out, index_logp = attend(table, latent, pages, rest)
+    return (index_logp.reshape(1, -1), latent_out.reshape(1, -1))
 
 
 def solution(mesh):

time: 112 us -> 115 us (1.027)
  blocking collectives: 21.5 us -> 56.5 us
  waiting for transfers between devices: 36.1 us -> 8.56 us
  starting transfers between devices: 27.6 us -> 19 us
  other arithmetic: 1.51 us -> 3.12 us
  local copies, waits for them, and re-layouts: 2.4 us -> 3.67 us
    all_to_all x0 -> x1, blocking collectives: none -> 37.8 us  [per_device(): rest = exchange(rest)]
    all_to_all x2 -> x1, waiting for transfers between devices: 27.1 us -> 0.01 us  [per_device(): pages = exchange(packed)]
    all_to_all x2 -> x1, starting transfers between devices: 13 us -> 4.09 us  [per_device(): pages = exchange(packed)]
    all_to_all x1, blocking collectives: 21.5 us -> 18.8 us  [per_device(): got = exchange(sent)]
    unnamed x1, other arithmetic: 0.89 us -> 2.43 us
    pallas_call x1, Pallas kernels: 0.38 us -> 1.74 us  [partner_parts(): pl.pallas_call(partner_kernel, in_specs=[pl.BlockSpec(memory_space=pltpu....]
    ppermute x7 -> x8, waiting for transfers between devices: 9.02 us -> 8.55 us  [swap(): return lax.ppermute(x, axis, [(i, i ^ bits) for i in range(size)])]
    unnamed x8 -> x7, local copies, waits for them, and re-layouts: 2.25 us -> 2.6 us
  transfers between devices with their start and end apart: 9 -> 9, of which waited for: 4 -> 4; matrix products, arithmetic and copies ran while one was open for 2% -> 3% of each run, Pallas kernels for 10% -> 9%
where the time goes in v5:
time: 115 us; the launch traced here: 114 us
  blocking collectives  56.5 us (49%)
  Pallas kernels  22.3 us (19%)
  starting transfers between devices  19 us (17%)
  waiting for transfers between devices  8.56 us (7%)
  local copies, waits for them, and re-layouts  3.67 us (3%)
  other arithmetic  3.12 us (3%)
    all_to_all x1, blocking collectives, per_device(): rest = exchange(rest)  37.8 us
    all_to_all x1, blocking collectives, per_device(): got = exchange(sent)  18.8 us
    ppermute x8, starting transfers between devices, swap(): return lax.ppermute(x, axis, [(i, i ^ bits) for i in range(size)])  14.9 us
    pallas_call x2, Pallas kernels, pack_pages(): pl.pallas_call(functools.partial(pack_kernel, first_row), in_specs=[pl.Bl...  9.98 us
    ppermute x8, waiting for transfers between devices, swap(): return lax.ppermute(x, axis, [(i, i ^ bits) for i in range(size)])  8.55 us
    pallas_call x1, Pallas kernels, attend(): pl.pallas_call(attend_kernel, grid=(peers // sources,), in_specs=[pl.Bloc...  5.14 us
    all_to_all x1, starting transfers between devices, per_device(): pages = exchange(packed)  4.09 us
    pallas_call x1, Pallas kernels, index_scores(): pl.pallas_call(score_kernel, grid=(peers // sources,), in_specs=[pl.Block...  3.72 us
  transfers between devices with their start and end apart: 9, of which 4 were waited for; matrix products, arithmetic and copies ran while one was open for 3% of the time, Pallas kernels for 9%

profile of v5, /device:TPU:1, one launch (start us, length us, event | category | flops | bytes accessed | tf_op | source)
XLA Modules:
  0.0 113.9 jit_solution(9115890570126637972)
XLA Ops:
  0.6 1.7 %requests.1 = (bf16[32,6,8,128]{3,2,1,0:T(8,128)(2,1)}, s32[32,1,128]{2,1,0:T(1,128)}) custom-call(s32[1,32]{1,0:T(1,128)} %ids_ref.1, bf16[8,1024]{1,0:T(8,128)(2,1)} %query_ref.1, bf16[8,8]{1,0:T(8,128)(2,1)} %weight_ref.1), custom_call_target="tpu_custom_call" | custom-call | tf_op jit(solution)/shard_map/requests/pallas_call | solution.py:60
  2.3 18.8 %all_to_all.15.got_ref = bf16[32,6,8,128]{3,2,1,0:T(8,128)(2,1)S(1)} all-to-all(bf16[32,6,8,128]{3,2,1,0:T(8,128)(2,1)} %get-tuple-element.20), channel_id=1, replica_groups=mesh['ctx'=32,'qry'=8] {'ctx'}, dimensions={0} | all-to-all | bytes 786432 | tf_op jit(solution)/shard_map/all_to_all | solution.py:347
  21.1 0.6 slice_convert_fusion
  21.7 5.2 %pack_pages.2 = bf16[32,320,128]{2,1,0:T(8,128)(2,1)} custom-call(s32[32,2]{1,0:T(8,128)} %bitcast.12, bf16[576,2048]{1,0:T(8,128)(2,1)} %bitcast.9), custom_call_target="tpu_custom_call" | custom-call | bytes 8388608 | tf_op jit(solution)/shard_map/pack_pages/pallas_call | solution.py:122
  26.9 4.1 %all-to-all-start.1 = ((bf16[32,320,128]{2,1,0:T(8,128)(2,1)}), bf16[32,320,128]{2,1,0:T(8,128)(2,1)S(1)}, u32[]{:S(2)}, u32[]{:S(2)}) async-start(bf16[32,320,128]{2,1,0:T(8,128)(2,1)} %pack_pages.2), calls=%async_computation.1 | async-start | bytes 5242880 | tf_op jit(solution)/shard_map/all_to_all | solution.py:350
  31.0 0.4 collective-permute-start
  31.4 0.1 pad_add_fusion.place_ref
  31.5 1.3 %collective-permute-done.other_ref = bf16[32,6,8,128]{3,2,1,0:T(8,128)(2,1)S(1)} collective-permute-done((bf16[32,6,8,128]{3,2,1,0:T(8,128)(2,1)S(1)}, bf16[32,6,8,128]{3,2,1,0:T(8,128)(2,1)S(1)}, u32[]{:S(2)}, u32[]{:S(2)}) %collective-permute-start) | collective-permute-done | bytes 393248 | tf_op jit(solution)/shard_map/ppermute | solution.py:343
  32.8 1.7 %partner_parts.1 = (bf16[36,8,128]{2,1,0:T(8,128)(2,1)S(1)}, bf16[36,8,128]{2,1,0:T(8,128)(2,1)S(1)}, bf16[36,8,128]{2,1,0:T(8,128)(2,1)S(1)}, bf16[36,8,128]{2,...) custom-call(s32[2]{0:T(128)S(1)} %pad_add_fusion.place_ref, ...), custom_call_target="tpu_custom_call" | custom-call | bytes 2097152 | tf_op jit(solution)/shard_map/partner_parts/pallas_call | solution.py:166
  34.5 1.6 %collective-permute-start.1 = (bf16[36,8,128]{2,1,0:T(8,128)(2,1)S(1)}, bf16[36,8,128]{2,1,0:T(8,128)(2,1)S(1)}, u32[]{:S(2)}, u32[]{:S(2)}) collective-permute-start(bf16[36,8,128]{2,1,0:T(8,128)(2,1)S(1)} %get-tuple-element.23), channel_id=1, source_target_pairs={{0,1},{1,0},{2,3},{3,2},{4,5},{5,4},{6,7},{7,6},{8,9},{9,8},{10,11... | collective-permute-start | bytes 221192 | tf_op jit(solution)/shard_map/ppermute | solution.py:343
  36.2 3.0 %collective-permute-start.2 = (bf16[36,8,128]{2,1,0:T(8,128)(2,1)S(1)}, bf16[36,8,128]{2,1,0:T(8,128)(2,1)S(1)}, u32[]{:S(2)}, u32[]{:S(2)}) collective-permute-start(bf16[36,8,128]{2,1,0:T(8,128)(2,1)S(1)} %get-tuple-element.24), channel_id=1, source_target_pairs={{0,2},{1,3},{2,0},{3,1},{4,6},{5,7},{6,4},{7,5},{8,10},{9,11},{10,... | collective-permute-start | bytes 221192 | tf_op jit(solution)/shard_map/ppermute | solution.py:343
  39.1 0.0 collective-permute-start.3
  39.1 5.8 %collective-permute-start.4 = (bf16[36,8,128]{2,1,0:T(8,128)(2,1)}, bf16[36,8,128]{2,1,0:T(8,128)(2,1)S(1)}, u32[]{:S(2)}, u32[]{:S(2)}) collective-permute-start(bf16[36,8,128]{2,1,0:T(8,128)(2,1)} %get-tuple-element.26), channel_id=1, source_target_pairs={{0,4},{1,5},{2,6},{3,7},{4,0},{5,1},{6,2},{7,3},{8,12},{9,13},{10,... | collective-permute-start | bytes 221192 | tf_op jit(solution)/shard_map/ppermute | solution.py:343
  45.0 0.0 collective-permute-start.5
  45.0 0.0 collective-permute-done.1.refs_1_
  45.0 4.0 %collective-permute-start.6 = (bf16[36,8,128]{2,1,0:T(8,128)(2,1)}, bf16[36,8,128]{2,1,0:T(8,128)(2,1)S(1)}, u32[]{:S(2)}, u32[]{:S(2)}) collective-permute-start(bf16[36,8,128]{2,1,0:T(8,128)(2,1)} %get-tuple-element.28), channel_id=1, source_target_pairs={{0,6},{1,7},{2,4},{3,5},{4,2},{5,3},{6,0},{7,1},{8,14},{9,15},{10,... | collective-permute-start | bytes 221192 | tf_op jit(solution)/shard_map/ppermute | solution.py:343
  49.0 0.0 collective-permute-done.2.refs_2_
  49.0 0.0 collective-permute-start.7
  49.0 2.4 %reduce = bf16[73728]{0:T(1024)(128)(2,1)} reduce(bf16[1,73728]{1,0:T(2,128)(2,1)} %param.9, bf16[]{:T(256)} %constant.26), dimensions={0}, to_apply=%param.9.reduce_sub_computation | reduce | bytes 294914 | tf_op args[3]
  51.5 1.1 reshape.15.query_ref
  52.5 0.0 collective-permute-done.3.refs_3_
  52.5 0.0 collective-permute-done.4.refs_4_
  52.6 2.3 %collective-permute-done.5.refs_5_ = bf16[36,8,128]{2,1,0:T(8,128)(2,1)S(1)} collective-permute-done((bf16[36,8,128]{2,1,0:T(8,128)(2,1)}, bf16[36,8,128]{2,1,0:T(8,128)(2,1)S(1)}, u32[]{:S(2)}, u32[]{:S(2)}) %collective-permute-start.5) | collective-permute-done | bytes 73760 | tf_op jit(solution)/shard_map/ppermute | solution.py:343
  54.8 0.9 collective-permute-done.6.refs_6_
  55.7 4.1 %collective-permute-done.7.refs_7_ = bf16[36,8,128]{2,1,0:T(8,128)(2,1)S(1)} collective-permute-done((bf16[36,8,128]{2,1,0:T(8,128)(2,1)S(1)}, bf16[36,8,128]{2,1,0:T(8,128)(2,1)S(1)}, u32[]{:S(2)}, u32[]{:S(2)}) %collective-permute-start.7) | collective-permute-done | bytes 73760 | tf_op jit(solution)/shard_map/ppermute | solution.py:343
  59.8 0.0 copy-start.2
  59.8 1.0 copy-done.2
  60.8 3.7 %index_scores.1.refs_0_ = bf16[32,16,128]{2,1,0:T(8,128)(2,1)S(1)} custom-call(bf16[2048,128]{1,0:T(8,128)(2,1)S(1)} %copy-done.2, bf16[36,8,128]{2,1,0:T(8,128)(2,1)S(1)} %get-tuple-element.22.refs_0_, bf16[36,8,128]{2,1,0:T(8,128)(2,1)S(1)} %collective-permute-done.1.refs_1_, bf16[36,8,128]{2,1,0:T(8,128)(2,1)S(1)} %collective-permute-done.2.refs_2_, ...), custom_call_target="tpu_custom_call" | custom-call | flops 1073741824 | bytes 2097152 | tf_op jit(solution)/shard_map/index_scores/pallas_call | solution.py:226
  64.6 0.0 copy-start
  64.6 0.6 copy-done
  65.2 4.8 %pack_pages.3 = bf16[32,272,128]{2,1,0:T(8,128)(2,1)} custom-call(s32[32,2]{1,0:T(8,128)} %bitcast.13, bf16[576,2048]{1,0:T(8,128)(2,1)} %bitcast.10, bf16[32,16,128]{2,1,0:T(8,128)(2,1)} %copy-done), custom_call_target="tpu_custom_call" | custom-call | bytes 8388608 | tf_op jit(solution)/shard_map/pack_pages/pallas_call | solution.py:122
  70.0 0.0 copy-start.1
  70.1 0.0 all-to-all-done.1.page_ref
  70.1 37.8 %all_to_all.16.rest_ref.score_ref = bf16[32,272,128]{2,1,0:T(8,128)(2,1)S(1)} all-to-all(bf16[32,272,128]{2,1,0:T(8,128)(2,1)} %pack_pages.3), channel_id=1, replica_groups=mesh['ctx'=32,'qry'=8] {'ctx'}, dimensions={0} | all-to-all | bytes 4456448 | tf_op jit(solution)/shard_map/all_to_all | solution.py:359
  107.9 0.0 copy-done.1
  107.9 5.1 %attend.1 = (bf16[128,512]{1,0:T(8,128)(2,1)S(1)}, f32[512,128]{1,0:T(8,128)}) custom-call(s32[32,1,128]{2,1,0:T(1,128)S(1)} %copy-done.1, bf16[128,576]{1,0:T(8,128)(2,1)S(1)} %reshape.15.query_ref, bf16[32,320,128]{2,1,0:T(8,128)(2,1)S(1)} %all-to-all-done.1.page_ref, bf16[32,272,128]{2,1,0:T(8,128)(2,1)S(1)} %all_to_all.16.rest_ref.score_ref, ...), custom_call_target="tpu_custom_call" | custom-call | flops 1140850688 | bytes 5242880 | tf_op jit(solution)/shard_map/attend/pallas_call | solution.py:301
  113.0 0.9 copy.18
Async XLA Ops:
  26.9 43.2 %all-to-all-start.1 = ((bf16[32,320,128]{2,1,0:T(8,128)(2,1)}), bf16[32,320,128]{2,1,0:T(8,128)(2,1)S(1)}, u32[]{:S(2)}, u32[]{:S(2)}) async-start(bf16[32,320,128]{2,1,0:T(8,128)(2,1)} %pack_pages.2), calls=%async_computation.1 | async-start | bytes 5242880 | tf_op jit(solution)/shard_map/all_to_all | solution.py:350
  31.0 1.8 %collective-permute-start = (bf16[32,6,8,128]{3,2,1,0:T(8,128)(2,1)S(1)}, bf16[32,6,8,128]{3,2,1,0:T(8,128)(2,1)S(1)}, u32[]{:S(2)}, u32[]{:S(2)}) collective-permute-start(bf16[32,6,8,128]{3,2,1,0:T(8,128)(2,1)S(1)} %all_to_all.15.got_ref), channel_id=1, source_target_pairs={{0,8},{8,0},{16,24},{24,16},{32,40},{40,32},{48,56},{56,48},{64,72... | collective-permute-start | bytes 1179656 | tf_op jit(solution)/shard_map/ppermute | solution.py:343
  34.5 10.5 %collective-permute-start.1 = (bf16[36,8,128]{2,1,0:T(8,128)(2,1)S(1)}, bf16[36,8,128]{2,1,0:T(8,128)(2,1)S(1)}, u32[]{:S(2)}, u32[]{:S(2)}) collective-permute-start(bf16[36,8,128]{2,1,0:T(8,128)(2,1)S(1)} %get-tuple-element.23), channel_id=1, source_target_pairs={{0,1},{1,0},{2,3},{3,2},{4,5},{5,4},{6,7},{7,6},{8,9},{9,8},{10,11... | collective-permute-start | bytes 221192 | tf_op jit(solution)/shard_map/ppermute | solution.py:343
  36.2 12.9 %collective-permute-start.2 = (bf16[36,8,128]{2,1,0:T(8,128)(2,1)S(1)}, bf16[36,8,128]{2,1,0:T(8,128)(2,1)S(1)}, u32[]{:S(2)}, u32[]{:S(2)}) collective-permute-start(bf16[36,8,128]{2,1,0:T(8,128)(2,1)S(1)} %get-tuple-element.24), channel_id=1, source_target_pairs={{0,2},{1,3},{2,0},{3,1},{4,6},{5,7},{6,4},{7,5},{8,10},{9,11},{10,... | collective-permute-start | bytes 221192 | tf_op jit(solution)/shard_map/ppermute | solution.py:343
  39.1 13.4 %collective-permute-start.3 = (bf16[36,8,128]{2,1,0:T(8,128)(2,1)}, bf16[36,8,128]{2,1,0:T(8,128)(2,1)S(1)}, u32[]{:S(2)}, u32[]{:S(2)}) collective-permute-start(bf16[36,8,128]{2,1,0:T(8,128)(2,1)} %get-tuple-element.25), channel_id=1, source_target_pairs={{0,3},{1,2},{2,1},{3,0},{4,7},{5,6},{6,5},{7,4},{8,11},{9,10},{10,... | collective-permute-start | bytes 221192 | tf_op jit(solution)/shard_map/ppermute | solution.py:343
  39.1 13.4 %collective-permute-start.4 = (bf16[36,8,128]{2,1,0:T(8,128)(2,1)}, bf16[36,8,128]{2,1,0:T(8,128)(2,1)S(1)}, u32[]{:S(2)}, u32[]{:S(2)}) collective-permute-start(bf16[36,8,128]{2,1,0:T(8,128)(2,1)} %get-tuple-element.26), channel_id=1, source_target_pairs={{0,4},{1,5},{2,6},{3,7},{4,0},{5,1},{6,2},{7,3},{8,12},{9,13},{10,... | collective-permute-start | bytes 221192 | tf_op jit(solution)/shard_map/ppermute | solution.py:343
  45.0 9.9 %collective-permute-start.5 = (bf16[36,8,128]{2,1,0:T(8,128)(2,1)}, bf16[36,8,128]{2,1,0:T(8,128)(2,1)S(1)}, u32[]{:S(2)}, u32[]{:S(2)}) collective-permute-start(bf16[36,8,128]{2,1,0:T(8,128)(2,1)} %get-tuple-element.27), channel_id=1, source_target_pairs={{0,5},{1,4},{2,7},{3,6},{4,1},{5,0},{6,3},{7,2},{8,13},{9,12},{10,... | collective-permute-start | bytes 221192 | tf_op jit(solution)/shard_map/ppermute | solution.py:343
  45.0 10.7 %collective-permute-start.6 = (bf16[36,8,128]{2,1,0:T(8,128)(2,1)}, bf16[36,8,128]{2,1,0:T(8,128)(2,1)S(1)}, u32[]{:S(2)}, u32[]{:S(2)}) collective-permute-start(bf16[36,8,128]{2,1,0:T(8,128)(2,1)} %get-tuple-element.28), channel_id=1, source_target_pairs={{0,6},{1,7},{2,4},{3,5},{4,2},{5,3},{6,0},{7,1},{8,14},{9,15},{10,... | collective-permute-start | bytes 221192 | tf_op jit(solution)/shard_map/ppermute | solution.py:343
  49.0 10.8 %collective-permute-start.7 = (bf16[36,8,128]{2,1,0:T(8,128)(2,1)S(1)}, bf16[36,8,128]{2,1,0:T(8,128)(2,1)S(1)}, u32[]{:S(2)}, u32[]{:S(2)}) collective-permute-start(bf16[36,8,128]{2,1,0:T(8,128)(2,1)S(1)} %get-tuple-element.29), channel_id=1, source_target_pairs={{0,7},{1,6},{2,5},{3,4},{4,3},{5,2},{6,1},{7,0},{8,15},{9,14},{10,... | collective-permute-start | bytes 221192 | tf_op jit(solution)/shard_map/ppermute | solution.py:343
  59.8 1.0 copy-start.2
  64.6 0.7 copy-start
  70.0 37.8 %copy-start.1 = (s32[32,1,128]{2,1,0:T(1,128)S(1)}, s32[32,1,128]{2,1,0:T(1,128)}, u32[]{:S(2)}) copy-start(s32[32,1,128]{2,1,0:T(1,128)} %get-tuple-element.19.used_ref) | copy-start | bytes 49156

commit v6 on v5

--- a/solution.py
+++ b/solution.py
@@ -18,7 +18,7 @@
 TOPP = 32
 LANES = 128
 NEG = -1e30
-FIRST = 320
+FIRST = 384
 MIB = 1 << 20
 
 
@@ -68,29 +68,45 @@
     )(page_ids, query, weight)
 
 
+def stage_kernel(cache_hbm, out_ref, sem):
+    load = pltpu.make_async_copy(cache_hbm, out_ref, sem)
+    load.start()
+    load.wait()
+
+
+def stage(cache):
+    return pl.pallas_call(
+        stage_kernel,
+        in_specs=[pl.BlockSpec(memory_space=pltpu.HBM)],
+        out_specs=pl.BlockSpec(memory_space=pltpu.VMEM),
+        out_shape=pltpu.VMEM(cache.shape, cache.dtype),
+        scratch_shapes=[pltpu.SemaphoreType.DMA],
+        compiler_params=pltpu.CompilerParams(vmem_limit_bytes=60 * MIB),
+        cost_estimate=pl.CostEstimate(flops=0, bytes_accessed=5 * MIB, transcendentals=0),
+        name="stage",
+    )(cache)
+
+
 GROUP = 4
 
 
-def pack_kernel(first_row, table_ref, cache_hbm, *refs):
-    score_refs, (out_hbm, cache_ref, stage_ref, in_sem, out_sems) = refs[:-5], refs[-5:]
+def pack_kernel(first_row, depth, table_ref, cache_ref, *refs):
+    score_refs, (out_hbm, stage_ref, out_sems) = refs[:-3], refs[-3:]
     peers = stage_ref.shape[0]
-    depth = cache_ref.shape[0]
-    load = pltpu.make_async_copy(cache_hbm.at[pl.ds(first_row, depth)], cache_ref, in_sem)
-    load.start()
+    rows = slice(first_row, first_row + depth)
     for score_ref in score_refs:
         stage_ref[:, depth:, :] = score_ref[...]
     left = lax.broadcasted_iota(jnp.int32, (depth, LANES), 1) < PAGE
-    load.wait()
 
     def tile(page):
-        return cache_ref[:, pl.ds(pl.multiple_of(page // 2 * LANES, LANES), LANES)]
+        return cache_ref[rows, pl.ds(pl.multiple_of(page // 2 * LANES, LANES), LANES)]
 
     def turned(x):
         return jnp.concatenate([x[:, PAGE:], x[:, :PAGE]], axis=1)
 
     def send(g):
-        rows = pl.ds(g * GROUP, GROUP)
-        return pltpu.make_async_copy(stage_ref.at[rows], out_hbm.at[rows], out_sems.at[g])
+        peer = pl.ds(g * GROUP, GROUP)
+        return pltpu.make_async_copy(stage_ref.at[peer], out_hbm.at[peer], out_sems.at[g])
 
     for r in range(peers):
         first = table_ref[r, 0]
@@ -120,21 +136,19 @@
     peers = table.shape[0]
     length = depth + sum(s.shape[1] for s in scores)
     return pl.pallas_call(
-        functools.partial(pack_kernel, first_row),
+        functools.partial(pack_kernel, first_row, depth),
         in_specs=[
             pl.BlockSpec(memory_space=pltpu.SMEM),
-            pl.BlockSpec(memory_space=pltpu.HBM),
+            pl.BlockSpec(memory_space=pltpu.VMEM),
         ]
         + [pl.BlockSpec(memory_space=pltpu.VMEM)] * len(scores),
         out_specs=pl.BlockSpec(memory_space=pltpu.HBM),
         out_shape=pltpu.HBM((peers, length, LANES), cache.dtype),
         scratch_shapes=[
-            pltpu.VMEM((depth, cache.shape[1]), cache.dtype),
             pltpu.VMEM((peers, length, LANES), cache.dtype),
-            pltpu.SemaphoreType.DMA,
             pltpu.SemaphoreType.DMA((peers // GROUP,)),
         ],
-        compiler_params=pltpu.CompilerParams(vmem_limit_bytes=60 * MIB),
+        compiler_params=pltpu.CompilerParams(vmem_limit_bytes=24 * MIB),
         cost_estimate=pl.CostEstimate(flops=0, bytes_accessed=8 * MIB, transcendentals=0),
         name="pack_pages",
     )(table, cache, *scores)
@@ -342,9 +356,10 @@
     def swap(x, axis, size, bits):
         return lax.ppermute(x, axis, [(i, i ^ bits) for i in range(size)])
 
-    cache = latent_cache.T
     sent, table = requests(page_ids, idx_query, idx_weight, owners, idx_keys.shape[0] // PAGE)
-    got = exchange(sent)
+    got, latent, cache = lax.optimization_barrier(
+        (exchange(sent), q_latent.reshape(H, DK), stage(latent_cache.T))
+    )
     asked = got[:, rows // 2 + 1, 0, :2].astype(jnp.int32)
     packed, got = lax.optimization_barrier((pack_pages(asked, cache, 0, FIRST), got))
     pages = exchange(packed)
@@ -354,8 +369,7 @@
     parts = [parts[0]] + [swap(parts[d], "qry", groups, d) for d in range(1, groups)]
     scores = index_scores(idx_keys, parts)
     rest = pack_pages(asked, cache, FIRST, DK - FIRST, scores)
-    latent = q_latent.reshape(H, DK)
-    rest, pages, latent = lax.optimization_barrier((rest, pages, latent))
+    rest, pages = lax.optimization_barrier((rest, pages))
     rest = exchange(rest)
 
     latent_out, index_logp = attend(table, latent, pages, rest)

time: 115 us -> 107 us (0.930)
  blocking collectives: 56.5 us -> 30.7 us
  waiting for transfers between devices: 8.56 us -> 21.6 us
  starting transfers between devices: 19 us -> 28.5 us
  local copies, waits for them, and re-layouts: 3.67 us -> 2.1 us
  other arithmetic: 3.12 us -> 1.87 us
  Pallas kernels: 22.3 us -> 21.1 us
    all_to_all x1 -> x0, blocking collectives: 18.8 us -> none  [per_device(): got = exchange(sent)]
    all_to_all x0 -> x1, starting transfers between devices: none -> 8.59 us  [per_device(): exchange(sent)]
    all_to_all x1, blocking collectives: 37.8 us -> 30.7 us  [per_device(): rest = exchange(rest)]
    all_to_all x0 -> x1, waiting for transfers between devices: none -> 6.55 us  [per_device(): exchange(sent)]
    all_to_all x1, waiting for transfers between devices: 0.01 us -> 3.53 us  [per_device(): pages = exchange(packed)]
    ppermute x8, waiting for transfers between devices: 8.55 us -> 11.6 us  [swap(): return lax.ppermute(x, axis, [(i, i ^ bits) for i in range(size)])]
    pallas_call x2 -> x3, Pallas kernels: 9.98 us -> 8.92 us  [the longest x2 7.24 us: pack_pages(): pl.pallas_call(functools.partial(pack_kernel, first_row, depth), in_specs...]
    unnamed x7 -> x5, local copies, waits for them, and re-layouts: 2.6 us -> 1.95 us
  transfers between devices with their start and end apart: 9 -> 10, of which waited for: 4 -> 5; matrix products, arithmetic and copies ran while one was open for 3% -> 2% of each run, Pallas kernels for 9% -> 9%
where the time goes in v6:
time: 107 us
  blocking collectives  30.7 us (29%)
  starting transfers between devices  28.5 us (27%)
  waiting for transfers between devices  21.6 us (20%)
  Pallas kernels  21.1 us (20%)
  local copies, waits for them, and re-layouts  2.1 us (2%)
  other arithmetic  1.87 us (2%)
    all_to_all x1, blocking collectives, per_device(): rest = exchange(rest)  30.7 us
    ppermute x8, starting transfers between devices, swap(): return lax.ppermute(x, axis, [(i, i ^ bits) for i in range(size)])  15.1 us
    ppermute x8, waiting for transfers between devices, swap(): return lax.ppermute(x, axis, [(i, i ^ bits) for i in range(size)])  11.6 us
    all_to_all x1, starting transfers between devices, per_device(): exchange(sent)  8.59 us
    pallas_call x2, Pallas kernels, pack_pages(): pl.pallas_call(functools.partial(pack_kernel, first_row, depth), in_specs...  7.24 us
    all_to_all x1, waiting for transfers between devices, per_device(): exchange(sent)  6.55 us
    pallas_call x1, Pallas kernels, attend(): pl.pallas_call(attend_kernel, grid=(peers // sources,), in_specs=[pl.Bloc...  5.68 us
    all_to_all x1, starting transfers between devices, per_device(): pages = exchange(packed)  4.78 us
  transfers between devices with their start and end apart: 10, of which 5 were waited for; matrix products, arithmetic and copies ran while one was open for 2% of the time, Pallas kernels for 9%

profile of v6, /device:TPU:1, one launch (start us, length us, event | category | flops | bytes accessed | tf_op | source)
XLA Modules:
  0.0 106.6 jit_solution(6975812802622866121)
XLA Ops:
  0.6 1.7 %requests.1 = (bf16[32,6,8,128]{3,2,1,0:T(8,128)(2,1)}, s32[32,1,128]{2,1,0:T(1,128)}) custom-call(s32[1,32]{1,0:T(1,128)} %ids_ref.1, bf16[8,1024]{1,0:T(8,128)(2,1)} %query_ref.1, bf16[8,8]{1,0:T(8,128)(2,1)} %weight_ref.1), custom_call_target="tpu_custom_call" | custom-call | tf_op jit(solution)/shard_map/requests/pallas_call | solution.py:60
  2.3 8.6 %all-to-all-start = ((bf16[32,6,8,128]{3,2,1,0:T(8,128)(2,1)}), bf16[32,6,8,128]{3,2,1,0:T(8,128)(2,1)S(1)}, u32[]{:S(2)}, u32[]{:S(2)}) async-start(bf16[32,6,8,128]{3,2,1,0:T(8,128)(2,1)} %get-tuple-element.22), calls=%async_computation | async-start | bytes 786432 | tf_op jit(solution)/shard_map/all_to_all | solution.py:361
  10.9 1.8 %reduce = bf16[73728]{0:T(1024)(128)(2,1)S(1)} reduce(bf16[1,73728]{1,0:T(2,128)(2,1)} %param.9, bf16[]{:T(256)} %constant.26), dimensions={0}, to_apply=%param.9.reduce_sub_computation | reduce | bytes 294914 | tf_op args[3]
  12.7 0.2 reshape.15.query_ref
  12.8 1.7 %stage.1.cache_ref = bf16[576,2048]{1,0:T(8,128)(2,1)S(1)} custom-call(bf16[576,2048]{1,0:T(8,128)(2,1)} %bitcast.11), custom_call_target="tpu_custom_call" | custom-call | bytes 5242880 | tf_op jit(solution)/shard_map/stage/pallas_call | solution.py:78
  14.5 6.5 %all-to-all-done.got_ref = bf16[32,6,8,128]{3,2,1,0:T(8,128)(2,1)S(1)} async-done(((bf16[32,6,8,128]{3,2,1,0:T(8,128)(2,1)}), bf16[32,6,8,128]{3,2,1,0:T(8,128)(2,1)S(1)}, u32[]{:S(2)}, u32[]{:S(2)}) %all-to-all-start) | async-done | bytes 393248 | tf_op jit(solution)/shard_map/all_to_all | solution.py:361
  21.1 4.1 %pack_pages.2 = bf16[32,384,128]{2,1,0:T(8,128)(2,1)} custom-call(s32[32,2]{1,0:T(8,128)S(1)} %bitcast.8, bf16[576,2048]{1,0:T(8,128)(2,1)S(1)} %stage.1.cache_ref), custom_call_target="tpu_custom_call" | custom-call | bytes 8388608 | tf_op jit(solution)/shard_map/pack_pages/pallas_call | solution.py:138
  25.2 4.8 %all-to-all-start.1 = ((bf16[32,384,128]{2,1,0:T(8,128)(2,1)}), bf16[32,384,128]{2,1,0:T(8,128)(2,1)}, u32[]{:S(2)}, u32[]{:S(2)}) async-start(bf16[32,384,128]{2,1,0:T(8,128)(2,1)} %pack_pages.2), calls=%async_computation.1 | async-start | bytes 6291456 | tf_op jit(solution)/shard_map/all_to_all | solution.py:365
  30.0 0.5 collective-permute-start
  30.5 0.1 pad_add_fusion.place_ref
  30.5 1.3 %collective-permute-done.other_ref = bf16[32,6,8,128]{3,2,1,0:T(8,128)(2,1)S(1)} collective-permute-done((bf16[32,6,8,128]{3,2,1,0:T(8,128)(2,1)S(1)}, bf16[32,6,8,128]{3,2,1,0:T(8,128)(2,1)S(1)}, u32[]{:S(2)}, u32[]{:S(2)}) %collective-permute-start) | collective-permute-done | bytes 393248 | tf_op jit(solution)/shard_map/ppermute | solution.py:357
  31.8 1.1 %partner_parts.1 = (bf16[36,8,128]{2,1,0:T(8,128)(2,1)S(1)}, bf16[36,8,128]{2,1,0:T(8,128)(2,1)S(1)}, bf16[36,8,128]{2,1,0:T(8,128)(2,1)S(1)}, bf16[36,8,128]{2,...) custom-call(s32[2]{0:T(128)S(1)} %pad_add_fusion.place_ref, ...), custom_call_target="tpu_custom_call" | custom-call | bytes 2097152 | tf_op jit(solution)/shard_map/partner_parts/pallas_call | solution.py:180
  32.9 1.7 %collective-permute-start.1 = (bf16[36,8,128]{2,1,0:T(8,128)(2,1)S(1)}, bf16[36,8,128]{2,1,0:T(8,128)(2,1)S(1)}, u32[]{:S(2)}, u32[]{:S(2)}) collective-permute-start(bf16[36,8,128]{2,1,0:T(8,128)(2,1)S(1)} %get-tuple-element.28), channel_id=1, source_target_pairs={{0,1},{1,0},{2,3},{3,2},{4,5},{5,4},{6,7},{7,6},{8,9},{9,8},{10,11... | collective-permute-start | bytes 221192 | tf_op jit(solution)/shard_map/ppermute | solution.py:357
  34.6 3.0 %collective-permute-start.2 = (bf16[36,8,128]{2,1,0:T(8,128)(2,1)S(1)}, bf16[36,8,128]{2,1,0:T(8,128)(2,1)S(1)}, u32[]{:S(2)}, u32[]{:S(2)}) collective-permute-start(bf16[36,8,128]{2,1,0:T(8,128)(2,1)S(1)} %get-tuple-element.29), channel_id=1, source_target_pairs={{0,2},{1,3},{2,0},{3,1},{4,6},{5,7},{6,4},{7,5},{8,10},{9,11},{10,... | collective-permute-start | bytes 221192 | tf_op jit(solution)/shard_map/ppermute | solution.py:357
  37.6 0.0 collective-permute-start.3
  37.6 5.8 %collective-permute-start.4 = (bf16[36,8,128]{2,1,0:T(8,128)(2,1)S(1)}, bf16[36,8,128]{2,1,0:T(8,128)(2,1)S(1)}, u32[]{:S(2)}, u32[]{:S(2)}) collective-permute-start(bf16[36,8,128]{2,1,0:T(8,128)(2,1)S(1)} %get-tuple-element.31), channel_id=1, source_target_pairs={{0,4},{1,5},{2,6},{3,7},{4,0},{5,1},{6,2},{7,3},{8,12},{9,13},{10,... | collective-permute-start | bytes 221192 | tf_op jit(solution)/shard_map/ppermute | solution.py:357
  43.4 0.0 collective-permute-start.5
  43.4 0.0 collective-permute-done.1.refs_1_
  43.4 4.0 %collective-permute-start.6 = (bf16[36,8,128]{2,1,0:T(8,128)(2,1)S(1)}, bf16[36,8,128]{2,1,0:T(8,128)(2,1)S(1)}, u32[]{:S(2)}, u32[]{:S(2)}) collective-permute-start(bf16[36,8,128]{2,1,0:T(8,128)(2,1)S(1)} %get-tuple-element.33), channel_id=1, source_target_pairs={{0,6},{1,7},{2,4},{3,5},{4,2},{5,3},{6,0},{7,1},{8,14},{9,15},{10,... | collective-permute-start | bytes 221192 | tf_op jit(solution)/shard_map/ppermute | solution.py:357
  47.5 0.0 collective-permute-done.2.refs_2_
  47.5 0.0 collective-permute-start.7
  47.5 0.0 collective-permute-done.3.refs_3_
  47.5 0.0 collective-permute-done.4.refs_4_
  47.5 6.2 %collective-permute-done.5.refs_5_ = bf16[36,8,128]{2,1,0:T(8,128)(2,1)S(1)} collective-permute-done((bf16[36,8,128]{2,1,0:T(8,128)(2,1)S(1)}, bf16[36,8,128]{2,1,0:T(8,128)(2,1)S(1)}, u32[]{:S(2)}, u32[]{:S(2)}) %collective-permute-start.5) | collective-permute-done | bytes 73760 | tf_op jit(solution)/shard_map/ppermute | solution.py:357
  53.7 0.0 collective-permute-done.6.refs_6_
  53.7 4.1 %collective-permute-done.7.refs_7_ = bf16[36,8,128]{2,1,0:T(8,128)(2,1)S(1)} collective-permute-done((bf16[36,8,128]{2,1,0:T(8,128)(2,1)S(1)}, bf16[36,8,128]{2,1,0:T(8,128)(2,1)S(1)}, u32[]{:S(2)}, u32[]{:S(2)}) %collective-permute-start.7) | collective-permute-done | bytes 73760 | tf_op jit(solution)/shard_map/ppermute | solution.py:357
  57.8 0.0 copy-start.1
  57.8 1.0 copy-done.1
  58.8 3.7 %index_scores.1.refs_0_ = bf16[32,16,128]{2,1,0:T(8,128)(2,1)S(1)} custom-call(bf16[2048,128]{1,0:T(8,128)(2,1)S(1)} %copy-done.1, bf16[36,8,128]{2,1,0:T(8,128)(2,1)S(1)} %get-tuple-element.27.refs_0_, bf16[36,8,128]{2,1,0:T(8,128)(2,1)S(1)} %collective-permute-done.1.refs_1_, bf16[36,8,128]{2,1,0:T(8,128)(2,1)S(1)} %collective-permute-done.2.refs_2_, ...), custom_call_target="tpu_custom_call" | custom-call | flops 1073741824 | bytes 2097152 | tf_op jit(solution)/shard_map/index_scores/pallas_call | solution.py:240
  62.5 3.2 %pack_pages.3 = bf16[32,208,128]{2,1,0:T(8,128)(2,1)} custom-call(s32[32,2]{1,0:T(8,128)S(1)} %bitcast.9, bf16[576,2048]{1,0:T(8,128)(2,1)S(1)} %stage.1.cache_ref, bf16[32,16,128]{2,1,0:T(8,128)(2,1)S(1)} %index_scores.1.refs_0_), custom_call_target="tpu_custom_call" | custom-call | bytes 8388608 | tf_op jit(solution)/shard_map/pack_pages/pallas_call | solution.py:138
  65.7 0.0 copy-start
  65.7 3.5 %all-to-all-done.1.page_ref = bf16[32,384,128]{2,1,0:T(8,128)(2,1)} async-done(((bf16[32,384,128]{2,1,0:T(8,128)(2,1)}), bf16[32,384,128]{2,1,0:T(8,128)(2,1)}, u32[]{:S(2)}, u32[]{:S(2)}) %all-to-all-start.1) | async-done | bytes 3145760 | tf_op jit(solution)/shard_map/all_to_all | solution.py:365
  69.3 30.7 %all_to_all.15.rest_ref.score_ref = bf16[32,208,128]{2,1,0:T(8,128)(2,1)S(1)} all-to-all(bf16[32,208,128]{2,1,0:T(8,128)(2,1)} %pack_pages.3), channel_id=1, replica_groups=mesh['ctx'=32,'qry'=8] {'ctx'}, dimensions={0} | all-to-all | bytes 3407872 | tf_op jit(solution)/shard_map/all_to_all | solution.py:373
  100.0 0.0 copy-done
  100.0 5.7 %attend.1 = (bf16[128,512]{1,0:T(8,128)(2,1)S(1)}, f32[512,128]{1,0:T(8,128)}) custom-call(s32[32,1,128]{2,1,0:T(1,128)S(1)} %copy-done, bf16[128,576]{1,0:T(8,128)(2,1)S(1)} %reshape.15.query_ref, bf16[32,384,128]{2,1,0:T(8,128)(2,1)} %all-to-all-done.1.page_ref, bf16[32,208,128]{2,1,0:T(8,128)(2,1)S(1)} %all_to_all.15.rest_ref.score_ref, ...), custom_call_target="tpu_custom_call" | custom-call | flops 1140850688 | bytes 5242880 | tf_op jit(solution)/shard_map/attend/pallas_call | solution.py:315
  105.7 0.9 copy.18
  (1 shorter events, 0.0 us)
Async XLA Ops:
  2.3 18.8 %all-to-all-start = ((bf16[32,6,8,128]{3,2,1,0:T(8,128)(2,1)}), bf16[32,6,8,128]{3,2,1,0:T(8,128)(2,1)S(1)}, u32[]{:S(2)}, u32[]{:S(2)}) async-start(bf16[32,6,8,128]{3,2,1,0:T(8,128)(2,1)} %get-tuple-element.22), calls=%async_computation | async-start | bytes 786432 | tf_op jit(solution)/shard_map/all_to_all | solution.py:361
  25.2 44.1 %all-to-all-start.1 = ((bf16[32,384,128]{2,1,0:T(8,128)(2,1)}), bf16[32,384,128]{2,1,0:T(8,128)(2,1)}, u32[]{:S(2)}, u32[]{:S(2)}) async-start(bf16[32,384,128]{2,1,0:T(8,128)(2,1)} %pack_pages.2), calls=%async_computation.1 | async-start | bytes 6291456 | tf_op jit(solution)/shard_map/all_to_all | solution.py:365
  30.0 1.9 %collective-permute-start = (bf16[32,6,8,128]{3,2,1,0:T(8,128)(2,1)S(1)}, bf16[32,6,8,128]{3,2,1,0:T(8,128)(2,1)S(1)}, u32[]{:S(2)}, u32[]{:S(2)}) collective-permute-start(bf16[32,6,8,128]{3,2,1,0:T(8,128)(2,1)S(1)} %all-to-all-done.got_ref), channel_id=1, source_target_pairs={{0,8},{8,0},{16,24},{24,16},{32,40},{40,32},{48,56},{56,48},{64,72... | collective-permute-start | bytes 1179656 | tf_op jit(solution)/shard_map/ppermute | solution.py:357
  32.9 10.5 %collective-permute-start.1 = (bf16[36,8,128]{2,1,0:T(8,128)(2,1)S(1)}, bf16[36,8,128]{2,1,0:T(8,128)(2,1)S(1)}, u32[]{:S(2)}, u32[]{:S(2)}) collective-permute-start(bf16[36,8,128]{2,1,0:T(8,128)(2,1)S(1)} %get-tuple-element.28), channel_id=1, source_target_pairs={{0,1},{1,0},{2,3},{3,2},{4,5},{5,4},{6,7},{7,6},{8,9},{9,8},{10,11... | collective-permute-start | bytes 221192 | tf_op jit(solution)/shard_map/ppermute | solution.py:357
  34.6 12.9 %collective-permute-start.2 = (bf16[36,8,128]{2,1,0:T(8,128)(2,1)S(1)}, bf16[36,8,128]{2,1,0:T(8,128)(2,1)S(1)}, u32[]{:S(2)}, u32[]{:S(2)}) collective-permute-start(bf16[36,8,128]{2,1,0:T(8,128)(2,1)S(1)} %get-tuple-element.29), channel_id=1, source_target_pairs={{0,2},{1,3},{2,0},{3,1},{4,6},{5,7},{6,4},{7,5},{8,10},{9,11},{10,... | collective-permute-start | bytes 221192 | tf_op jit(solution)/shard_map/ppermute | solution.py:357
  37.6 9.9 %collective-permute-start.3 = (bf16[36,8,128]{2,1,0:T(8,128)(2,1)S(1)}, bf16[36,8,128]{2,1,0:T(8,128)(2,1)S(1)}, u32[]{:S(2)}, u32[]{:S(2)}) collective-permute-start(bf16[36,8,128]{2,1,0:T(8,128)(2,1)S(1)} %get-tuple-element.30), channel_id=1, source_target_pairs={{0,3},{1,2},{2,1},{3,0},{4,7},{5,6},{6,5},{7,4},{8,11},{9,10},{10,... | collective-permute-start | bytes 221192 | tf_op jit(solution)/shard_map/ppermute | solution.py:357
  37.6 9.9 %collective-permute-start.4 = (bf16[36,8,128]{2,1,0:T(8,128)(2,1)S(1)}, bf16[36,8,128]{2,1,0:T(8,128)(2,1)S(1)}, u32[]{:S(2)}, u32[]{:S(2)}) collective-permute-start(bf16[36,8,128]{2,1,0:T(8,128)(2,1)S(1)} %get-tuple-element.31), channel_id=1, source_target_pairs={{0,4},{1,5},{2,6},{3,7},{4,0},{5,1},{6,2},{7,3},{8,12},{9,13},{10,... | collective-permute-start | bytes 221192 | tf_op jit(solution)/shard_map/ppermute | solution.py:357
  43.4 10.2 %collective-permute-start.5 = (bf16[36,8,128]{2,1,0:T(8,128)(2,1)S(1)}, bf16[36,8,128]{2,1,0:T(8,128)(2,1)S(1)}, u32[]{:S(2)}, u32[]{:S(2)}) collective-permute-start(bf16[36,8,128]{2,1,0:T(8,128)(2,1)S(1)} %get-tuple-element.32), channel_id=1, source_target_pairs={{0,5},{1,4},{2,7},{3,6},{4,1},{5,0},{6,3},{7,2},{8,13},{9,12},{10,... | collective-permute-start | bytes 221192 | tf_op jit(solution)/shard_map/ppermute | solution.py:357
  43.4 10.2 %collective-permute-start.6 = (bf16[36,8,128]{2,1,0:T(8,128)(2,1)S(1)}, bf16[36,8,128]{2,1,0:T(8,128)(2,1)S(1)}, u32[]{:S(2)}, u32[]{:S(2)}) collective-permute-start(bf16[36,8,128]{2,1,0:T(8,128)(2,1)S(1)} %get-tuple-element.33), channel_id=1, source_target_pairs={{0,6},{1,7},{2,4},{3,5},{4,2},{5,3},{6,0},{7,1},{8,14},{9,15},{10,... | collective-permute-start | bytes 221192 | tf_op jit(solution)/shard_map/ppermute | solution.py:357
  47.5 10.3 %collective-permute-start.7 = (bf16[36,8,128]{2,1,0:T(8,128)(2,1)S(1)}, bf16[36,8,128]{2,1,0:T(8,128)(2,1)S(1)}, u32[]{:S(2)}, u32[]{:S(2)}) collective-permute-start(bf16[36,8,128]{2,1,0:T(8,128)(2,1)S(1)} %get-tuple-element.34), channel_id=1, source_target_pairs={{0,7},{1,6},{2,5},{3,4},{4,3},{5,2},{6,1},{7,0},{8,15},{9,14},{10,... | collective-permute-start | bytes 221192 | tf_op jit(solution)/shard_map/ppermute | solution.py:357
  57.8 1.0 copy-start.1
  65.7 34.3 %copy-start = (s32[32,1,128]{2,1,0:T(1,128)S(1)}, s32[32,1,128]{2,1,0:T(1,128)}, u32[]{:S(2)}) copy-start(s32[32,1,128]{2,1,0:T(1,128)} %get-tuple-element.21.used_ref) | copy-start | bytes 49156

commit v7 on v6

--- a/solution.py
+++ b/solution.py
@@ -18,7 +18,6 @@
 TOPP = 32
 LANES = 128
 NEG = -1e30
-FIRST = 384
 MIB = 1 << 20
 
 
@@ -43,7 +42,8 @@
     weight = jnp.concatenate(
         [weight_ref[...].astype(jnp.float32), jnp.zeros((rows, LANES - heads), jnp.float32)], axis=1
     )
-    asked = jnp.broadcast_to(table.astype(jnp.float32), (owners, rows, LANES))
+    asked = jnp.where(lane == heads, left, jnp.where(lane == heads + 1, right, 0))
+    asked = asked.astype(jnp.float32).reshape(owners, 1, LANES)
     for h in range(heads):
         turn_ref[pl.ds(h, rows, stride=heads), :] = query_ref[
             :, h * LANES : (h + 1) * LANES
@@ -51,8 +51,7 @@
     query = turn_ref[...].astype(out_ref.dtype).reshape(rows, heads, LANES)
     for t in range(owners):
         out_ref[t, :part] = query[t % 2 * part : (t % 2 + 1) * part]
-    out_ref[:, part] = jnp.broadcast_to(weight[None], (owners, rows, LANES)).astype(out_ref.dtype)
-    out_ref[:, part + 1] = asked.astype(out_ref.dtype)
+    out_ref[:, part] = (weight[None] + asked).astype(out_ref.dtype)
 
 
 def requests(page_ids, query, weight, owners, pages_dev):
@@ -60,7 +59,7 @@
     return pl.pallas_call(
         functools.partial(request_kernel, pages_dev),
         out_shape=(
-            pltpu.HBM((owners, rows // 2 + 2, heads, LANES), query.dtype),
+            pltpu.HBM((owners, rows // 2 + 1, heads, LANES), query.dtype),
             jax.ShapeDtypeStruct((owners, 1, LANES), jnp.int32),
         ),
         scratch_shapes=[pltpu.VMEM((rows * heads, LANES), jnp.float32)],
@@ -90,16 +89,12 @@
 GROUP = 4
 
 
-def pack_kernel(first_row, depth, table_ref, cache_ref, *refs):
-    score_refs, (out_hbm, stage_ref, out_sems) = refs[:-3], refs[-3:]
+def pack_kernel(table_ref, cache_ref, out_hbm, stage_ref, out_sems):
     peers = stage_ref.shape[0]
-    rows = slice(first_row, first_row + depth)
-    for score_ref in score_refs:
-        stage_ref[:, depth:, :] = score_ref[...]
-    left = lax.broadcasted_iota(jnp.int32, (depth, LANES), 1) < PAGE
+    left = lax.broadcasted_iota(jnp.int32, (DK, LANES), 1) < PAGE
 
     def tile(page):
-        return cache_ref[rows, pl.ds(pl.multiple_of(page // 2 * LANES, LANES), LANES)]
+        return cache_ref[:, pl.ds(pl.multiple_of(page // 2 * LANES, LANES), LANES)]
 
     def turned(x):
         return jnp.concatenate([x[:, PAGE:], x[:, :PAGE]], axis=1)
@@ -117,14 +112,14 @@
 
         @pl.when(straight)
         def _(r=r, first=first, second=second):
-            stage_ref[r, :depth] = jnp.where(left, tile(first), tile(second))
+            stage_ref[r] = jnp.where(left, tile(first), tile(second))
 
         @pl.when(jnp.logical_not(straight))
         def _(r=r, first=first, second=second):
             a, b = tile(first), tile(second)
             a = jnp.where(first % 2 == 0, a, turned(a))
             b = jnp.where(second % 2 == 1, b, turned(b))
-            stage_ref[r, :depth] = jnp.where(left, a, b)
+            stage_ref[r] = jnp.where(left, a, b)
 
         if r % GROUP == GROUP - 1:
             send(r // GROUP).start()
@@ -132,30 +127,28 @@
         send(g).wait()
 
 
-def pack_pages(table, cache, first_row, depth, *scores):
+def pack_pages(table, cache):
     peers = table.shape[0]
-    length = depth + sum(s.shape[1] for s in scores)
-    return pl.pallas_call(
-        functools.partial(pack_kernel, first_row, depth),
+    return pl.pallas_call(
+        pack_kernel,
         in_specs=[
             pl.BlockSpec(memory_space=pltpu.SMEM),
             pl.BlockSpec(memory_space=pltpu.VMEM),
-        ]
-        + [pl.BlockSpec(memory_space=pltpu.VMEM)] * len(scores),
+        ],
         out_specs=pl.BlockSpec(memory_space=pltpu.HBM),
-        out_shape=pltpu.HBM((peers, length, LANES), cache.dtype),
+        out_shape=pltpu.HBM((peers, DK, LANES), cache.dtype),
         scratch_shapes=[
-            pltpu.VMEM((peers, length, LANES), cache.dtype),
+            pltpu.VMEM((peers, DK, LANES), cache.dtype),
             pltpu.SemaphoreType.DMA((peers // GROUP,)),
         ],
         compiler_params=pltpu.CompilerParams(vmem_limit_bytes=24 * MIB),
         cost_estimate=pl.CostEstimate(flops=0, bytes_accessed=8 * MIB, transcendentals=0),
         name="pack_pages",
-    )(table, cache, *scores)
+    )(table, cache)
 
 
 def partner_kernel(place_ref, got_ref, other_ref, *out_refs):
-    peers, part = got_ref.shape[0], got_ref.shape[1] - 2
+    peers, part = got_ref.shape[0], got_ref.shape[1] - 1
     weights = got_ref[:, part].astype(jnp.float32)
     place = lax.broadcasted_iota(jnp.int32, weights.shape, 1)
     for d, out_ref in enumerate(out_refs):
@@ -254,9 +247,26 @@
     )(keys, *parts)
 
 
-def attend_kernel(
-    used_ref, query_ref, page_ref, rest_ref, score_ref, out_ref, logp_ref, top_ref, total_ref, sum_ref
-):
+def logp_kernel(score_ref, out_ref):
+    scores = score_ref[...].astype(jnp.float32)
+    top = jnp.max(scores)
+    total = jnp.sum(jnp.exp(scores - top), keepdims=True)
+    out_ref[...] = scores - (top + jnp.log(total)) + jnp.log(jnp.float32(scores.size))
+
+
+def log_distribution(scores):
+    return pl.pallas_call(
+        logp_kernel,
+        out_shape=jax.ShapeDtypeStruct(scores.shape, jnp.float32),
+        compiler_params=pltpu.CompilerParams(vmem_limit_bytes=8 * MIB),
+        cost_estimate=pl.CostEstimate(
+            flops=4 * scores.size, bytes_accessed=6 * scores.size, transcendentals=scores.size
+        ),
+        name="log_distribution",
+    )(scores)
+
+
+def attend_kernel(used_ref, query_ref, page_ref, out_ref, top_ref, total_ref, sum_ref):
     step = pl.program_id(0)
     sources = page_ref.shape[0]
 
@@ -265,10 +275,6 @@
         top_ref[...] = jnp.full_like(top_ref, NEG)
         total_ref[...] = jnp.zeros_like(total_ref)
         sum_ref[...] = jnp.zeros_like(sum_ref)
-        scores = score_ref[...].astype(jnp.float32).reshape(logp_ref.shape)
-        top = jnp.max(scores)
-        total = jnp.sum(jnp.exp(scores - top), keepdims=True)
-        logp_ref[...] = scores - (top + jnp.log(total)) + jnp.log(jnp.float32(scores.size))
 
     left = lax.broadcasted_iota(jnp.int32, (1, LANES), 1) < PAGE
     live = []
@@ -278,13 +284,7 @@
         ]
         live.append(jnp.where(left, slots[0], slots[1]))
     live = jnp.concatenate(live, axis=1)
-    keys = jnp.concatenate(
-        [
-            jnp.concatenate([page_ref[i] for i in range(sources)], axis=1),
-            jnp.concatenate([rest_ref[i, : DK - FIRST] for i in range(sources)], axis=1),
-        ],
-        axis=0,
-    )
+    keys = jnp.concatenate([page_ref[i] for i in range(sources)], axis=1)
     scale = (QK_NOPE + D_ROPE) ** (-0.5)
     logits = jnp.dot(query_ref[...], keys, preferred_element_type=jnp.float32) * scale + live
     old = top_ref[...]
@@ -306,11 +306,9 @@
         out_ref[...] = (sum_ref[...] / total_ref[...][:, :1]).astype(out_ref.dtype)
 
 
-def attend(used, query, pages, rest):
+def attend(used, query, pages):
     sources = 16
     peers = pages.shape[0]
-    depth = DK - FIRST
-    blocks = rest.shape[1] - depth
     tokens = peers * LANES
     return pl.pallas_call(
         attend_kernel,
@@ -318,23 +316,15 @@
         in_specs=[
             pl.BlockSpec(memory_space=pltpu.SMEM),
             pl.BlockSpec(memory_space=pltpu.VMEM),
-            pl.BlockSpec((sources, FIRST, LANES), lambda i: (i, 0, 0)),
-            pl.BlockSpec((sources, depth, LANES), lambda i: (i, 0, 0)),
-            pl.BlockSpec((peers, blocks, LANES), lambda i: (0, depth // blocks, 0)),
-        ],
-        out_specs=(
-            pl.BlockSpec((H, D_LAT), lambda i: (0, 0)),
-            pl.BlockSpec((peers * blocks, LANES), lambda i: (0, 0)),
-        ),
+            pl.BlockSpec((sources, DK, LANES), lambda i: (i, 0, 0)),
+        ],
+        out_specs=pl.BlockSpec((H, D_LAT), lambda i: (0, 0)),
         scratch_shapes=[
             pltpu.VMEM((H, LANES), jnp.float32),
             pltpu.VMEM((H, LANES), jnp.float32),
             pltpu.VMEM((H, D_LAT), jnp.float32),
         ],
-        out_shape=(
-            jax.ShapeDtypeStruct((H, D_LAT), jnp.bfloat16),
-            jax.ShapeDtypeStruct((peers * blocks, LANES), jnp.float32),
-        ),
+        out_shape=jax.ShapeDtypeStruct((H, D_LAT), jnp.bfloat16),
         compiler_params=pltpu.CompilerParams(vmem_limit_bytes=40 * MIB),
         cost_estimate=pl.CostEstimate(
             flops=2 * H * tokens * (2 * D_LAT + D_ROPE),
@@ -342,7 +332,7 @@
             transcendentals=H * tokens,
         ),
         name="attend",
-    )(used, query, pages, rest, rest)
+    )(used, query, pages)
 
 
 def per_device(idx_query, idx_weight, idx_keys, q_latent, latent_cache, page_ids):
@@ -360,19 +350,20 @@
     got, latent, cache = lax.optimization_barrier(
         (exchange(sent), q_latent.reshape(H, DK), stage(latent_cache.T))
     )
-    asked = got[:, rows // 2 + 1, 0, :2].astype(jnp.int32)
-    packed, got = lax.optimization_barrier((pack_pages(asked, cache, 0, FIRST), got))
+    heads = idx_weight.shape[1]
+    asked = got[:, rows // 2, 0, heads : heads + 2].astype(jnp.int32)
+    packed, got = lax.optimization_barrier((pack_pages(asked, cache), got))
     pages = exchange(packed)
 
     place = jnp.stack([lax.axis_index("qry"), lax.axis_index("ctx") % 2]).astype(jnp.int32)
     parts = partner_parts(place, got, swap(got, "ctx", owners, 1), rows)
     parts = [parts[0]] + [swap(parts[d], "qry", groups, d) for d in range(1, groups)]
     scores = index_scores(idx_keys, parts)
-    rest = pack_pages(asked, cache, FIRST, DK - FIRST, scores)
-    rest, pages = lax.optimization_barrier((rest, pages))
-    rest = exchange(rest)
-
-    latent_out, index_logp = attend(table, latent, pages, rest)
+    scores, pages = lax.optimization_barrier((scores, pages))
+    scores = exchange(scores)
+
+    latent_out = attend(table, latent, pages)
+    index_logp = log_distribution(scores.reshape(-1, LANES))
     return (index_logp.reshape(1, -1), latent_out.reshape(1, -1))
 
 

time: 107 us -> 103 us (0.963)
  blocking collectives: 30.7 us -> 0 us
  waiting for transfers between devices: 21.6 us -> 43.4 us
  starting transfers between devices: 28.5 us -> 36.6 us
    all_to_all x1 -> x0, blocking collectives: 30.7 us -> none  [per_device(): rest = exchange(rest)]
    all_to_all x1, waiting for transfers between devices: 3.53 us -> 23.2 us  [per_device(): pages = exchange(packed)]
    all_to_all x0 -> x1, starting transfers between devices: none -> 7.83 us  [per_device(): scores = exchange(scores)]
    all_to_all x0 -> x1, waiting for transfers between devices: none -> 1.94 us  [per_device(): scores = exchange(scores)]
    pallas_call x2, Pallas kernels: 7.24 us -> 6.05 us  [the longest x1 4.95 us: pack_pages(): pl.pallas_call(pack_kernel, in_specs=[pl.BlockSpec(memory_space=pltpu.SME...]
  transfers between devices with their start and end apart: 10 -> 11, of which waited for: 5 -> 6; matrix products, arithmetic and copies ran while one was open for 2% -> 2% of each run, Pallas kernels for 9% -> 12%
where the time goes in v7:
time: 103 us
  waiting for transfers between devices  43.4 us (42%)
  starting transfers between devices  36.6 us (36%)
  Pallas kernels  20.1 us (20%)
  local copies, waits for them, and re-layouts  1.07 us (1%)
  other arithmetic  1.03 us (1%)
    all_to_all x1, waiting for transfers between devices, per_device(): pages = exchange(packed)  23.2 us
    ppermute x8, starting transfers between devices, swap(): return lax.ppermute(x, axis, [(i, i ^ bits) for i in range(size)])  15.3 us
    ppermute x8, waiting for transfers between devices, swap(): return lax.ppermute(x, axis, [(i, i ^ bits) for i in range(size)])  11.5 us
    all_to_all x1, starting transfers between devices, per_device(): exchange(sent)  8.59 us
    all_to_all x1, starting transfers between devices, per_device(): scores = exchange(scores)  7.83 us
    all_to_all x1, waiting for transfers between devices, per_device(): exchange(sent)  6.81 us
    pallas_call x1, Pallas kernels, pack_pages(): pl.pallas_call(pack_kernel, in_specs=[pl.BlockSpec(memory_space=pltpu.SME...  4.95 us
    all_to_all x1, starting transfers between devices, per_device(): pages = exchange(packed)  4.9 us
  transfers between devices with their start and end apart: 11, of which 6 were waited for; matrix products, arithmetic and copies ran while one was open for 2% of the time, Pallas kernels for 12%

profile of v7, /device:TPU:1, one launch (start us, length us, event | category | flops | bytes accessed | tf_op | source)
XLA Modules:
  0.0 103.0 jit_solution(16027285567646039061)
XLA Ops:
  0.6 0.0 copy-start.2
  0.6 1.7 %requests.1 = (bf16[32,5,8,128]{3,2,1,0:T(8,128)(2,1)}, s32[32,1,128]{2,1,0:T(1,128)}) custom-call(s32[1,32]{1,0:T(1,128)} %ids_ref.1, bf16[8,1024]{1,0:T(8,128)(2,1)} %query_ref.1, bf16[8,8]{1,0:T(8,128)(2,1)} %weight_ref.1), custom_call_target="tpu_custom_call" | custom-call | tf_op jit(solution)/shard_map/requests/pallas_call | solution.py:59
  2.4 8.6 %all-to-all-start = ((bf16[32,5,8,128]{3,2,1,0:T(8,128)(2,1)}), bf16[32,5,8,128]{3,2,1,0:T(8,128)(2,1)S(1)}, u32[]{:S(2)}, u32[]{:S(2)}) async-start(bf16[32,5,8,128]{3,2,1,0:T(8,128)(2,1)} %get-tuple-element.19), calls=%async_computation | async-start | bytes 655360 | tf_op jit(solution)/shard_map/all_to_all | solution.py:351
  10.9 1.7 %stage.1.cache_ref = bf16[576,2048]{1,0:T(8,128)(2,1)S(1)} custom-call(bf16[576,2048]{1,0:T(8,128)(2,1)} %bitcast.12), custom_call_target="tpu_custom_call" | custom-call | bytes 5242880 | tf_op jit(solution)/shard_map/stage/pallas_call | solution.py:77
  12.6 0.0 copy-done.2
  12.6 0.9 reduce
  13.5 0.2 reshape.18.query_ref
  13.7 6.8 %all-to-all-done.got_ref = bf16[32,5,8,128]{3,2,1,0:T(8,128)(2,1)S(1)} async-done(((bf16[32,5,8,128]{3,2,1,0:T(8,128)(2,1)}), bf16[32,5,8,128]{3,2,1,0:T(8,128)(2,1)S(1)}, u32[]{:S(2)}, u32[]{:S(2)}) %all-to-all-start) | async-done | bytes 327712 | tf_op jit(solution)/shard_map/all_to_all | solution.py:351
  20.5 0.1 slice_convert_fusion
  20.6 5.0 %pack_pages.1 = bf16[32,576,128]{2,1,0:T(8,128)(2,1)} custom-call(s32[32,2]{1,0:T(8,128)S(1)} %bitcast.11, bf16[576,2048]{1,0:T(8,128)(2,1)S(1)} %stage.1.cache_ref), custom_call_target="tpu_custom_call" | custom-call | bytes 8388608 | tf_op jit(solution)/shard_map/pack_pages/pallas_call | solution.py:132
  25.5 0.0 copy-start.1
  25.6 4.9 %all-to-all-start.1 = ((bf16[32,576,128]{2,1,0:T(8,128)(2,1)}), bf16[32,576,128]{2,1,0:T(8,128)(2,1)}, u32[]{:S(2)}, u32[]{:S(2)}) async-start(bf16[32,576,128]{2,1,0:T(8,128)(2,1)} %pack_pages.1), calls=%async_computation.1 | async-start | bytes 9437184 | tf_op jit(solution)/shard_map/all_to_all | solution.py:356
  30.5 0.0 copy-start
  30.5 0.5 collective-permute-start
  31.0 0.1 pad_add_fusion.place_ref
  31.0 1.2 %collective-permute-done.other_ref = bf16[32,5,8,128]{3,2,1,0:T(8,128)(2,1)S(1)} collective-permute-done((bf16[32,5,8,128]{3,2,1,0:T(8,128)(2,1)S(1)}, bf16[32,5,8,128]{3,2,1,0:T(8,128)(2,1)S(1)}, u32[]{:S(2)}, u32[]{:S(2)}) %collective-permute-start) | collective-permute-done | bytes 327712 | tf_op jit(solution)/shard_map/ppermute | solution.py:347
  32.2 1.1 %partner_parts.1 = (bf16[36,8,128]{2,1,0:T(8,128)(2,1)S(1)}, bf16[36,8,128]{2,1,0:T(8,128)(2,1)S(1)}, bf16[36,8,128]{2,1,0:T(8,128)(2,1)S(1)}, bf16[36,8,128]{2,...) custom-call(s32[2]{0:T(128)S(1)} %pad_add_fusion.place_ref, ...), custom_call_target="tpu_custom_call" | custom-call | bytes 2097152 | tf_op jit(solution)/shard_map/partner_parts/pallas_call | solution.py:173
  33.3 1.9 %collective-permute-start.1 = (bf16[36,8,128]{2,1,0:T(8,128)(2,1)S(1)}, bf16[36,8,128]{2,1,0:T(8,128)(2,1)S(1)}, u32[]{:S(2)}, u32[]{:S(2)}) collective-permute-start(bf16[36,8,128]{2,1,0:T(8,128)(2,1)S(1)} %get-tuple-element.24), channel_id=1, source_target_pairs={{0,1},{1,0},{2,3},{3,2},{4,5},{5,4},{6,7},{7,6},{8,9},{9,8},{10,11... | collective-permute-start | bytes 221192 | tf_op jit(solution)/shard_map/ppermute | solution.py:347
  35.2 3.0 %collective-permute-start.2 = (bf16[36,8,128]{2,1,0:T(8,128)(2,1)S(1)}, bf16[36,8,128]{2,1,0:T(8,128)(2,1)S(1)}, u32[]{:S(2)}, u32[]{:S(2)}) collective-permute-start(bf16[36,8,128]{2,1,0:T(8,128)(2,1)S(1)} %get-tuple-element.25), channel_id=1, source_target_pairs={{0,2},{1,3},{2,0},{3,1},{4,6},{5,7},{6,4},{7,5},{8,10},{9,11},{10,... | collective-permute-start | bytes 221192 | tf_op jit(solution)/shard_map/ppermute | solution.py:347
  38.2 0.0 collective-permute-start.3
  38.2 5.8 %collective-permute-start.4 = (bf16[36,8,128]{2,1,0:T(8,128)(2,1)S(1)}, bf16[36,8,128]{2,1,0:T(8,128)(2,1)S(1)}, u32[]{:S(2)}, u32[]{:S(2)}) collective-permute-start(bf16[36,8,128]{2,1,0:T(8,128)(2,1)S(1)} %get-tuple-element.27), channel_id=1, source_target_pairs={{0,4},{1,5},{2,6},{3,7},{4,0},{5,1},{6,2},{7,3},{8,12},{9,13},{10,... | collective-permute-start | bytes 221192 | tf_op jit(solution)/shard_map/ppermute | solution.py:347
  44.0 0.0 collective-permute-start.5
  44.0 0.0 collective-permute-done.1.refs_1_
  44.0 4.0 %collective-permute-start.6 = (bf16[36,8,128]{2,1,0:T(8,128)(2,1)S(1)}, bf16[36,8,128]{2,1,0:T(8,128)(2,1)S(1)}, u32[]{:S(2)}, u32[]{:S(2)}) collective-permute-start(bf16[36,8,128]{2,1,0:T(8,128)(2,1)S(1)} %get-tuple-element.29), channel_id=1, source_target_pairs={{0,6},{1,7},{2,4},{3,5},{4,2},{5,3},{6,0},{7,1},{8,14},{9,15},{10,... | collective-permute-start | bytes 221192 | tf_op jit(solution)/shard_map/ppermute | solution.py:347
  48.1 0.0 collective-permute-done.2.refs_2_
  48.1 0.0 collective-permute-start.7
  48.1 0.0 collective-permute-done.3.refs_3_
  48.1 0.0 collective-permute-done.4.refs_4_
  48.1 6.2 %collective-permute-done.5.refs_5_ = bf16[36,8,128]{2,1,0:T(8,128)(2,1)S(1)} collective-permute-done((bf16[36,8,128]{2,1,0:T(8,128)(2,1)S(1)}, bf16[36,8,128]{2,1,0:T(8,128)(2,1)S(1)}, u32[]{:S(2)}, u32[]{:S(2)}) %collective-permute-start.5) | collective-permute-done | bytes 73760 | tf_op jit(solution)/shard_map/ppermute | solution.py:347
  54.3 0.0 collective-permute-done.6.refs_6_
  54.3 4.1 %collective-permute-done.7.refs_7_ = bf16[36,8,128]{2,1,0:T(8,128)(2,1)S(1)} collective-permute-done((bf16[36,8,128]{2,1,0:T(8,128)(2,1)S(1)}, bf16[36,8,128]{2,1,0:T(8,128)(2,1)S(1)}, u32[]{:S(2)}, u32[]{:S(2)}) %collective-permute-start.7) | collective-permute-done | bytes 73760 | tf_op jit(solution)/shard_map/ppermute | solution.py:347
  58.4 0.0 copy-done.1
  58.4 4.7 %index_scores.1 = bf16[32,16,128]{2,1,0:T(8,128)(2,1)} custom-call(bf16[2048,128]{1,0:T(8,128)(2,1)S(1)} %copy-done.1, bf16[36,8,128]{2,1,0:T(8,128)(2,1)S(1)} %get-tuple-element.23.refs_0_, bf16[36,8,128]{2,1,0:T(8,128)(2,1)S(1)} %collective-permute-done.1.refs_1_, bf16[36,8,128]{2,1,0:T(8,128)(2,1)S(1)} %collective-permute-done.2.refs_2_, ...), custom_call_target="tpu_custom_call" | custom-call | flops 1073741824 | bytes 2097152 | tf_op jit(solution)/shard_map/index_scores/pallas_call | solution.py:233
  63.1 23.2 %all-to-all-done.1.page_ref = bf16[32,576,128]{2,1,0:T(8,128)(2,1)} async-done(((bf16[32,576,128]{2,1,0:T(8,128)(2,1)}), bf16[32,576,128]{2,1,0:T(8,128)(2,1)}, u32[]{:S(2)}, u32[]{:S(2)}) %all-to-all-start.1) | async-done | bytes 4718624 | tf_op jit(solution)/shard_map/all_to_all | solution.py:356
  86.3 7.8 %all-to-all-start.2 = ((bf16[32,16,128]{2,1,0:T(8,128)(2,1)}), bf16[32,16,128]{2,1,0:T(8,128)(2,1)S(1)}, u32[]{:S(2)}, u32[]{:S(2)}) async-start(bf16[32,16,128]{2,1,0:T(8,128)(2,1)} %index_scores.1), calls=%async_computation.2 | async-start | bytes 262144 | tf_op jit(solution)/shard_map/all_to_all | solution.py:363
  94.1 0.0 copy-done
  94.2 4.9 %attend.1 = bf16[128,512]{1,0:T(8,128)(2,1)S(1)} custom-call(s32[32,1,128]{2,1,0:T(1,128)S(1)} %copy-done, bf16[128,576]{1,0:T(8,128)(2,1)S(1)} %reshape.18.query_ref, bf16[32,576,128]{2,1,0:T(8,128)(2,1)} %all-to-all-done.1.page_ref), custom_call_target="tpu_custom_call" | custom-call | flops 1140850688 | bytes 5242880 | tf_op jit(solution)/shard_map/attend/pallas_call | solution.py:313
  99.0 0.9 copy.15
  99.9 1.9 %all-to-all-done.2 = bf16[32,16,128]{2,1,0:T(8,128)(2,1)S(1)} async-done(((bf16[32,16,128]{2,1,0:T(8,128)(2,1)}), bf16[32,16,128]{2,1,0:T(8,128)(2,1)S(1)}, u32[]{:S(2)}, u32[]{:S(2)}) %all-to-all-start.2) | async-done | bytes 131104 | tf_op jit(solution)/shard_map/all_to_all | solution.py:363
  101.9 1.1 %log_distribution.1 = f32[512,128]{1,0:T(8,128)} custom-call(bf16[512,128]{1,0:T(8,128)(2,1)S(1)} %bitcast.10), custom_call_target="tpu_custom_call" | custom-call | flops 262144 | bytes 393216 | tf_op jit(solution)/shard_map/log_distribution/pallas_call | solution.py:258
Async XLA Ops:
  0.6 12.0 %copy-start.2 = (bf16[1,73728]{1,0:T(2,128)(2,1)S(1)}, bf16[1,73728]{1,0:T(2,128)(2,1)}, u32[]{:S(2)}) copy-start(bf16[1,73728]{1,0:T(2,128)(2,1)} %param.9) | copy-start | bytes 442372
  2.4 18.1 %all-to-all-start = ((bf16[32,5,8,128]{3,2,1,0:T(8,128)(2,1)}), bf16[32,5,8,128]{3,2,1,0:T(8,128)(2,1)S(1)}, u32[]{:S(2)}, u32[]{:S(2)}) async-start(bf16[32,5,8,128]{3,2,1,0:T(8,128)(2,1)} %get-tuple-element.19), calls=%async_computation | async-start | bytes 655360 | tf_op jit(solution)/shard_map/all_to_all | solution.py:351
  25.5 32.9 %copy-start.1 = (bf16[2048,128]{1,0:T(8,128)(2,1)S(1)}, bf16[2048,128]{1,0:T(8,128)(2,1)}, u32[]{:S(2)}) copy-start(bf16[2048,128]{1,0:T(8,128)(2,1)} %key_ref.1) | copy-start | bytes 1572868
  25.6 60.7 %all-to-all-start.1 = ((bf16[32,576,128]{2,1,0:T(8,128)(2,1)}), bf16[32,576,128]{2,1,0:T(8,128)(2,1)}, u32[]{:S(2)}, u32[]{:S(2)}) async-start(bf16[32,576,128]{2,1,0:T(8,128)(2,1)} %pack_pages.1), calls=%async_computation.1 | async-start | bytes 9437184 | tf_op jit(solution)/shard_map/all_to_all | solution.py:356
  30.5 63.7 %copy-start = (s32[32,1,128]{2,1,0:T(1,128)S(1)}, s32[32,1,128]{2,1,0:T(1,128)}, u32[]{:S(2)}) copy-start(s32[32,1,128]{2,1,0:T(1,128)} %get-tuple-element.33.used_ref) | copy-start | bytes 49156
  30.5 1.8 %collective-permute-start = (bf16[32,5,8,128]{3,2,1,0:T(8,128)(2,1)S(1)}, bf16[32,5,8,128]{3,2,1,0:T(8,128)(2,1)S(1)}, u32[]{:S(2)}, u32[]{:S(2)}) collective-permute-start(bf16[32,5,8,128]{3,2,1,0:T(8,128)(2,1)S(1)} %all-to-all-done.got_ref), channel_id=1, source_target_pairs={{0,8},{8,0},{16,24},{24,16},{32,40},{40,32},{48,56},{56,48},{64,72... | collective-permute-start | bytes 983048 | tf_op jit(solution)/shard_map/ppermute | solution.py:347
  33.3 10.7 %collective-permute-start.1 = (bf16[36,8,128]{2,1,0:T(8,128)(2,1)S(1)}, bf16[36,8,128]{2,1,0:T(8,128)(2,1)S(1)}, u32[]{:S(2)}, u32[]{:S(2)}) collective-permute-start(bf16[36,8,128]{2,1,0:T(8,128)(2,1)S(1)} %get-tuple-element.24), channel_id=1, source_target_pairs={{0,1},{1,0},{2,3},{3,2},{4,5},{5,4},{6,7},{7,6},{8,9},{9,8},{10,11... | collective-permute-start | bytes 221192 | tf_op jit(solution)/shard_map/ppermute | solution.py:347
  35.2 12.9 %collective-permute-start.2 = (bf16[36,8,128]{2,1,0:T(8,128)(2,1)S(1)}, bf16[36,8,128]{2,1,0:T(8,128)(2,1)S(1)}, u32[]{:S(2)}, u32[]{:S(2)}) collective-permute-start(bf16[36,8,128]{2,1,0:T(8,128)(2,1)S(1)} %get-tuple-element.25), channel_id=1, source_target_pairs={{0,2},{1,3},{2,0},{3,1},{4,6},{5,7},{6,4},{7,5},{8,10},{9,11},{10,... | collective-permute-start | bytes 221192 | tf_op jit(solution)/shard_map/ppermute | solution.py:347
  38.2 9.9 %collective-permute-start.3 = (bf16[36,8,128]{2,1,0:T(8,128)(2,1)S(1)}, bf16[36,8,128]{2,1,0:T(8,128)(2,1)S(1)}, u32[]{:S(2)}, u32[]{:S(2)}) collective-permute-start(bf16[36,8,128]{2,1,0:T(8,128)(2,1)S(1)} %get-tuple-element.26), channel_id=1, source_target_pairs={{0,3},{1,2},{2,1},{3,0},{4,7},{5,6},{6,5},{7,4},{8,11},{9,10},{10,... | collective-permute-start | bytes 221192 | tf_op jit(solution)/shard_map/ppermute | solution.py:347
  38.2 9.9 %collective-permute-start.4 = (bf16[36,8,128]{2,1,0:T(8,128)(2,1)S(1)}, bf16[36,8,128]{2,1,0:T(8,128)(2,1)S(1)}, u32[]{:S(2)}, u32[]{:S(2)}) collective-permute-start(bf16[36,8,128]{2,1,0:T(8,128)(2,1)S(1)} %get-tuple-element.27), channel_id=1, source_target_pairs={{0,4},{1,5},{2,6},{3,7},{4,0},{5,1},{6,2},{7,3},{8,12},{9,13},{10,... | collective-permute-start | bytes 221192 | tf_op jit(solution)/shard_map/ppermute | solution.py:347
  44.0 10.2 %collective-permute-start.5 = (bf16[36,8,128]{2,1,0:T(8,128)(2,1)S(1)}, bf16[36,8,128]{2,1,0:T(8,128)(2,1)S(1)}, u32[]{:S(2)}, u32[]{:S(2)}) collective-permute-start(bf16[36,8,128]{2,1,0:T(8,128)(2,1)S(1)} %get-tuple-element.28), channel_id=1, source_target_pairs={{0,5},{1,4},{2,7},{3,6},{4,1},{5,0},{6,3},{7,2},{8,13},{9,12},{10,... | collective-permute-start | bytes 221192 | tf_op jit(solution)/shard_map/ppermute | solution.py:347
  44.0 10.2 %collective-permute-start.6 = (bf16[36,8,128]{2,1,0:T(8,128)(2,1)S(1)}, bf16[36,8,128]{2,1,0:T(8,128)(2,1)S(1)}, u32[]{:S(2)}, u32[]{:S(2)}) collective-permute-start(bf16[36,8,128]{2,1,0:T(8,128)(2,1)S(1)} %get-tuple-element.29), channel_id=1, source_target_pairs={{0,6},{1,7},{2,4},{3,5},{4,2},{5,3},{6,0},{7,1},{8,14},{9,15},{10,... | collective-permute-start | bytes 221192 | tf_op jit(solution)/shard_map/ppermute | solution.py:347
  48.1 10.3 %collective-permute-start.7 = (bf16[36,8,128]{2,1,0:T(8,128)(2,1)S(1)}, bf16[36,8,128]{2,1,0:T(8,128)(2,1)S(1)}, u32[]{:S(2)}, u32[]{:S(2)}) collective-permute-start(bf16[36,8,128]{2,1,0:T(8,128)(2,1)S(1)} %get-tuple-element.30), channel_id=1, source_target_pairs={{0,7},{1,6},{2,5},{3,4},{4,3},{5,2},{6,1},{7,0},{8,15},{9,14},{10,... | collective-permute-start | bytes 221192 | tf_op jit(solution)/shard_map/ppermute | solution.py:347
  86.3 15.6 %all-to-all-start.2 = ((bf16[32,16,128]{2,1,0:T(8,128)(2,1)}), bf16[32,16,128]{2,1,0:T(8,128)(2,1)S(1)}, u32[]{:S(2)}, u32[]{:S(2)}) async-start(bf16[32,16,128]{2,1,0:T(8,128)(2,1)} %index_scores.1), calls=%async_computation.2 | async-start | bytes 262144 | tf_op jit(solution)/shard_map/all_to_all | solution.py:363

commit v8 on v7

--- a/solution.py
+++ b/solution.py
@@ -106,11 +106,18 @@
     for r in range(peers):
         first = table_ref[r, 0]
         second = table_ref[r, 1]
-        first = jnp.where(first > 0, first - 1, 0)
-        second = jnp.where(second > 0, second - 1, 1)
+        first, second = (
+            jnp.where(first > 0, first - 1, jnp.where(second > 0, second - 2, 0)),
+            jnp.where(second > 0, second - 1, jnp.where(first > 0, first, 1)),
+        )
         straight = (first % 2 == 0) & (second % 2 == 1)
-
-        @pl.when(straight)
+        beside = straight & (first + 1 == second)
+
+        @pl.when(beside)
+        def _(r=r, first=first):
+            stage_ref[r] = tile(first)
+
+        @pl.when(straight & jnp.logical_not(beside))
         def _(r=r, first=first, second=second):
             stage_ref[r] = jnp.where(left, tile(first), tile(second))
 

time: 103 us -> 103 us (level)
  waiting for transfers between devices: 43.4 us -> 40.7 us
  starting transfers between devices: 36.6 us -> 39.2 us
    ppermute x8, waiting for transfers between devices: 11.5 us -> 8.73 us  [swap(): return lax.ppermute(x, axis, [(i, i ^ bits) for i in range(size)])]
    ppermute x8, starting transfers between devices: 15.3 us -> 17.8 us  [swap(): return lax.ppermute(x, axis, [(i, i ^ bits) for i in range(size)])]
where the time goes in v8:
time: 103 us; the launch traced here: 102 us
  waiting for transfers between devices  40.7 us (40%)
  starting transfers between devices  39.2 us (38%)
  Pallas kernels  19.4 us (19%)
  local copies, waits for them, and re-layouts  1.07 us (1%)
  other arithmetic  1.03 us (1%)
    all_to_all x1, waiting for transfers between devices, per_device(): pages = exchange(packed)  23.2 us
    ppermute x8, starting transfers between devices, swap(): return lax.ppermute(x, axis, [(i, i ^ bits) for i in range(size)])  17.8 us
    ppermute x8, waiting for transfers between devices, swap(): return lax.ppermute(x, axis, [(i, i ^ bits) for i in range(size)])  8.73 us
    all_to_all x1, starting transfers between devices, per_device(): exchange(sent)  8.59 us
    all_to_all x1, starting transfers between devices, per_device(): scores = exchange(scores)  7.83 us
    all_to_all x1, waiting for transfers between devices, per_device(): exchange(sent)  6.81 us
    all_to_all x1, starting transfers between devices, per_device(): pages = exchange(packed)  4.97 us
    pallas_call x1, Pallas kernels, attend(): pl.pallas_call(attend_kernel, grid=(peers // sources,), in_specs=[pl.Bloc...  4.87 us
  transfers between devices with their start and end apart: 11, of which 6 were waited for; matrix products, arithmetic and copies ran while one was open for 2% of the time, Pallas kernels for 12%

profile of v8, /device:TPU:1, one launch (start us, length us, event | category | flops | bytes accessed | tf_op | source)
XLA Modules:
  0.0 102.2 jit_solution(6504784509690093338)
XLA Ops:
  0.6 0.0 copy-start.2
  0.6 1.7 %requests.1 = (bf16[32,5,8,128]{3,2,1,0:T(8,128)(2,1)}, s32[32,1,128]{2,1,0:T(1,128)}) custom-call(s32[1,32]{1,0:T(1,128)} %ids_ref.1, bf16[8,1024]{1,0:T(8,128)(2,1)} %query_ref.1, bf16[8,8]{1,0:T(8,128)(2,1)} %weight_ref.1), custom_call_target="tpu_custom_call" | custom-call | tf_op jit(solution)/shard_map/requests/pallas_call | solution.py:59
  2.4 8.6 %all-to-all-start = ((bf16[32,5,8,128]{3,2,1,0:T(8,128)(2,1)}), bf16[32,5,8,128]{3,2,1,0:T(8,128)(2,1)S(1)}, u32[]{:S(2)}, u32[]{:S(2)}) async-start(bf16[32,5,8,128]{3,2,1,0:T(8,128)(2,1)} %get-tuple-element.19), calls=%async_computation | async-start | bytes 655360 | tf_op jit(solution)/shard_map/all_to_all | solution.py:358
  10.9 1.7 %stage.1.cache_ref = bf16[576,2048]{1,0:T(8,128)(2,1)S(1)} custom-call(bf16[576,2048]{1,0:T(8,128)(2,1)} %bitcast.12), custom_call_target="tpu_custom_call" | custom-call | bytes 5242880 | tf_op jit(solution)/shard_map/stage/pallas_call | solution.py:77
  12.6 0.0 copy-done.2
  12.6 0.9 reduce
  13.5 0.2 reshape.18.query_ref
  13.7 6.8 %all-to-all-done.got_ref = bf16[32,5,8,128]{3,2,1,0:T(8,128)(2,1)S(1)} async-done(((bf16[32,5,8,128]{3,2,1,0:T(8,128)(2,1)}), bf16[32,5,8,128]{3,2,1,0:T(8,128)(2,1)S(1)}, u32[]{:S(2)}, u32[]{:S(2)}) %all-to-all-start) | async-done | bytes 327712 | tf_op jit(solution)/shard_map/all_to_all | solution.py:358
  20.5 0.1 slice_convert_fusion
  20.6 4.2 %pack_pages.1 = bf16[32,576,128]{2,1,0:T(8,128)(2,1)} custom-call(s32[32,2]{1,0:T(8,128)S(1)} %bitcast.11, bf16[576,2048]{1,0:T(8,128)(2,1)S(1)} %stage.1.cache_ref), custom_call_target="tpu_custom_call" | custom-call | bytes 8388608 | tf_op jit(solution)/shard_map/pack_pages/pallas_call | solution.py:139
  24.8 0.0 copy-start.1
  24.8 5.0 %all-to-all-start.1 = ((bf16[32,576,128]{2,1,0:T(8,128)(2,1)}), bf16[32,576,128]{2,1,0:T(8,128)(2,1)}, u32[]{:S(2)}, u32[]{:S(2)}) async-start(bf16[32,576,128]{2,1,0:T(8,128)(2,1)} %pack_pages.1), calls=%async_computation.1 | async-start | bytes 9437184 | tf_op jit(solution)/shard_map/all_to_all | solution.py:363
  29.8 0.0 copy-start
  29.8 0.3 collective-permute-start
  30.1 0.1 pad_add_fusion.place_ref
  30.2 1.3 %collective-permute-done.other_ref = bf16[32,5,8,128]{3,2,1,0:T(8,128)(2,1)S(1)} collective-permute-done((bf16[32,5,8,128]{3,2,1,0:T(8,128)(2,1)S(1)}, bf16[32,5,8,128]{3,2,1,0:T(8,128)(2,1)S(1)}, u32[]{:S(2)}, u32[]{:S(2)}) %collective-permute-start) | collective-permute-done | bytes 327712 | tf_op jit(solution)/shard_map/ppermute | solution.py:354
  31.5 1.1 %partner_parts.1 = (bf16[36,8,128]{2,1,0:T(8,128)(2,1)S(1)}, bf16[36,8,128]{2,1,0:T(8,128)(2,1)S(1)}, bf16[36,8,128]{2,1,0:T(8,128)(2,1)S(1)}, bf16[36,8,128]{2,...) custom-call(s32[2]{0:T(128)S(1)} %pad_add_fusion.place_ref, ...), custom_call_target="tpu_custom_call" | custom-call | bytes 2097152 | tf_op jit(solution)/shard_map/partner_parts/pallas_call | solution.py:180
  32.6 1.6 %collective-permute-start.1 = (bf16[36,8,128]{2,1,0:T(8,128)(2,1)S(1)}, bf16[36,8,128]{2,1,0:T(8,128)(2,1)S(1)}, u32[]{:S(2)}, u32[]{:S(2)}) collective-permute-start(bf16[36,8,128]{2,1,0:T(8,128)(2,1)S(1)} %get-tuple-element.24), channel_id=1, source_target_pairs={{0,1},{1,0},{2,3},{3,2},{4,5},{5,4},{6,7},{7,6},{8,9},{9,8},{10,11... | collective-permute-start | bytes 221192 | tf_op jit(solution)/shard_map/ppermute | solution.py:354
  34.2 3.0 %collective-permute-start.2 = (bf16[36,8,128]{2,1,0:T(8,128)(2,1)S(1)}, bf16[36,8,128]{2,1,0:T(8,128)(2,1)S(1)}, u32[]{:S(2)}, u32[]{:S(2)}) collective-permute-start(bf16[36,8,128]{2,1,0:T(8,128)(2,1)S(1)} %get-tuple-element.25), channel_id=1, source_target_pairs={{0,2},{1,3},{2,0},{3,1},{4,6},{5,7},{6,4},{7,5},{8,10},{9,11},{10,... | collective-permute-start | bytes 221192 | tf_op jit(solution)/shard_map/ppermute | solution.py:354
  37.2 0.0 collective-permute-start.3
  37.2 5.8 %collective-permute-start.4 = (bf16[36,8,128]{2,1,0:T(8,128)(2,1)S(1)}, bf16[36,8,128]{2,1,0:T(8,128)(2,1)S(1)}, u32[]{:S(2)}, u32[]{:S(2)}) collective-permute-start(bf16[36,8,128]{2,1,0:T(8,128)(2,1)S(1)} %get-tuple-element.27), channel_id=1, source_target_pairs={{0,4},{1,5},{2,6},{3,7},{4,0},{5,1},{6,2},{7,3},{8,12},{9,13},{10,... | collective-permute-start | bytes 221192 | tf_op jit(solution)/shard_map/ppermute | solution.py:354
  43.0 0.0 collective-permute-start.5
  43.0 0.0 collective-permute-done.1.refs_1_
  43.0 4.0 %collective-permute-start.6 = (bf16[36,8,128]{2,1,0:T(8,128)(2,1)S(1)}, bf16[36,8,128]{2,1,0:T(8,128)(2,1)S(1)}, u32[]{:S(2)}, u32[]{:S(2)}) collective-permute-start(bf16[36,8,128]{2,1,0:T(8,128)(2,1)S(1)} %get-tuple-element.29), channel_id=1, source_target_pairs={{0,6},{1,7},{2,4},{3,5},{4,2},{5,3},{6,0},{7,1},{8,14},{9,15},{10,... | collective-permute-start | bytes 221192 | tf_op jit(solution)/shard_map/ppermute | solution.py:354
  47.1 0.0 collective-permute-done.2.refs_2_
  47.1 3.1 %collective-permute-start.7 = (bf16[36,8,128]{2,1,0:T(8,128)(2,1)S(1)}, bf16[36,8,128]{2,1,0:T(8,128)(2,1)S(1)}, u32[]{:S(2)}, u32[]{:S(2)}) collective-permute-start(bf16[36,8,128]{2,1,0:T(8,128)(2,1)S(1)} %get-tuple-element.30), channel_id=1, source_target_pairs={{0,7},{1,6},{2,5},{3,4},{4,3},{5,2},{6,1},{7,0},{8,15},{9,14},{10,... | collective-permute-start | bytes 221192 | tf_op jit(solution)/shard_map/ppermute | solution.py:354
  50.1 0.0 collective-permute-done.3.refs_3_
  50.1 0.0 collective-permute-done.4.refs_4_
  50.1 3.4 %collective-permute-done.5.refs_5_ = bf16[36,8,128]{2,1,0:T(8,128)(2,1)S(1)} collective-permute-done((bf16[36,8,128]{2,1,0:T(8,128)(2,1)S(1)}, bf16[36,8,128]{2,1,0:T(8,128)(2,1)S(1)}, u32[]{:S(2)}, u32[]{:S(2)}) %collective-permute-start.5) | collective-permute-done | bytes 73760 | tf_op jit(solution)/shard_map/ppermute | solution.py:354
  53.5 0.0 collective-permute-done.6.refs_6_
  53.5 4.0 %collective-permute-done.7.refs_7_ = bf16[36,8,128]{2,1,0:T(8,128)(2,1)S(1)} collective-permute-done((bf16[36,8,128]{2,1,0:T(8,128)(2,1)S(1)}, bf16[36,8,128]{2,1,0:T(8,128)(2,1)S(1)}, u32[]{:S(2)}, u32[]{:S(2)}) %collective-permute-start.7) | collective-permute-done | bytes 73760 | tf_op jit(solution)/shard_map/ppermute | solution.py:354
  57.5 0.0 copy-done.1
  57.5 4.7 %index_scores.1 = bf16[32,16,128]{2,1,0:T(8,128)(2,1)} custom-call(bf16[2048,128]{1,0:T(8,128)(2,1)S(1)} %copy-done.1, bf16[36,8,128]{2,1,0:T(8,128)(2,1)S(1)} %get-tuple-element.23.refs_0_, bf16[36,8,128]{2,1,0:T(8,128)(2,1)S(1)} %collective-permute-done.1.refs_1_, bf16[36,8,128]{2,1,0:T(8,128)(2,1)S(1)} %collective-permute-done.2.refs_2_, ...), custom_call_target="tpu_custom_call" | custom-call | flops 1073741824 | bytes 2097152 | tf_op jit(solution)/shard_map/index_scores/pallas_call | solution.py:240
  62.3 23.2 %all-to-all-done.1.page_ref = bf16[32,576,128]{2,1,0:T(8,128)(2,1)} async-done(((bf16[32,576,128]{2,1,0:T(8,128)(2,1)}), bf16[32,576,128]{2,1,0:T(8,128)(2,1)}, u32[]{:S(2)}, u32[]{:S(2)}) %all-to-all-start.1) | async-done | bytes 4718624 | tf_op jit(solution)/shard_map/all_to_all | solution.py:363
  85.5 7.8 %all-to-all-start.2 = ((bf16[32,16,128]{2,1,0:T(8,128)(2,1)}), bf16[32,16,128]{2,1,0:T(8,128)(2,1)S(1)}, u32[]{:S(2)}, u32[]{:S(2)}) async-start(bf16[32,16,128]{2,1,0:T(8,128)(2,1)} %index_scores.1), calls=%async_computation.2 | async-start | bytes 262144 | tf_op jit(solution)/shard_map/all_to_all | solution.py:370
  93.3 0.0 copy-done
  93.3 4.9 %attend.1 = bf16[128,512]{1,0:T(8,128)(2,1)S(1)} custom-call(s32[32,1,128]{2,1,0:T(1,128)S(1)} %copy-done, bf16[128,576]{1,0:T(8,128)(2,1)S(1)} %reshape.18.query_ref, bf16[32,576,128]{2,1,0:T(8,128)(2,1)} %all-to-all-done.1.page_ref), custom_call_target="tpu_custom_call" | custom-call | flops 1140850688 | bytes 5242880 | tf_op jit(solution)/shard_map/attend/pallas_call | solution.py:320
  98.2 0.9 copy.15
  99.1 1.9 %all-to-all-done.2 = bf16[32,16,128]{2,1,0:T(8,128)(2,1)S(1)} async-done(((bf16[32,16,128]{2,1,0:T(8,128)(2,1)}), bf16[32,16,128]{2,1,0:T(8,128)(2,1)S(1)}, u32[]{:S(2)}, u32[]{:S(2)}) %all-to-all-start.2) | async-done | bytes 131104 | tf_op jit(solution)/shard_map/all_to_all | solution.py:370
  101.0 1.1 %log_distribution.1 = f32[512,128]{1,0:T(8,128)} custom-call(bf16[512,128]{1,0:T(8,128)(2,1)S(1)} %bitcast.10), custom_call_target="tpu_custom_call" | custom-call | flops 262144 | bytes 393216 | tf_op jit(solution)/shard_map/log_distribution/pallas_call | solution.py:265
Async XLA Ops:
  0.6 12.0 %copy-start.2 = (bf16[1,73728]{1,0:T(2,128)(2,1)S(1)}, bf16[1,73728]{1,0:T(2,128)(2,1)}, u32[]{:S(2)}) copy-start(bf16[1,73728]{1,0:T(2,128)(2,1)} %param.9) | copy-start | bytes 442372
  2.4 18.1 %all-to-all-start = ((bf16[32,5,8,128]{3,2,1,0:T(8,128)(2,1)}), bf16[32,5,8,128]{3,2,1,0:T(8,128)(2,1)S(1)}, u32[]{:S(2)}, u32[]{:S(2)}) async-start(bf16[32,5,8,128]{3,2,1,0:T(8,128)(2,1)} %get-tuple-element.19), calls=%async_computation | async-start | bytes 655360 | tf_op jit(solution)/shard_map/all_to_all | solution.py:358
  24.8 32.7 %copy-start.1 = (bf16[2048,128]{1,0:T(8,128)(2,1)S(1)}, bf16[2048,128]{1,0:T(8,128)(2,1)}, u32[]{:S(2)}) copy-start(bf16[2048,128]{1,0:T(8,128)(2,1)} %key_ref.1) | copy-start | bytes 1572868
  24.8 60.7 %all-to-all-start.1 = ((bf16[32,576,128]{2,1,0:T(8,128)(2,1)}), bf16[32,576,128]{2,1,0:T(8,128)(2,1)}, u32[]{:S(2)}, u32[]{:S(2)}) async-start(bf16[32,576,128]{2,1,0:T(8,128)(2,1)} %pack_pages.1), calls=%async_computation.1 | async-start | bytes 9437184 | tf_op jit(solution)/shard_map/all_to_all | solution.py:363
  29.8 63.5 %copy-start = (s32[32,1,128]{2,1,0:T(1,128)S(1)}, s32[32,1,128]{2,1,0:T(1,128)}, u32[]{:S(2)}) copy-start(s32[32,1,128]{2,1,0:T(1,128)} %get-tuple-element.33.used_ref) | copy-start | bytes 49156
  29.8 1.7 %collective-permute-start = (bf16[32,5,8,128]{3,2,1,0:T(8,128)(2,1)S(1)}, bf16[32,5,8,128]{3,2,1,0:T(8,128)(2,1)S(1)}, u32[]{:S(2)}, u32[]{:S(2)}) collective-permute-start(bf16[32,5,8,128]{3,2,1,0:T(8,128)(2,1)S(1)} %all-to-all-done.got_ref), channel_id=1, source_target_pairs={{0,8},{8,0},{16,24},{24,16},{32,40},{40,32},{48,56},{56,48},{64,72... | collective-permute-start | bytes 983048 | tf_op jit(solution)/shard_map/ppermute | solution.py:354
  32.6 10.4 %collective-permute-start.1 = (bf16[36,8,128]{2,1,0:T(8,128)(2,1)S(1)}, bf16[36,8,128]{2,1,0:T(8,128)(2,1)S(1)}, u32[]{:S(2)}, u32[]{:S(2)}) collective-permute-start(bf16[36,8,128]{2,1,0:T(8,128)(2,1)S(1)} %get-tuple-element.24), channel_id=1, source_target_pairs={{0,1},{1,0},{2,3},{3,2},{4,5},{5,4},{6,7},{7,6},{8,9},{9,8},{10,11... | collective-permute-start | bytes 221192 | tf_op jit(solution)/shard_map/ppermute | solution.py:354
  34.2 12.8 %collective-permute-start.2 = (bf16[36,8,128]{2,1,0:T(8,128)(2,1)S(1)}, bf16[36,8,128]{2,1,0:T(8,128)(2,1)S(1)}, u32[]{:S(2)}, u32[]{:S(2)}) collective-permute-start(bf16[36,8,128]{2,1,0:T(8,128)(2,1)S(1)} %get-tuple-element.25), channel_id=1, source_target_pairs={{0,2},{1,3},{2,0},{3,1},{4,6},{5,7},{6,4},{7,5},{8,10},{9,11},{10,... | collective-permute-start | bytes 221192 | tf_op jit(solution)/shard_map/ppermute | solution.py:354
  37.2 12.9 %collective-permute-start.3 = (bf16[36,8,128]{2,1,0:T(8,128)(2,1)S(1)}, bf16[36,8,128]{2,1,0:T(8,128)(2,1)S(1)}, u32[]{:S(2)}, u32[]{:S(2)}) collective-permute-start(bf16[36,8,128]{2,1,0:T(8,128)(2,1)S(1)} %get-tuple-element.26), channel_id=1, source_target_pairs={{0,3},{1,2},{2,1},{3,0},{4,7},{5,6},{6,5},{7,4},{8,11},{9,10},{10,... | collective-permute-start | bytes 221192 | tf_op jit(solution)/shard_map/ppermute | solution.py:354
  37.2 12.9 %collective-permute-start.4 = (bf16[36,8,128]{2,1,0:T(8,128)(2,1)S(1)}, bf16[36,8,128]{2,1,0:T(8,128)(2,1)S(1)}, u32[]{:S(2)}, u32[]{:S(2)}) collective-permute-start(bf16[36,8,128]{2,1,0:T(8,128)(2,1)S(1)} %get-tuple-element.27), channel_id=1, source_target_pairs={{0,4},{1,5},{2,6},{3,7},{4,0},{5,1},{6,2},{7,3},{8,12},{9,13},{10,... | collective-permute-start | bytes 221192 | tf_op jit(solution)/shard_map/ppermute | solution.py:354
  43.0 10.5 %collective-permute-start.5 = (bf16[36,8,128]{2,1,0:T(8,128)(2,1)S(1)}, bf16[36,8,128]{2,1,0:T(8,128)(2,1)S(1)}, u32[]{:S(2)}, u32[]{:S(2)}) collective-permute-start(bf16[36,8,128]{2,1,0:T(8,128)(2,1)S(1)} %get-tuple-element.28), channel_id=1, source_target_pairs={{0,5},{1,4},{2,7},{3,6},{4,1},{5,0},{6,3},{7,2},{8,13},{9,12},{10,... | collective-permute-start | bytes 221192 | tf_op jit(solution)/shard_map/ppermute | solution.py:354
  43.0 10.5 %collective-permute-start.6 = (bf16[36,8,128]{2,1,0:T(8,128)(2,1)S(1)}, bf16[36,8,128]{2,1,0:T(8,128)(2,1)S(1)}, u32[]{:S(2)}, u32[]{:S(2)}) collective-permute-start(bf16[36,8,128]{2,1,0:T(8,128)(2,1)S(1)} %get-tuple-element.29), channel_id=1, source_target_pairs={{0,6},{1,7},{2,4},{3,5},{4,2},{5,3},{6,0},{7,1},{8,14},{9,15},{10,... | collective-permute-start | bytes 221192 | tf_op jit(solution)/shard_map/ppermute | solution.py:354
  47.1 10.5 %collective-permute-start.7 = (bf16[36,8,128]{2,1,0:T(8,128)(2,1)S(1)}, bf16[36,8,128]{2,1,0:T(8,128)(2,1)S(1)}, u32[]{:S(2)}, u32[]{:S(2)}) collective-permute-start(bf16[36,8,128]{2,1,0:T(8,128)(2,1)S(1)} %get-tuple-element.30), channel_id=1, source_target_pairs={{0,7},{1,6},{2,5},{3,4},{4,3},{5,2},{6,1},{7,0},{8,15},{9,14},{10,... | collective-permute-start | bytes 221192 | tf_op jit(solution)/shard_map/ppermute | solution.py:354
  85.5 15.6 %all-to-all-start.2 = ((bf16[32,16,128]{2,1,0:T(8,128)(2,1)}), bf16[32,16,128]{2,1,0:T(8,128)(2,1)S(1)}, u32[]{:S(2)}, u32[]{:S(2)}) async-start(bf16[32,16,128]{2,1,0:T(8,128)(2,1)} %index_scores.1), calls=%async_computation.2 | async-start | bytes 262144 | tf_op jit(solution)/shard_map/all_to_all | solution.py:370

commit v9 on v8

--- a/solution.py
+++ b/solution.py
@@ -17,14 +17,14 @@
 PAGE = 64
 TOPP = 32
 LANES = 128
+CORES = 2
 NEG = -1e30
 MIB = 1 << 20
 
 
 def request_kernel(pages_dev, ids_ref, query_ref, weight_ref, out_ref, table_ref, turn_ref):
-    owners = out_ref.shape[0]
+    owners = table_ref.shape[0]
     rows, heads = weight_ref.shape
-    part = rows // 2
     ids = ids_ref[...]
     owner, local = ids // pages_dev, ids % pages_dev
     mine = owner == lax.broadcasted_iota(jnp.int32, (owners, TOPP), 0)
@@ -42,16 +42,19 @@
     weight = jnp.concatenate(
         [weight_ref[...].astype(jnp.float32), jnp.zeros((rows, LANES - heads), jnp.float32)], axis=1
     )
-    asked = jnp.where(lane == heads, left, jnp.where(lane == heads + 1, right, 0))
-    asked = asked.astype(jnp.float32).reshape(owners, 1, LANES)
+    pair = table.reshape(owners // CORES, CORES, LANES).astype(jnp.float32)
+    lane = lax.broadcasted_iota(jnp.int32, (owners // CORES, LANES), 1)
+    asked = jnp.zeros((owners // CORES, LANES), jnp.float32)
+    for core in range(CORES):
+        for s in range(2):
+            asked = jnp.where(lane == heads + 2 * core + s, pair[:, core, s : s + 1], asked)
     for h in range(heads):
         turn_ref[pl.ds(h, rows, stride=heads), :] = query_ref[
             :, h * LANES : (h + 1) * LANES
         ].astype(jnp.float32)
     query = turn_ref[...].astype(out_ref.dtype).reshape(rows, heads, LANES)
-    for t in range(owners):
-        out_ref[t, :part] = query[t % 2 * part : (t % 2 + 1) * part]
-    out_ref[:, part] = (weight[None] + asked).astype(out_ref.dtype)
+    out_ref[:, :rows] = jnp.broadcast_to(query[None], (owners // CORES, rows, heads, LANES))
+    out_ref[:, rows] = (weight[None] + asked[:, None]).astype(out_ref.dtype)
 
 
 def requests(page_ids, query, weight, owners, pages_dev):
@@ -59,7 +62,7 @@
     return pl.pallas_call(
         functools.partial(request_kernel, pages_dev),
         out_shape=(
-            pltpu.HBM((owners, rows // 2 + 1, heads, LANES), query.dtype),
+            pltpu.HBM((owners // CORES, rows + 1, heads, LANES), query.dtype),
             jax.ShapeDtypeStruct((owners, 1, LANES), jnp.int32),
         ),
         scratch_shapes=[pltpu.VMEM((rows * heads, LANES), jnp.float32)],
@@ -86,26 +89,22 @@
     )(cache)
 
 
-GROUP = 4
-
-
-def pack_kernel(table_ref, cache_ref, out_hbm, stage_ref, out_sems):
-    peers = stage_ref.shape[0]
+def pack_kernel(place_ref, table_ref, own_ref, other_hbm, out_hbm, other_ref, stage_ref, in_sem, out_sems):
+    peers = table_ref.shape[0]
+    load = pltpu.make_async_copy(other_hbm, other_ref, in_sem)
+    load.start()
     left = lax.broadcasted_iota(jnp.int32, (DK, LANES), 1) < PAGE
-
-    def tile(page):
-        return cache_ref[:, pl.ds(pl.multiple_of(page // 2 * LANES, LANES), LANES)]
 
     def turned(x):
         return jnp.concatenate([x[:, PAGE:], x[:, :PAGE]], axis=1)
 
-    def send(g):
-        peer = pl.ds(g * GROUP, GROUP)
-        return pltpu.make_async_copy(stage_ref.at[peer], out_hbm.at[peer], out_sems.at[g])
-
-    for r in range(peers):
-        first = table_ref[r, 0]
-        second = table_ref[r, 1]
+    def send(at, block):
+        return pltpu.make_async_copy(stage_ref.at[at], out_hbm.at[block], out_sems.at[at])
+
+    def pack(at, block, cache_ref, first, second):
+        def tile(page):
+            return cache_ref[:, pl.ds(pl.multiple_of(page // 2 * LANES, LANES), LANES)]
+
         first, second = (
             jnp.where(first > 0, first - 1, jnp.where(second > 0, second - 2, 0)),
             jnp.where(second > 0, second - 1, jnp.where(first > 0, first, 1)),
@@ -114,81 +113,89 @@
         beside = straight & (first + 1 == second)
 
         @pl.when(beside)
-        def _(r=r, first=first):
-            stage_ref[r] = tile(first)
+        def _():
+            stage_ref[at] = tile(first)
 
         @pl.when(straight & jnp.logical_not(beside))
-        def _(r=r, first=first, second=second):
-            stage_ref[r] = jnp.where(left, tile(first), tile(second))
+        def _():
+            stage_ref[at] = jnp.where(left, tile(first), tile(second))
 
         @pl.when(jnp.logical_not(straight))
-        def _(r=r, first=first, second=second):
+        def _():
             a, b = tile(first), tile(second)
             a = jnp.where(first % 2 == 0, a, turned(a))
             b = jnp.where(second % 2 == 1, b, turned(b))
-            stage_ref[r] = jnp.where(left, a, b)
-
-        if r % GROUP == GROUP - 1:
-            send(r // GROUP).start()
-    for g in range(peers // GROUP):
-        send(g).wait()
-
-
-def pack_pages(table, cache):
-    peers = table.shape[0]
+            stage_ref[at] = jnp.where(left, a, b)
+
+        send(at, block).start()
+
+    own = place_ref[1]
+    for half, (cache_ref, core) in enumerate(((own_ref, own), (other_ref, 1 - own))):
+        if half == 1:
+            load.wait()
+        for r in range(peers):
+            pack(
+                half * peers + r,
+                CORES * r + core,
+                cache_ref,
+                table_ref[r, 2 * core],
+                table_ref[r, 2 * core + 1],
+            )
+    for half, core in enumerate((own, 1 - own)):
+        for r in range(peers):
+            send(half * peers + r, CORES * r + core).wait()
+
+
+def pack_pages(place, table, own, other):
+    blocks = table.shape[0] * CORES
     return pl.pallas_call(
         pack_kernel,
         in_specs=[
             pl.BlockSpec(memory_space=pltpu.SMEM),
+            pl.BlockSpec(memory_space=pltpu.SMEM),
             pl.BlockSpec(memory_space=pltpu.VMEM),
+            pl.BlockSpec(memory_space=pltpu.HBM),
         ],
         out_specs=pl.BlockSpec(memory_space=pltpu.HBM),
-        out_shape=pltpu.HBM((peers, DK, LANES), cache.dtype),
+        out_shape=pltpu.HBM((blocks, DK, LANES), own.dtype),
         scratch_shapes=[
-            pltpu.VMEM((peers, DK, LANES), cache.dtype),
-            pltpu.SemaphoreType.DMA((peers // GROUP,)),
+            pltpu.VMEM(own.shape, own.dtype),
+            pltpu.VMEM((blocks, DK, LANES), own.dtype),
+            pltpu.SemaphoreType.DMA,
+            pltpu.SemaphoreType.DMA((blocks,)),
         ],
-        compiler_params=pltpu.CompilerParams(vmem_limit_bytes=24 * MIB),
+        compiler_params=pltpu.CompilerParams(vmem_limit_bytes=50 * MIB),
         cost_estimate=pl.CostEstimate(flops=0, bytes_accessed=8 * MIB, transcendentals=0),
         name="pack_pages",
-    )(table, cache)
-
-
-def partner_kernel(place_ref, got_ref, other_ref, *out_refs):
-    peers, part = got_ref.shape[0], got_ref.shape[1] - 1
-    weights = got_ref[:, part].astype(jnp.float32)
+    )(place, table, own, other)
+
+
+def partner_kernel(place_ref, got_ref, *out_refs):
+    peers = got_ref.shape[0]
+    rows = len(out_refs)
+    weights = got_ref[:, rows].astype(jnp.float32)
     place = lax.broadcasted_iota(jnp.int32, weights.shape, 1)
     for d, out_ref in enumerate(out_refs):
         row = place_ref[0] ^ d
-        mine = row // part == place_ref[1]
-
-        @pl.when(mine)
-        def _(out_ref=out_ref, row=row):
-            out_ref[:peers] = got_ref[:, row % part]
-
-        @pl.when(jnp.logical_not(mine))
-        def _(out_ref=out_ref, row=row):
-            out_ref[:peers] = other_ref[:, row % part]
-
+        out_ref[:peers] = got_ref[:, row]
         weight = jnp.sum(jnp.where(place == row, weights, 0.0), axis=1)
         out_ref[peers:] = weight.reshape(peers // 8, 8, LANES).astype(out_ref.dtype)
 
 
-def partner_parts(place, got, other, rows):
+def partner_parts(place, got, rows):
     peers, _, heads, _ = got.shape
     part = jax.ShapeDtypeStruct((peers + peers // 8, heads, LANES), got.dtype)
     return pl.pallas_call(
         partner_kernel,
         in_specs=[
             pl.BlockSpec(memory_space=pltpu.SMEM),
-            pl.BlockSpec(memory_space=pltpu.VMEM),
             pl.BlockSpec(memory_space=pltpu.VMEM),
         ],
         out_shape=(part,) * rows,
         compiler_params=pltpu.CompilerParams(vmem_limit_bytes=16 * MIB),
         cost_estimate=pl.CostEstimate(flops=0, bytes_accessed=2 * MIB, transcendentals=0),
         name="partner_parts",
-    )(place, got, other)
+    )(place, got)
 
 
 def score_kernel(key_ref, *refs):
@@ -346,26 +353,41 @@
     owners = lax.axis_size("ctx")
     groups = lax.axis_size("qry")
     rows = idx_weight.shape[0]
+    same_core = [list(range(core, owners, CORES)) for core in range(CORES)]
     exchange = functools.partial(
-        lax.all_to_all, axis_name="ctx", split_axis=0, concat_axis=0, tiled=True
+        lax.all_to_all,
+        axis_name="ctx",
+        split_axis=0,
+        concat_axis=0,
+        axis_index_groups=same_core,
+        tiled=True,
     )
 
     def swap(x, axis, size, bits):
         return lax.ppermute(x, axis, [(i, i ^ bits) for i in range(size)])
 
+    core = lax.axis_index("ctx") & 1
+    place = jnp.stack([lax.axis_index("qry"), core]).astype(jnp.int32)
     sent, table = requests(page_ids, idx_query, idx_weight, owners, idx_keys.shape[0] // PAGE)
-    got, latent, cache = lax.optimization_barrier(
-        (exchange(sent), q_latent.reshape(H, DK), stage(latent_cache.T))
+    cache = latent_cache.T
+    other = swap(cache, "ctx", owners, 1)
+    got, latent, cache, other = lax.optimization_barrier(
+        (exchange(sent), q_latent.reshape(H, DK), stage(cache), other)
     )
     heads = idx_weight.shape[1]
-    asked = got[:, rows // 2, 0, heads : heads + 2].astype(jnp.int32)
-    packed, got = lax.optimization_barrier((pack_pages(asked, cache), got))
+    asked = got[:, rows, 0, heads : heads + 2 * CORES].astype(jnp.int32)
+    packed, got = lax.optimization_barrier((pack_pages(place, asked, cache, other), got))
     pages = exchange(packed)
 
-    place = jnp.stack([lax.axis_index("qry"), lax.axis_index("ctx") % 2]).astype(jnp.int32)
-    parts = partner_parts(place, got, swap(got, "ctx", owners, 1), rows)
+    other_keys = swap(idx_keys, "ctx", owners, 1)
+    keys = jnp.where(
+        core == 0,
+        jnp.concatenate([idx_keys, other_keys], axis=0),
+        jnp.concatenate([other_keys, idx_keys], axis=0),
+    )
+    parts = partner_parts(place, got, rows)
     parts = [parts[0]] + [swap(parts[d], "qry", groups, d) for d in range(1, groups)]
-    scores = index_scores(idx_keys, parts)
+    scores = index_scores(keys, parts)
     scores, pages = lax.optimization_barrier((scores, pages))
     scores = exchange(scores)
 

time: 103 us -> 115 us (1.12); the launches traced: 102 us -> 113 us
  waiting for transfers between devices: 40.7 us -> 56.5 us
  starting transfers between devices: 39.2 us -> 33.4 us
    all_to_all x1, waiting for transfers between devices: 23.2 us -> 45.4 us  [per_device(): pages = exchange(packed)]
    ppermute x8 -> x9, waiting for transfers between devices: 8.73 us -> 4.11 us  [swap(): return lax.ppermute(x, axis, [(i, i ^ bits) for i in range(size)])]
    all_to_all x1, starting transfers between devices: 8.59 us -> 5.02 us  [per_device(): exchange(sent)]
    all_to_all x1, starting transfers between devices: 7.83 us -> 4.8 us  [per_device(): scores = exchange(scores)]
    pallas_call x1, Pallas kernels: 4.21 us -> 5.73 us  [pack_pages(): pl.pallas_call(pack_kernel, in_specs=[pl.BlockSpec(memory_space=pltpu.SME...]
    ppermute x8 -> x9, starting transfers between devices: 17.8 us -> 18.9 us  [swap(): return lax.ppermute(x, axis, [(i, i ^ bits) for i in range(size)])]
  transfers between devices with their start and end apart: 11 -> 12, of which waited for: 6 -> 5; matrix products, arithmetic and copies ran while one was open for 2% -> 2% of each run, Pallas kernels for 12% -> 11%
where the time goes in v9:
time: 115 us; the launch traced here: 113 us
  waiting for transfers between devices  56.5 us (49%)
  starting transfers between devices  33.4 us (29%)
  Pallas kernels  19.5 us (17%)
  other arithmetic  1.32 us (1%)
    all_to_all x1, waiting for transfers between devices, per_device(): pages = exchange(packed)  45.4 us
    ppermute x9, starting transfers between devices, swap(): return lax.ppermute(x, axis, [(i, i ^ bits) for i in range(size)])  18.9 us
    all_to_all x1, waiting for transfers between devices, per_device(): exchange(sent)  5.89 us
    pallas_call x1, Pallas kernels, pack_pages(): pl.pallas_call(pack_kernel, in_specs=[pl.BlockSpec(memory_space=pltpu.SME...  5.73 us
    all_to_all x1, starting transfers between devices, per_device(): exchange(sent)  5.02 us
    pallas_call x1, Pallas kernels, attend(): pl.pallas_call(attend_kernel, grid=(peers // sources,), in_specs=[pl.Bloc...  4.87 us
    all_to_all x1, starting transfers between devices, per_device(): scores = exchange(scores)  4.8 us
    all_to_all x1, starting transfers between devices, per_device(): pages = exchange(packed)  4.71 us
  transfers between devices with their start and end apart: 12, of which 5 were waited for; matrix products, arithmetic and copies ran while one was open for 2% of the time, Pallas kernels for 11%

profile of v9, /device:TPU:1, one launch (start us, length us, event | category | flops | bytes accessed | tf_op | source)
XLA Modules:
  0.0 112.6 jit_solution(7538598034622664989)
XLA Ops:
  0.6 3.3 %collective-permute-start.1 = (bf16[576,2048]{1,0:T(8,128)(2,1)}, bf16[576,2048]{1,0:T(8,128)(2,1)}, u32[]{:S(2)}, u32[]{:S(2)}) collective-permute-start(bf16[576,2048]{1,0:T(8,128)(2,1)} %bitcast.12), channel_id=1, source_target_pairs={{0,8},{8,0},{16,24},{24,16},{32,40},{40,32},{48,56},{56,48},{64,72... | collective-permute-start | bytes 7077896 | tf_op jit(solution)/shard_map/ppermute | solution.py:367
  4.0 1.8 %requests.1 = (bf16[16,9,8,128]{3,2,1,0:T(8,128)(2,1)}, s32[32,1,128]{2,1,0:T(1,128)}) custom-call(s32[1,32]{1,0:T(1,128)} %ids_ref.1, bf16[8,1024]{1,0:T(8,128)(2,1)} %query_ref.1, bf16[8,8]{1,0:T(8,128)(2,1)} %weight_ref.1), custom_call_target="tpu_custom_call" | custom-call | tf_op jit(solution)/shard_map/requests/pallas_call | solution.py:62
  5.7 5.0 %all-to-all-start = ((bf16[16,9,8,128]{3,2,1,0:T(8,128)(2,1)}), bf16[16,9,8,128]{3,2,1,0:T(8,128)(2,1)S(1)}, u32[]{:S(2)}, u32[]{:S(2)}) async-start(bf16[16,9,8,128]{3,2,1,0:T(8,128)(2,1)} %get-tuple-element.20), calls=%async_computation | async-start | bytes 589824 | tf_op jit(solution)/shard_map/all_to_all | solution.py:375
  10.7 0.0 copy-start.2
  10.8 1.7 %stage.1.own_ref = bf16[576,2048]{1,0:T(8,128)(2,1)S(1)} custom-call(bf16[576,2048]{1,0:T(8,128)(2,1)} %bitcast.13), custom_call_target="tpu_custom_call" | custom-call | bytes 5242880 | tf_op jit(solution)/shard_map/stage/pallas_call | solution.py:80
  12.5 0.0 copy-done.2
  12.5 0.9 reduce
  13.4 0.2 reshape.18.query_ref
  13.5 0.1 pad_add_fusion.place_ref
  13.6 5.9 %all-to-all-done.got_ref = bf16[16,9,8,128]{3,2,1,0:T(8,128)(2,1)S(1)} async-done(((bf16[16,9,8,128]{3,2,1,0:T(8,128)(2,1)}), bf16[16,9,8,128]{3,2,1,0:T(8,128)(2,1)S(1)}, u32[]{:S(2)}, u32[]{:S(2)}) %all-to-all-start) | async-done | bytes 294944 | tf_op jit(solution)/shard_map/all_to_all | solution.py:375
  19.5 0.0 collective-permute-done.1.other_hbm
  19.5 0.1 slice_convert_fusion
  19.6 5.7 %pack_pages.1 = bf16[32,576,128]{2,1,0:T(8,128)(2,1)} custom-call(s32[2]{0:T(128)S(1)} %pad_add_fusion.place_ref, s32[16,4]{1,0:T(8,128)S(1)} %bitcast.11, bf16[576,2048]{1,0:T(8,128)(2,1)S(1)} %stage.1.own_ref, bf16[576,2048]{1,0:T(8,128)(2,1)} %collective-permute-done.1.other_hbm), custom_call_target="tpu_custom_call" | custom-call | bytes 8388608 | tf_op jit(solution)/shard_map/pack_pages/pallas_call | solution.py:151
  25.3 0.0 copy-start.1
  25.3 4.7 %all-to-all-start.1 = ((bf16[32,576,128]{2,1,0:T(8,128)(2,1)}), bf16[32,576,128]{2,1,0:T(8,128)(2,1)}, u32[]{:S(2)}, u32[]{:S(2)}) async-start(bf16[32,576,128]{2,1,0:T(8,128)(2,1)} %pack_pages.1), calls=%async_computation.1 | async-start | bytes 9437184 | tf_op jit(solution)/shard_map/all_to_all | solution.py:380
  30.1 0.0 copy-done.1
  30.1 1.1 collective-permute-start
  31.1 0.7 partner_parts.1
  31.9 1.7 %collective-permute-start.2 = (bf16[18,8,128]{2,1,0:T(8,128)(2,1)S(1)}, bf16[18,8,128]{2,1,0:T(8,128)(2,1)S(1)}, u32[]{:S(2)}, u32[]{:S(2)}) collective-permute-start(bf16[18,8,128]{2,1,0:T(8,128)(2,1)S(1)} %get-tuple-element.26), channel_id=1, source_target_pairs={{0,1},{1,0},{2,3},{3,2},{4,5},{5,4},{6,7},{7,6},{8,9},{9,8},{10,11... | collective-permute-start | bytes 110600 | tf_op jit(solution)/shard_map/ppermute | solution.py:367
  33.6 3.0 %collective-permute-start.3 = (bf16[18,8,128]{2,1,0:T(8,128)(2,1)S(1)}, bf16[18,8,128]{2,1,0:T(8,128)(2,1)S(1)}, u32[]{:S(2)}, u32[]{:S(2)}) collective-permute-start(bf16[18,8,128]{2,1,0:T(8,128)(2,1)S(1)} %get-tuple-element.27), channel_id=1, source_target_pairs={{0,2},{1,3},{2,0},{3,1},{4,6},{5,7},{6,4},{7,5},{8,10},{9,11},{10,... | collective-permute-start | bytes 110600 | tf_op jit(solution)/shard_map/ppermute | solution.py:367
  36.6 0.0 collective-permute-start.4
  36.6 5.8 %collective-permute-start.5 = (bf16[18,8,128]{2,1,0:T(8,128)(2,1)S(1)}, bf16[18,8,128]{2,1,0:T(8,128)(2,1)S(1)}, u32[]{:S(2)}, u32[]{:S(2)}) collective-permute-start(bf16[18,8,128]{2,1,0:T(8,128)(2,1)S(1)} %get-tuple-element.29), channel_id=1, source_target_pairs={{0,4},{1,5},{2,6},{3,7},{4,0},{5,1},{6,2},{7,3},{8,12},{9,13},{10,... | collective-permute-start | bytes 110600 | tf_op jit(solution)/shard_map/ppermute | solution.py:367
  42.3 0.0 collective-permute-done
  42.4 0.0 collective-permute-start.6
  42.4 0.0 collective-permute-done.2.refs_1_
  42.4 4.0 %collective-permute-start.7 = (bf16[18,8,128]{2,1,0:T(8,128)(2,1)S(1)}, bf16[18,8,128]{2,1,0:T(8,128)(2,1)S(1)}, u32[]{:S(2)}, u32[]{:S(2)}) collective-permute-start(bf16[18,8,128]{2,1,0:T(8,128)(2,1)S(1)} %get-tuple-element.31), channel_id=1, source_target_pairs={{0,6},{1,7},{2,4},{3,5},{4,2},{5,3},{6,0},{7,1},{8,14},{9,15},{10,... | collective-permute-start | bytes 110600 | tf_op jit(solution)/shard_map/ppermute | solution.py:367
  46.4 0.0 collective-permute-done.3.refs_2_
  46.4 0.0 collective-permute-start.8
  46.4 0.3 maximum_select_fusion.key_ref
  46.7 0.0 collective-permute-done.4.refs_3_
  46.7 0.0 collective-permute-done.5.refs_4_
  46.7 2.4 %collective-permute-done.6.refs_5_ = bf16[18,8,128]{2,1,0:T(8,128)(2,1)S(1)} collective-permute-done((bf16[18,8,128]{2,1,0:T(8,128)(2,1)S(1)}, bf16[18,8,128]{2,1,0:T(8,128)(2,1)S(1)}, u32[]{:S(2)}, u32[]{:S(2)}) %collective-permute-start.6) | collective-permute-done | bytes 36896 | tf_op jit(solution)/shard_map/ppermute | solution.py:367
  49.1 0.0 collective-permute-done.7.refs_6_
  49.1 1.7 %collective-permute-done.8.refs_7_ = bf16[18,8,128]{2,1,0:T(8,128)(2,1)S(1)} collective-permute-done((bf16[18,8,128]{2,1,0:T(8,128)(2,1)S(1)}, bf16[18,8,128]{2,1,0:T(8,128)(2,1)S(1)}, u32[]{:S(2)}, u32[]{:S(2)}) %collective-permute-start.8) | collective-permute-done | bytes 36896 | tf_op jit(solution)/shard_map/ppermute | solution.py:367
  50.8 0.0 copy-start
  50.8 3.6 %index_scores.1 = bf16[16,32,128]{2,1,0:T(8,128)(2,1)} custom-call(bf16[4096,128]{1,0:T(8,128)(2,1)S(1)} %maximum_select_fusion.key_ref, bf16[18,8,128]{2,1,0:T(8,128)(2,1)S(1)} %get-tuple-element.25.refs_0_, bf16[18,8,128]{2,1,0:T(8,128)(2,1)S(1)} %collective-permute-done.2.refs_1_, bf16[18,8,128]{2,1,0:T(8,128)(2,1)S(1)} %collective-permute-done.3.refs_2_, ...), custom_call_target="tpu_custom_call" | custom-call | flops 1073741824 | bytes 2097152 | tf_op jit(solution)/shard_map/index_scores/pallas_call | solution.py:247
  54.4 45.4 %all-to-all-done.1.page_ref = bf16[32,576,128]{2,1,0:T(8,128)(2,1)} async-done(((bf16[32,576,128]{2,1,0:T(8,128)(2,1)}), bf16[32,576,128]{2,1,0:T(8,128)(2,1)}, u32[]{:S(2)}, u32[]{:S(2)}) %all-to-all-start.1) | async-done | bytes 4718624 | tf_op jit(solution)/shard_map/all_to_all | solution.py:380
  99.8 4.8 %all-to-all-start.2 = ((bf16[16,32,128]{2,1,0:T(8,128)(2,1)}), bf16[16,32,128]{2,1,0:T(8,128)(2,1)S(1)}, u32[]{:S(2)}, u32[]{:S(2)}) async-start(bf16[16,32,128]{2,1,0:T(8,128)(2,1)} %index_scores.1), calls=%async_computation.2 | async-start | bytes 262144 | tf_op jit(solution)/shard_map/all_to_all | solution.py:392
  104.6 0.0 copy-done
  104.6 4.9 %attend.1 = bf16[128,512]{1,0:T(8,128)(2,1)S(1)} custom-call(s32[32,1,128]{2,1,0:T(1,128)S(1)} %copy-done, bf16[128,576]{1,0:T(8,128)(2,1)S(1)} %reshape.18.query_ref, bf16[32,576,128]{2,1,0:T(8,128)(2,1)} %all-to-all-done.1.page_ref), custom_call_target="tpu_custom_call" | custom-call | flops 1140850688 | bytes 5242880 | tf_op jit(solution)/shard_map/attend/pallas_call | solution.py:327
  109.5 0.9 copy.15
  110.4 1.1 all-to-all-done.2
  111.5 1.1 log_distribution.1
Async XLA Ops:
  0.6 18.9 %collective-permute-start.1 = (bf16[576,2048]{1,0:T(8,128)(2,1)}, bf16[576,2048]{1,0:T(8,128)(2,1)}, u32[]{:S(2)}, u32[]{:S(2)}) collective-permute-start(bf16[576,2048]{1,0:T(8,128)(2,1)} %bitcast.12), channel_id=1, source_target_pairs={{0,8},{8,0},{16,24},{24,16},{32,40},{40,32},{48,56},{56,48},{64,72... | collective-permute-start | bytes 7077896 | tf_op jit(solution)/shard_map/ppermute | solution.py:367
  5.7 13.8 %all-to-all-start = ((bf16[16,9,8,128]{3,2,1,0:T(8,128)(2,1)}), bf16[16,9,8,128]{3,2,1,0:T(8,128)(2,1)S(1)}, u32[]{:S(2)}, u32[]{:S(2)}) async-start(bf16[16,9,8,128]{3,2,1,0:T(8,128)(2,1)} %get-tuple-element.20), calls=%async_computation | async-start | bytes 589824 | tf_op jit(solution)/shard_map/all_to_all | solution.py:375
  10.7 1.7 %copy-start.2 = (bf16[1,73728]{1,0:T(2,128)(2,1)S(1)}, bf16[1,73728]{1,0:T(2,128)(2,1)}, u32[]{:S(2)}) copy-start(bf16[1,73728]{1,0:T(2,128)(2,1)} %param.9) | copy-start | bytes 442372
  25.3 4.7 %copy-start.1 = (bf16[2048,128]{1,0:T(8,128)(2,1)S(1)}, bf16[2048,128]{1,0:T(8,128)(2,1)}, u32[]{:S(2)}) copy-start(bf16[2048,128]{1,0:T(8,128)(2,1)} %param.8) | copy-start | bytes 1572868
  25.3 74.5 %all-to-all-start.1 = ((bf16[32,576,128]{2,1,0:T(8,128)(2,1)}), bf16[32,576,128]{2,1,0:T(8,128)(2,1)}, u32[]{:S(2)}, u32[]{:S(2)}) async-start(bf16[32,576,128]{2,1,0:T(8,128)(2,1)} %pack_pages.1), calls=%async_computation.1 | async-start | bytes 9437184 | tf_op jit(solution)/shard_map/all_to_all | solution.py:380
  30.1 12.3 %collective-permute-start = (bf16[2048,128]{1,0:T(8,128)(2,1)S(1)}, bf16[2048,128]{1,0:T(8,128)(2,1)S(1)}, u32[]{:S(2)}, u32[]{:S(2)}) collective-permute-start(bf16[2048,128]{1,0:T(8,128)(2,1)S(1)} %copy-done.1), channel_id=1, source_target_pairs={{0,8},{8,0},{16,24},{24,16},{32,40},{40,32},{48,56},{56,48},{64,72... | collective-permute-start | bytes 1572872 | tf_op jit(solution)/shard_map/ppermute | solution.py:367
  31.9 10.5 %collective-permute-start.2 = (bf16[18,8,128]{2,1,0:T(8,128)(2,1)S(1)}, bf16[18,8,128]{2,1,0:T(8,128)(2,1)S(1)}, u32[]{:S(2)}, u32[]{:S(2)}) collective-permute-start(bf16[18,8,128]{2,1,0:T(8,128)(2,1)S(1)} %get-tuple-element.26), channel_id=1, source_target_pairs={{0,1},{1,0},{2,3},{3,2},{4,5},{5,4},{6,7},{7,6},{8,9},{9,8},{10,11... | collective-permute-start | bytes 110600 | tf_op jit(solution)/shard_map/ppermute | solution.py:367
  33.6 12.8 %collective-permute-start.3 = (bf16[18,8,128]{2,1,0:T(8,128)(2,1)S(1)}, bf16[18,8,128]{2,1,0:T(8,128)(2,1)S(1)}, u32[]{:S(2)}, u32[]{:S(2)}) collective-permute-start(bf16[18,8,128]{2,1,0:T(8,128)(2,1)S(1)} %get-tuple-element.27), channel_id=1, source_target_pairs={{0,2},{1,3},{2,0},{3,1},{4,6},{5,7},{6,4},{7,5},{8,10},{9,11},{10,... | collective-permute-start | bytes 110600 | tf_op jit(solution)/shard_map/ppermute | solution.py:367
  36.6 10.1 %collective-permute-start.4 = (bf16[18,8,128]{2,1,0:T(8,128)(2,1)S(1)}, bf16[18,8,128]{2,1,0:T(8,128)(2,1)S(1)}, u32[]{:S(2)}, u32[]{:S(2)}) collective-permute-start(bf16[18,8,128]{2,1,0:T(8,128)(2,1)S(1)} %get-tuple-element.28), channel_id=1, source_target_pairs={{0,3},{1,2},{2,1},{3,0},{4,7},{5,6},{6,5},{7,4},{8,11},{9,10},{10,... | collective-permute-start | bytes 110600 | tf_op jit(solution)/shard_map/ppermute | solution.py:367
  36.6 10.1 %collective-permute-start.5 = (bf16[18,8,128]{2,1,0:T(8,128)(2,1)S(1)}, bf16[18,8,128]{2,1,0:T(8,128)(2,1)S(1)}, u32[]{:S(2)}, u32[]{:S(2)}) collective-permute-start(bf16[18,8,128]{2,1,0:T(8,128)(2,1)S(1)} %get-tuple-element.29), channel_id=1, source_target_pairs={{0,4},{1,5},{2,6},{3,7},{4,0},{5,1},{6,2},{7,3},{8,12},{9,13},{10,... | collective-permute-start | bytes 110600 | tf_op jit(solution)/shard_map/ppermute | solution.py:367
  42.4 6.8 %collective-permute-start.6 = (bf16[18,8,128]{2,1,0:T(8,128)(2,1)S(1)}, bf16[18,8,128]{2,1,0:T(8,128)(2,1)S(1)}, u32[]{:S(2)}, u32[]{:S(2)}) collective-permute-start(bf16[18,8,128]{2,1,0:T(8,128)(2,1)S(1)} %get-tuple-element.30), channel_id=1, source_target_pairs={{0,5},{1,4},{2,7},{3,6},{4,1},{5,0},{6,3},{7,2},{8,13},{9,12},{10,... | collective-permute-start | bytes 110600 | tf_op jit(solution)/shard_map/ppermute | solution.py:367
  42.4 6.8 %collective-permute-start.7 = (bf16[18,8,128]{2,1,0:T(8,128)(2,1)S(1)}, bf16[18,8,128]{2,1,0:T(8,128)(2,1)S(1)}, u32[]{:S(2)}, u32[]{:S(2)}) collective-permute-start(bf16[18,8,128]{2,1,0:T(8,128)(2,1)S(1)} %get-tuple-element.31), channel_id=1, source_target_pairs={{0,6},{1,7},{2,4},{3,5},{4,2},{5,3},{6,0},{7,1},{8,14},{9,15},{10,... | collective-permute-start | bytes 110600 | tf_op jit(solution)/shard_map/ppermute | solution.py:367
  46.4 4.4 %collective-permute-start.8 = (bf16[18,8,128]{2,1,0:T(8,128)(2,1)S(1)}, bf16[18,8,128]{2,1,0:T(8,128)(2,1)S(1)}, u32[]{:S(2)}, u32[]{:S(2)}) collective-permute-start(bf16[18,8,128]{2,1,0:T(8,128)(2,1)S(1)} %get-tuple-element.32), channel_id=1, source_target_pairs={{0,7},{1,6},{2,5},{3,4},{4,3},{5,2},{6,1},{7,0},{8,15},{9,14},{10,... | collective-permute-start | bytes 110600 | tf_op jit(solution)/shard_map/ppermute | solution.py:367
  50.8 53.8 %copy-start = (s32[32,1,128]{2,1,0:T(1,128)S(1)}, s32[32,1,128]{2,1,0:T(1,128)}, u32[]{:S(2)}) copy-start(s32[32,1,128]{2,1,0:T(1,128)} %get-tuple-element.35.used_ref) | copy-start | bytes 49156
  99.8 11.7 %all-to-all-start.2 = ((bf16[16,32,128]{2,1,0:T(8,128)(2,1)}), bf16[16,32,128]{2,1,0:T(8,128)(2,1)S(1)}, u32[]{:S(2)}, u32[]{:S(2)}) async-start(bf16[16,32,128]{2,1,0:T(8,128)(2,1)} %index_scores.1), calls=%async_computation.2 | async-start | bytes 262144 | tf_op jit(solution)/shard_map/all_to_all | solution.py:392

commit v10 on v8

--- a/solution.py
+++ b/solution.py
@@ -310,7 +310,9 @@
 
     @pl.when(step == pl.num_programs(0) - 1)
     def _():
-        out_ref[...] = (sum_ref[...] / total_ref[...][:, :1]).astype(out_ref.dtype)
+        sum_ref[...] = sum_ref[...] / total_ref[...][:, :1]
+        for h in range(H):
+            out_ref[:, h * D_LAT : (h + 1) * D_LAT] = sum_ref[h : h + 1, :].astype(out_ref.dtype)
 
 
 def attend(used, query, pages):
@@ -325,13 +327,13 @@
             pl.BlockSpec(memory_space=pltpu.VMEM),
             pl.BlockSpec((sources, DK, LANES), lambda i: (i, 0, 0)),
         ],
-        out_specs=pl.BlockSpec((H, D_LAT), lambda i: (0, 0)),
+        out_specs=pl.BlockSpec((1, H * D_LAT), lambda i: (0, 0)),
         scratch_shapes=[
             pltpu.VMEM((H, LANES), jnp.float32),
             pltpu.VMEM((H, LANES), jnp.float32),
             pltpu.VMEM((H, D_LAT), jnp.float32),
         ],
-        out_shape=jax.ShapeDtypeStruct((H, D_LAT), jnp.bfloat16),
+        out_shape=jax.ShapeDtypeStruct((1, H * D_LAT), jnp.bfloat16),
         compiler_params=pltpu.CompilerParams(vmem_limit_bytes=40 * MIB),
         cost_estimate=pl.CostEstimate(
             flops=2 * H * tokens * (2 * D_LAT + D_ROPE),

time: 103 us -> 103 us (level)
  waiting for transfers between devices: 40.7 us -> 43.7 us
  starting transfers between devices: 39.2 us -> 36.3 us
    ppermute x8, starting transfers between devices: 17.8 us -> 14.9 us  [swap(): return lax.ppermute(x, axis, [(i, i ^ bits) for i in range(size)])]
    ppermute x8, waiting for transfers between devices: 8.73 us -> 11.5 us  [swap(): return lax.ppermute(x, axis, [(i, i ^ bits) for i in range(size)])]
  transfers between devices with their start and end apart: 11 -> 11, of which waited for: 6 -> 8; matrix products, arithmetic and copies ran while one was open for 2% -> 1% of each run, Pallas kernels for 12% -> 13%
where the time goes in v10:
time: 103 us; the launch traced here: 102 us
  waiting for transfers between devices  43.7 us (42%)
  starting transfers between devices  36.3 us (35%)
  Pallas kernels  20.4 us (20%)
  other arithmetic  1.03 us (1%)
    all_to_all x1, waiting for transfers between devices, per_device(): pages = exchange(packed)  23.3 us
    ppermute x8, starting transfers between devices, swap(): return lax.ppermute(x, axis, [(i, i ^ bits) for i in range(size)])  14.9 us
    ppermute x8, waiting for transfers between devices, swap(): return lax.ppermute(x, axis, [(i, i ^ bits) for i in range(size)])  11.5 us
    all_to_all x1, starting transfers between devices, per_device(): exchange(sent)  8.59 us
    all_to_all x1, starting transfers between devices, per_device(): scores = exchange(scores)  7.83 us
    all_to_all x1, waiting for transfers between devices, per_device(): exchange(sent)  6.81 us
    pallas_call x1, Pallas kernels, attend(): pl.pallas_call(attend_kernel, grid=(peers // sources,), in_specs=[pl.Bloc...  5.69 us
    all_to_all x1, starting transfers between devices, per_device(): pages = exchange(packed)  4.97 us
  transfers between devices with their start and end apart: 11, of which 8 were waited for; matrix products, arithmetic and copies ran while one was open for 1% of the time, Pallas kernels for 13%

profile of v10, /device:TPU:1, one launch (start us, length us, event | category | flops | bytes accessed | tf_op | source)
XLA Modules:
  0.0 102.3 jit_solution(14651144377231822118)
XLA Ops:
  0.6 0.0 copy-start.2
  0.6 1.7 %requests.1 = (bf16[32,5,8,128]{3,2,1,0:T(8,128)(2,1)}, s32[32,1,128]{2,1,0:T(1,128)}) custom-call(s32[1,32]{1,0:T(1,128)} %ids_ref.1, bf16[8,1024]{1,0:T(8,128)(2,1)} %query_ref.1, bf16[8,8]{1,0:T(8,128)(2,1)} %weight_ref.1), custom_call_target="tpu_custom_call" | custom-call | tf_op jit(solution)/shard_map/requests/pallas_call | solution.py:59
  2.4 8.6 %all-to-all-start = ((bf16[32,5,8,128]{3,2,1,0:T(8,128)(2,1)}), bf16[32,5,8,128]{3,2,1,0:T(8,128)(2,1)S(1)}, u32[]{:S(2)}, u32[]{:S(2)}) async-start(bf16[32,5,8,128]{3,2,1,0:T(8,128)(2,1)} %get-tuple-element.19), calls=%async_computation | async-start | bytes 655360 | tf_op jit(solution)/shard_map/all_to_all | solution.py:360
  10.9 1.7 %stage.1.cache_ref = bf16[576,2048]{1,0:T(8,128)(2,1)S(1)} custom-call(bf16[576,2048]{1,0:T(8,128)(2,1)} %bitcast.8), custom_call_target="tpu_custom_call" | custom-call | bytes 5242880 | tf_op jit(solution)/shard_map/stage/pallas_call | solution.py:77
  12.6 0.0 copy-done.2
  12.6 0.9 reduce
  13.5 0.2 reshape.15.query_ref
  13.7 6.8 %all-to-all-done.got_ref = bf16[32,5,8,128]{3,2,1,0:T(8,128)(2,1)S(1)} async-done(((bf16[32,5,8,128]{3,2,1,0:T(8,128)(2,1)}), bf16[32,5,8,128]{3,2,1,0:T(8,128)(2,1)S(1)}, u32[]{:S(2)}, u32[]{:S(2)}) %all-to-all-start) | async-done | bytes 327712 | tf_op jit(solution)/shard_map/all_to_all | solution.py:360
  20.5 0.1 slice_convert_fusion
  20.6 4.4 %pack_pages.1 = bf16[32,576,128]{2,1,0:T(8,128)(2,1)} custom-call(s32[32,2]{1,0:T(8,128)S(1)} %bitcast.7, bf16[576,2048]{1,0:T(8,128)(2,1)S(1)} %stage.1.cache_ref), custom_call_target="tpu_custom_call" | custom-call | bytes 8388608 | tf_op jit(solution)/shard_map/pack_pages/pallas_call | solution.py:139
  25.0 0.0 copy-start.1
  25.0 5.0 %all-to-all-start.1 = ((bf16[32,576,128]{2,1,0:T(8,128)(2,1)}), bf16[32,576,128]{2,1,0:T(8,128)(2,1)}, u32[]{:S(2)}, u32[]{:S(2)}) async-start(bf16[32,576,128]{2,1,0:T(8,128)(2,1)} %pack_pages.1), calls=%async_computation.1 | async-start | bytes 9437184 | tf_op jit(solution)/shard_map/all_to_all | solution.py:365
  30.0 0.0 copy-start
  30.0 0.3 collective-permute-start
  30.3 0.1 pad_add_fusion.place_ref
  30.4 1.3 %collective-permute-done.other_ref = bf16[32,5,8,128]{3,2,1,0:T(8,128)(2,1)S(1)} collective-permute-done((bf16[32,5,8,128]{3,2,1,0:T(8,128)(2,1)S(1)}, bf16[32,5,8,128]{3,2,1,0:T(8,128)(2,1)S(1)}, u32[]{:S(2)}, u32[]{:S(2)}) %collective-permute-start) | collective-permute-done | bytes 327712 | tf_op jit(solution)/shard_map/ppermute | solution.py:356
  31.8 1.1 %partner_parts.1 = (bf16[36,8,128]{2,1,0:T(8,128)(2,1)S(1)}, bf16[36,8,128]{2,1,0:T(8,128)(2,1)S(1)}, bf16[36,8,128]{2,1,0:T(8,128)(2,1)S(1)}, bf16[36,8,128]{2,...) custom-call(s32[2]{0:T(128)S(1)} %pad_add_fusion.place_ref, ...), custom_call_target="tpu_custom_call" | custom-call | bytes 2097152 | tf_op jit(solution)/shard_map/partner_parts/pallas_call | solution.py:180
  32.8 1.9 %collective-permute-start.1 = (bf16[36,8,128]{2,1,0:T(8,128)(2,1)S(1)}, bf16[36,8,128]{2,1,0:T(8,128)(2,1)S(1)}, u32[]{:S(2)}, u32[]{:S(2)}) collective-permute-start(bf16[36,8,128]{2,1,0:T(8,128)(2,1)S(1)} %get-tuple-element.24), channel_id=1, source_target_pairs={{0,1},{1,0},{2,3},{3,2},{4,5},{5,4},{6,7},{7,6},{8,9},{9,8},{10,11... | collective-permute-start | bytes 221192 | tf_op jit(solution)/shard_map/ppermute | solution.py:356
  34.7 3.0 %collective-permute-start.2 = (bf16[36,8,128]{2,1,0:T(8,128)(2,1)S(1)}, bf16[36,8,128]{2,1,0:T(8,128)(2,1)S(1)}, u32[]{:S(2)}, u32[]{:S(2)}) collective-permute-start(bf16[36,8,128]{2,1,0:T(8,128)(2,1)S(1)} %get-tuple-element.25), channel_id=1, source_target_pairs={{0,2},{1,3},{2,0},{3,1},{4,6},{5,7},{6,4},{7,5},{8,10},{9,11},{10,... | collective-permute-start | bytes 221192 | tf_op jit(solution)/shard_map/ppermute | solution.py:356
  37.7 0.0 collective-permute-start.3
  37.7 5.7 %collective-permute-start.4 = (bf16[36,8,128]{2,1,0:T(8,128)(2,1)S(1)}, bf16[36,8,128]{2,1,0:T(8,128)(2,1)S(1)}, u32[]{:S(2)}, u32[]{:S(2)}) collective-permute-start(bf16[36,8,128]{2,1,0:T(8,128)(2,1)S(1)} %get-tuple-element.27), channel_id=1, source_target_pairs={{0,4},{1,5},{2,6},{3,7},{4,0},{5,1},{6,2},{7,3},{8,12},{9,13},{10,... | collective-permute-start | bytes 221192 | tf_op jit(solution)/shard_map/ppermute | solution.py:356
  43.5 0.0 collective-permute-start.5
  43.5 0.0 collective-permute-done.1.refs_1_
  43.5 4.0 %collective-permute-start.6 = (bf16[36,8,128]{2,1,0:T(8,128)(2,1)S(1)}, bf16[36,8,128]{2,1,0:T(8,128)(2,1)S(1)}, u32[]{:S(2)}, u32[]{:S(2)}) collective-permute-start(bf16[36,8,128]{2,1,0:T(8,128)(2,1)S(1)} %get-tuple-element.29), channel_id=1, source_target_pairs={{0,6},{1,7},{2,4},{3,5},{4,2},{5,3},{6,0},{7,1},{8,14},{9,15},{10,... | collective-permute-start | bytes 221192 | tf_op jit(solution)/shard_map/ppermute | solution.py:356
  47.4 0.0 collective-permute-done.2.refs_2_
  47.4 0.0 collective-permute-start.7
  47.4 0.0 collective-permute-done.3.refs_3_
  47.4 0.2 collective-permute-done.4.refs_4_
  47.6 6.2 %collective-permute-done.5.refs_5_ = bf16[36,8,128]{2,1,0:T(8,128)(2,1)S(1)} collective-permute-done((bf16[36,8,128]{2,1,0:T(8,128)(2,1)S(1)}, bf16[36,8,128]{2,1,0:T(8,128)(2,1)S(1)}, u32[]{:S(2)}, u32[]{:S(2)}) %collective-permute-start.5) | collective-permute-done | bytes 73760 | tf_op jit(solution)/shard_map/ppermute | solution.py:356
  53.8 0.1 collective-permute-done.6.refs_6_
  53.9 3.7 %collective-permute-done.7.refs_7_ = bf16[36,8,128]{2,1,0:T(8,128)(2,1)S(1)} collective-permute-done((bf16[36,8,128]{2,1,0:T(8,128)(2,1)S(1)}, bf16[36,8,128]{2,1,0:T(8,128)(2,1)S(1)}, u32[]{:S(2)}, u32[]{:S(2)}) %collective-permute-start.7) | collective-permute-done | bytes 73760 | tf_op jit(solution)/shard_map/ppermute | solution.py:356
  57.6 0.0 copy-done.1
  57.6 4.7 %index_scores.1 = bf16[32,16,128]{2,1,0:T(8,128)(2,1)} custom-call(bf16[2048,128]{1,0:T(8,128)(2,1)S(1)} %copy-done.1, bf16[36,8,128]{2,1,0:T(8,128)(2,1)S(1)} %get-tuple-element.23.refs_0_, bf16[36,8,128]{2,1,0:T(8,128)(2,1)S(1)} %collective-permute-done.1.refs_1_, bf16[36,8,128]{2,1,0:T(8,128)(2,1)S(1)} %collective-permute-done.2.refs_2_, ...), custom_call_target="tpu_custom_call" | custom-call | flops 1073741824 | bytes 2097152 | tf_op jit(solution)/shard_map/index_scores/pallas_call | solution.py:240
  62.3 23.3 %all-to-all-done.1.page_ref = bf16[32,576,128]{2,1,0:T(8,128)(2,1)} async-done(((bf16[32,576,128]{2,1,0:T(8,128)(2,1)}), bf16[32,576,128]{2,1,0:T(8,128)(2,1)}, u32[]{:S(2)}, u32[]{:S(2)}) %all-to-all-start.1) | async-done | bytes 4718624 | tf_op jit(solution)/shard_map/all_to_all | solution.py:365
  85.7 7.8 %all-to-all-start.2 = ((bf16[32,16,128]{2,1,0:T(8,128)(2,1)}), bf16[32,16,128]{2,1,0:T(8,128)(2,1)S(1)}, u32[]{:S(2)}, u32[]{:S(2)}) async-start(bf16[32,16,128]{2,1,0:T(8,128)(2,1)} %index_scores.1), calls=%async_computation.2 | async-start | bytes 262144 | tf_op jit(solution)/shard_map/all_to_all | solution.py:372
  93.5 0.0 copy-done
  93.5 5.7 %attend.1 = bf16[1,65536]{1,0:T(2,128)(2,1)} custom-call(s32[32,1,128]{2,1,0:T(1,128)S(1)} %copy-done, bf16[128,576]{1,0:T(8,128)(2,1)S(1)} %reshape.15.query_ref, bf16[32,576,128]{2,1,0:T(8,128)(2,1)} %all-to-all-done.1.page_ref), custom_call_target="tpu_custom_call" | custom-call | flops 1140850688 | bytes 5242880 | tf_op jit(solution)/shard_map/attend/pallas_call | solution.py:322
  99.2 2.0 %all-to-all-done.2 = bf16[32,16,128]{2,1,0:T(8,128)(2,1)S(1)} async-done(((bf16[32,16,128]{2,1,0:T(8,128)(2,1)}), bf16[32,16,128]{2,1,0:T(8,128)(2,1)S(1)}, u32[]{:S(2)}, u32[]{:S(2)}) %all-to-all-start.2) | async-done | bytes 131104 | tf_op jit(solution)/shard_map/all_to_all | solution.py:372
  101.2 1.1 %log_distribution.1 = f32[512,128]{1,0:T(8,128)} custom-call(bf16[512,128]{1,0:T(8,128)(2,1)S(1)} %bitcast.6), custom_call_target="tpu_custom_call" | custom-call | flops 262144 | bytes 393216 | tf_op jit(solution)/shard_map/log_distribution/pallas_call | solution.py:265
Async XLA Ops:
  0.6 12.0 %copy-start.2 = (bf16[1,73728]{1,0:T(2,128)(2,1)S(1)}, bf16[1,73728]{1,0:T(2,128)(2,1)}, u32[]{:S(2)}) copy-start(bf16[1,73728]{1,0:T(2,128)(2,1)} %param.9) | copy-start | bytes 442372
  2.4 18.1 %all-to-all-start = ((bf16[32,5,8,128]{3,2,1,0:T(8,128)(2,1)}), bf16[32,5,8,128]{3,2,1,0:T(8,128)(2,1)S(1)}, u32[]{:S(2)}, u32[]{:S(2)}) async-start(bf16[32,5,8,128]{3,2,1,0:T(8,128)(2,1)} %get-tuple-element.19), calls=%async_computation | async-start | bytes 655360 | tf_op jit(solution)/shard_map/all_to_all | solution.py:360
  25.0 32.6 %copy-start.1 = (bf16[2048,128]{1,0:T(8,128)(2,1)S(1)}, bf16[2048,128]{1,0:T(8,128)(2,1)}, u32[]{:S(2)}) copy-start(bf16[2048,128]{1,0:T(8,128)(2,1)} %key_ref.1) | copy-start | bytes 1572868
  25.0 60.6 %all-to-all-start.1 = ((bf16[32,576,128]{2,1,0:T(8,128)(2,1)}), bf16[32,576,128]{2,1,0:T(8,128)(2,1)}, u32[]{:S(2)}, u32[]{:S(2)}) async-start(bf16[32,576,128]{2,1,0:T(8,128)(2,1)} %pack_pages.1), calls=%async_computation.1 | async-start | bytes 9437184 | tf_op jit(solution)/shard_map/all_to_all | solution.py:365
  30.0 63.5 %copy-start = (s32[32,1,128]{2,1,0:T(1,128)S(1)}, s32[32,1,128]{2,1,0:T(1,128)}, u32[]{:S(2)}) copy-start(s32[32,1,128]{2,1,0:T(1,128)} %get-tuple-element.33.used_ref) | copy-start | bytes 49156
  30.0 1.7 %collective-permute-start = (bf16[32,5,8,128]{3,2,1,0:T(8,128)(2,1)S(1)}, bf16[32,5,8,128]{3,2,1,0:T(8,128)(2,1)S(1)}, u32[]{:S(2)}, u32[]{:S(2)}) collective-permute-start(bf16[32,5,8,128]{3,2,1,0:T(8,128)(2,1)S(1)} %all-to-all-done.got_ref), channel_id=1, source_target_pairs={{0,8},{8,0},{16,24},{24,16},{32,40},{40,32},{48,56},{56,48},{64,72... | collective-permute-start | bytes 983048 | tf_op jit(solution)/shard_map/ppermute | solution.py:356
  32.8 10.6 %collective-permute-start.1 = (bf16[36,8,128]{2,1,0:T(8,128)(2,1)S(1)}, bf16[36,8,128]{2,1,0:T(8,128)(2,1)S(1)}, u32[]{:S(2)}, u32[]{:S(2)}) collective-permute-start(bf16[36,8,128]{2,1,0:T(8,128)(2,1)S(1)} %get-tuple-element.24), channel_id=1, source_target_pairs={{0,1},{1,0},{2,3},{3,2},{4,5},{5,4},{6,7},{7,6},{8,9},{9,8},{10,11... | collective-permute-start | bytes 221192 | tf_op jit(solution)/shard_map/ppermute | solution.py:356
  34.7 12.7 %collective-permute-start.2 = (bf16[36,8,128]{2,1,0:T(8,128)(2,1)S(1)}, bf16[36,8,128]{2,1,0:T(8,128)(2,1)S(1)}, u32[]{:S(2)}, u32[]{:S(2)}) collective-permute-start(bf16[36,8,128]{2,1,0:T(8,128)(2,1)S(1)} %get-tuple-element.25), channel_id=1, source_target_pairs={{0,2},{1,3},{2,0},{3,1},{4,6},{5,7},{6,4},{7,5},{8,10},{9,11},{10,... | collective-permute-start | bytes 221192 | tf_op jit(solution)/shard_map/ppermute | solution.py:356
  37.7 9.7 %collective-permute-start.3 = (bf16[36,8,128]{2,1,0:T(8,128)(2,1)S(1)}, bf16[36,8,128]{2,1,0:T(8,128)(2,1)S(1)}, u32[]{:S(2)}, u32[]{:S(2)}) collective-permute-start(bf16[36,8,128]{2,1,0:T(8,128)(2,1)S(1)} %get-tuple-element.26), channel_id=1, source_target_pairs={{0,3},{1,2},{2,1},{3,0},{4,7},{5,6},{6,5},{7,4},{8,11},{9,10},{10,... | collective-permute-start | bytes 221192 | tf_op jit(solution)/shard_map/ppermute | solution.py:356
  37.7 9.9 %collective-permute-start.4 = (bf16[36,8,128]{2,1,0:T(8,128)(2,1)S(1)}, bf16[36,8,128]{2,1,0:T(8,128)(2,1)S(1)}, u32[]{:S(2)}, u32[]{:S(2)}) collective-permute-start(bf16[36,8,128]{2,1,0:T(8,128)(2,1)S(1)} %get-tuple-element.27), channel_id=1, source_target_pairs={{0,4},{1,5},{2,6},{3,7},{4,0},{5,1},{6,2},{7,3},{8,12},{9,13},{10,... | collective-permute-start | bytes 221192 | tf_op jit(solution)/shard_map/ppermute | solution.py:356
  43.5 10.4 %collective-permute-start.5 = (bf16[36,8,128]{2,1,0:T(8,128)(2,1)S(1)}, bf16[36,8,128]{2,1,0:T(8,128)(2,1)S(1)}, u32[]{:S(2)}, u32[]{:S(2)}) collective-permute-start(bf16[36,8,128]{2,1,0:T(8,128)(2,1)S(1)} %get-tuple-element.28), channel_id=1, source_target_pairs={{0,5},{1,4},{2,7},{3,6},{4,1},{5,0},{6,3},{7,2},{8,13},{9,12},{10,... | collective-permute-start | bytes 221192 | tf_op jit(solution)/shard_map/ppermute | solution.py:356
  43.5 10.4 %collective-permute-start.6 = (bf16[36,8,128]{2,1,0:T(8,128)(2,1)S(1)}, bf16[36,8,128]{2,1,0:T(8,128)(2,1)S(1)}, u32[]{:S(2)}, u32[]{:S(2)}) collective-permute-start(bf16[36,8,128]{2,1,0:T(8,128)(2,1)S(1)} %get-tuple-element.29), channel_id=1, source_target_pairs={{0,6},{1,7},{2,4},{3,5},{4,2},{5,3},{6,0},{7,1},{8,14},{9,15},{10,... | collective-permute-start | bytes 221192 | tf_op jit(solution)/shard_map/ppermute | solution.py:356
  47.4 10.2 %collective-permute-start.7 = (bf16[36,8,128]{2,1,0:T(8,128)(2,1)S(1)}, bf16[36,8,128]{2,1,0:T(8,128)(2,1)S(1)}, u32[]{:S(2)}, u32[]{:S(2)}) collective-permute-start(bf16[36,8,128]{2,1,0:T(8,128)(2,1)S(1)} %get-tuple-element.30), channel_id=1, source_target_pairs={{0,7},{1,6},{2,5},{3,4},{4,3},{5,2},{6,1},{7,0},{8,15},{9,14},{10,... | collective-permute-start | bytes 221192 | tf_op jit(solution)/shard_map/ppermute | solution.py:356
  85.7 15.6 %all-to-all-start.2 = ((bf16[32,16,128]{2,1,0:T(8,128)(2,1)}), bf16[32,16,128]{2,1,0:T(8,128)(2,1)S(1)}, u32[]{:S(2)}, u32[]{:S(2)}) async-start(bf16[32,16,128]{2,1,0:T(8,128)(2,1)} %index_scores.1), calls=%async_computation.2 | async-start | bytes 262144 | tf_op jit(solution)/shard_map/all_to_all | solution.py:372
